TPU v7x, 32 devices: a whole 2x2x4 slice. The times are simulated.
32 devices in a mesh: wide: 8 (over z, y), narrow: 4 (over x, core).
Axes of the slice: x: 2, y: 2, z: 4, core: 2. Of those that a mesh axis runs over, the one named last changes fastest.
Arguments:
- slab: bfloat16 [6144, 2048], P('wide', 'narrow'), may hold values from -1.1953125 to 1.1953125
- occupation: float32 [4096], replicated, may hold values from 0.02 to 2
- column_band: int32 [2048], P('narrow'), may hold values from 0 to 4095
- pattern: int32 [48, 12], P('wide'), may hold values from 0 to 47, as said below
Outputs:
- density: bfloat16 [48, 12, 128, 128], P('wide', 'narrow')
Inputs may be any that keep to these rules, and one draw needn't show every extreme that they name: `pattern`: each row c lists 12 different clusters, each equal to (c + d) mod 48 with -8 <= d <= 8; d = -8 and d = 8 appear in every row.
All inputs are finite; a program needn't handle non-finite values.
Results may differ from a plain program's by a relative error of at most 0.015.
Values may be sent and summed in bfloat16 or wider, within the bound.
No kernel may reach another device: no remote copies, remote signals or barrier semaphores. Data moves between devices by JAX's collectives and lax.ppermute only.
A program may use at most 64 MiB of HBM per device.

v0:
```python
import functools

import jax
import jax.numpy as jnp
from jax import lax
from jax.experimental import pallas as pl
from jax.experimental.pallas import tpu as pltpu
from jax.sharding import PartitionSpec as P

B = 128
REACH = 8
CL = 6
PAIR = 2
VMEM = pl.BlockSpec(memory_space=pltpu.VMEM)
SMEM = pl.BlockSpec(memory_space=pltpu.SMEM)
LIMIT = 40 * 1024 * 1024
LONG = pl.CostEstimate(flops=20 * 10**9, bytes_accessed=1, transcendentals=0)
SHORT = pl.CostEstimate(flops=1, bytes_accessed=1, transcendentals=0)


def move(value, axis, target):
    count = lax.axis_size(axis)
    return lax.ppermute(value, axis, [(s, target(s) % count) for s in range(count)])


def outward(w):
    return w + 2 if w % 2 == 0 else w - 2


def natural(low, high):
    odd = lax.rem(lax.axis_index("wide"), 2)
    return jnp.where(odd == 1, low, CL - 1 - high)


def multiply(left, right):
    product = lax.dot_general(left, right, (((1,), (1,)), ((), ())), preferred_element_type=jnp.float32)
    return product.astype(jnp.bfloat16)


def add_pieces(marks, pieces, left, dense):
    for piece, mark in zip(pieces, marks):
        count = piece.shape[0] // B
        for at in range(0, count, PAIR):
            low, high = mark + at, mark + at + PAIR - 1
            c0, c1 = max(0, low - REACH), min(CL - 1, high + REACH)
            offset, start, rows = natural(low, high), natural(c0, c1), (c1 - c0 + 1) * B
            row = pl.multiple_of((offset - natural(mark, mark + count - 1)) * B, PAIR * B)
            product = multiply(
                left[pl.ds(pl.multiple_of(start * B, B), rows), :], piece[pl.ds(row, PAIR * B), :]
            )
            for r in range(c1 - c0 + 1):
                for h in range(PAIR):
                    dense[start + r, offset + REACH + h] = product[r * B : (r + 1) * B, h * B : (h + 1) * B]


def early_kernel(marks, left, *refs):
    add_pieces(marks, refs[:-1], left, refs[-1])


def early_blocks(left, pieces):
    return pl.pallas_call(
        functools.partial(early_kernel, list(pieces)),
        out_shape=jax.ShapeDtypeStruct((CL, CL + 2 * REACH, B, B), jnp.bfloat16),
        in_specs=[VMEM] * (1 + len(pieces)),
        out_specs=VMEM,
        compiler_params=pltpu.CompilerParams(vmem_limit_bytes=LIMIT),
        cost_estimate=LONG,
        name="early_blocks",
    )(left, *pieces.values())


def ends_kernel(weight, near, far, out):
    odd = lax.rem(lax.axis_index("wide"), 2) == 1
    left = (near[...].astype(jnp.float32) * weight[...]).astype(jnp.bfloat16)
    product = multiply(left, far[...])
    for at, (c, m) in enumerate(((-1, 6), (-1, 7), (-2, 6))):
        here, there = ((c + 2) * B, (m - 6) * B), ((-1 - c) * B, (7 - m) * B)
        one, two = [product[row : row + B, column : column + B] for row, column in (here, there)]
        out[at] = jnp.where(odd, one, two)


def end_blocks(weight, near, far):
    return pl.pallas_call(
        ends_kernel,
        out_shape=jax.ShapeDtypeStruct((3, B, B), jnp.bfloat16),
        in_specs=[VMEM] * 3,
        out_specs=VMEM,
        compiler_params=pltpu.CompilerParams(vmem_limit_bytes=LIMIT),
        cost_estimate=SHORT,
        name="end_blocks",
    )(weight[None, :], near, far)


def blocks_kernel(share, marks, places, left, from_partner, *refs):
    dense = refs[len(marks) + 1]
    outs = refs[len(marks) + 2 :]
    add_pieces(marks, refs[: len(marks)], left, dense)
    for at, (c, m) in enumerate(((0, -7), (0, -8), (1, -7))):
        dense[natural(c, c), natural(m, m) + REACH] = from_partner[at]
    me = lax.axis_index("narrow")
    for out, mask in zip(outs, (3, 1, 2, 0)):
        slot0 = (me ^ mask) * share
        for c in range(CL):
            for s in range(share):
                out[c, s] = dense[c, places[c, slot0 + s]]


def late_blocks(share, places, left, from_partner, pieces, dense):
    shapes = [jax.ShapeDtypeStruct(dense.shape, dense.dtype)]
    shapes += [jax.ShapeDtypeStruct((CL, share, B, B), jnp.bfloat16)] * 4
    return pl.pallas_call(
        functools.partial(blocks_kernel, share, list(pieces)),
        out_shape=shapes,
        in_specs=[SMEM] + [VMEM] * (3 + len(pieces)),
        out_specs=[VMEM] * len(shapes),
        input_output_aliases={3 + len(pieces): 0},
        compiler_params=pltpu.CompilerParams(vmem_limit_bytes=LIMIT),
        cost_estimate=SHORT,
        name="late_blocks",
    )(places, left, from_partner, *pieces.values(), dense)[1:]


def take_kernel(near, slab, after, out):
    odd = lax.rem(lax.axis_index("wide"), 2)
    row = (1 - odd if near else odd) * 2 * PAIR * B
    out[...] = slab[pl.ds(pl.multiple_of(row, PAIR * B), PAIR * B), :]


def take(slab, near, after):
    return pl.pallas_call(
        functools.partial(take_kernel, near),
        out_shape=jax.ShapeDtypeStruct((PAIR * B, slab.shape[1]), slab.dtype),
        in_specs=[VMEM] * 2,
        out_specs=VMEM,
        compiler_params=pltpu.CompilerParams(vmem_limit_bytes=LIMIT),
        cost_estimate=SHORT,
        name="take",
    )(slab, after)


def per_device(slab, occupation, column_band, pattern):
    clusters = CL * lax.axis_size("wide")
    share = pattern.shape[1] // lax.axis_size("narrow")
    odd = lax.axis_index("wide") % 2
    rows = PAIR * B
    partner = lambda w: w ^ 1

    places = jnp.mod(pattern - (lax.axis_index("wide") * CL - REACH), clusters)
    picks = column_band[:, None] == jnp.arange(occupation.shape[0], dtype=jnp.int32)[None, :]
    weight = jnp.sum(jnp.where(picks, occupation[None, :], jnp.float32(0.0)), axis=1)
    scaled = (slab.astype(jnp.float32) * weight[None, :]).astype(jnp.bfloat16)

    near_rows = lax.dynamic_slice_in_dim(slab, (1 - odd) * 2 * rows, rows, 0)
    end_rows = lax.dynamic_slice_in_dim(slab, odd * 2 * rows, rows, 0)
    early = {0: slab}
    early[-2] = move(take(slab, True, places), "wide", partner)
    early[-6] = move(take(slab, False, places), "wide", partner)
    early[-4] = move(slab[rows : 2 * rows], "wide", partner)
    early[12] = move(near_rows, "wide", outward)
    early[10] = move(early[-2], "wide", outward)
    early[6] = move(early[-6], "wide", outward)
    late = {8: move(early[-4], "wide", outward)}
    from_partner = move(end_blocks(weight, early[-2], early[6]), "wide", partner)

    dense = early_blocks(scaled, early)
    send_far, send_near, keep_far, keep_near = late_blocks(
        share, places, scaled, from_partner, late, dense
    )
    got_far = move(send_far, "narrow", lambda n: n ^ 1)
    got_near = move(send_near, "narrow", lambda n: n ^ 1)
    far = (keep_far.astype(jnp.float32) + got_far.astype(jnp.float32)).astype(jnp.bfloat16)
    got = move(far, "narrow", lambda n: n ^ 2)
    near = keep_near.astype(jnp.float32) + got_near.astype(jnp.float32)
    return (near + got.astype(jnp.float32)).astype(jnp.bfloat16)


def solution(mesh):
    placed = (P("wide", "narrow"), P(), P("narrow"), P("wide", None))
    return jax.shard_map(
        per_device,
        mesh=mesh,
        in_specs=placed,
        out_specs=P("wide", "narrow", None, None),
        check_vma=False,
    )
```

profile of v0, /device:TPU:0, one launch (start us, length us, event | category | flops | bytes accessed | tf_op | source)
XLA Modules:
  0.0 51.9 jit_solution(14524924566122638473)
XLA Ops:
  0.0 0.7 %add_select_fusion.after.places = s32[6,12]{1,0:T(8,128)S(1)} fusion(s32[6,12]{1,0:T(8,128)} %param.7, s32[]{:T(128)S(6)} %sub.12), kind=kLoop, calls=%fused_computation.5 | loop fusion | flops 504 | bytes 580 | tf_op jit(solution)/shard_map/jit(remainder)/select_n | solution.py:148
  0.7 0.0 copy-start
  0.7 1.1 %copy-done = bf16[768,512]{1,0:T(8,128)(2,1)S(1)} copy-done((bf16[768,512]{1,0:T(8,128)(2,1)S(1)}, bf16[768,512]{1,0:T(8,128)(2,1)}, u32[]{:S(2)}) %copy-start) | copy-done | bytes 786456
  1.8 0.0 copy-start.1
  1.8 0.0 copy-start.2
  1.8 0.0 copy-start.3
  1.9 3.0 %collective-permute-start = (bf16[256,512]{1,0:T(8,128)(2,1)S(1)}, bf16[256,512]{1,0:T(8,128)(2,1)S(1)}, u32[]{:S(2)}, u32[]{:S(2)}) collective-permute-start(bf16[256,512]{1,0:T(8,128)(2,1)S(1)} %take.2), channel_id=1, source_target_pairs={{0,4},{4,0},{8,12},{12,8},{16,20},{20,16},{24,28},{28,24},{1,5},{5... | collective-permute-start | bytes 786440 | tf_op jit(solution)/shard_map/ppermute | solution.py:23
  4.9 0.1 collective-permute-start.1
  5.0 0.0 copy-done.1
  5.1 2.1 %collective-permute-start.6 = (bf16[256,512]{1,0:T(8,128)(2,1)S(1)}, bf16[256,512]{1,0:T(8,128)(2,1)S(1)}, u32[]{:S(2)}, u32[]{:S(2)}) collective-permute-start(bf16[256,512]{1,0:T(8,128)(2,1)S(1)} %get-tuple-element.13), channel_id=1, source_target_pairs={{0,8},{4,28},{8,16},{12,4},{16,24},{20,12},{24,0},{28,20},{1,9},{5... | collective-permute-start | bytes 786440 | tf_op jit(solution)/shard_map/ppermute | solution.py:23
  7.2 3.5 %collective-permute-start.4 = (bf16[256,512]{1,0:T(8,128)(2,1)S(1)}, bf16[256,512]{1,0:T(8,128)(2,1)S(1)}, u32[]{:S(2)}, u32[]{:S(2)}) collective-permute-start(bf16[256,512]{1,0:T(8,128)(2,1)S(1)} %get-tuple-element.14), channel_id=1, source_target_pairs={{0,4},{4,0},{8,12},{12,8},{16,20},{20,16},{24,28},{28,24},{1,5},{5... | collective-permute-start | bytes 786440 | tf_op jit(solution)/shard_map/ppermute | solution.py:23
  10.7 0.0 copy-done.2
  10.7 0.0 copy-done.3
  10.7 1.2 %select_reduce_fusion = f32[512]{0:T(512)S(1)} fusion(f32[4096]{0:T(1024)S(1)} %copy-done.2, s32[512]{0:T(512)S(1)} %copy-done.3), kind=kLoop, calls=%fused_computation | loop fusion | flops 6290944 | bytes 20480 | tf_op jit(solution)/shard_map/reduce_sum | solution.py:150
  11.9 0.1 collective-permute-done.near.refs_1_
  12.0 2.1 %collective-permute-start.7 = (bf16[256,512]{1,0:T(8,128)(2,1)S(1)}, bf16[256,512]{1,0:T(8,128)(2,1)S(1)}, u32[]{:S(2)}, u32[]{:S(2)}) collective-permute-start(bf16[256,512]{1,0:T(8,128)(2,1)S(1)} %collective-permute-done.near.refs_1_), channel_id=1, source_target_pairs={{0,8},{4,28},{8,16},{12,4},{16,24},{20,12},{24,0},{28,20},{1,9},{5... | collective-permute-start | bytes 786440 | tf_op jit(solution)/shard_map/ppermute | solution.py:23
  14.1 3.5 %collective-permute-done.1.refs_2_ = bf16[256,512]{1,0:T(8,128)(2,1)S(1)} collective-permute-done((bf16[256,512]{1,0:T(8,128)(2,1)S(1)}, bf16[256,512]{1,0:T(8,128)(2,1)S(1)}, u32[]{:S(2)}, u32[]{:S(2)}) %collective-permute-start.1) | collective-permute-done | bytes 262176 | tf_op jit(solution)/shard_map/ppermute | solution.py:23
  17.6 2.1 %collective-permute-start.2 = (bf16[256,512]{1,0:T(8,128)(2,1)S(1)}, bf16[256,512]{1,0:T(8,128)(2,1)S(1)}, u32[]{:S(2)}, u32[]{:S(2)}) collective-permute-start(bf16[256,512]{1,0:T(8,128)(2,1)S(1)} %collective-permute-done.1.refs_2_), channel_id=1, source_target_pairs={{0,8},{4,28},{8,16},{12,4},{16,24},{20,12},{24,0},{28,20},{1,9},{5... | collective-permute-start | bytes 786440 | tf_op jit(solution)/shard_map/ppermute | solution.py:23
  19.8 0.1 multiply_convert_fusion.left
  19.9 2.5 %collective-permute-done.4.refs_3_ = bf16[256,512]{1,0:T(8,128)(2,1)S(1)} collective-permute-done((bf16[256,512]{1,0:T(8,128)(2,1)S(1)}, bf16[256,512]{1,0:T(8,128)(2,1)S(1)}, u32[]{:S(2)}, u32[]{:S(2)}) %collective-permute-start.4) | collective-permute-done | bytes 262176 | tf_op jit(solution)/shard_map/ppermute | solution.py:23
  22.4 1.8 %collective-permute-start.5 = (bf16[256,512]{1,0:T(8,128)(2,1)S(1)}, bf16[256,512]{1,0:T(8,128)(2,1)S(1)}, u32[]{:S(2)}, u32[]{:S(2)}) collective-permute-start(bf16[256,512]{1,0:T(8,128)(2,1)S(1)} %collective-permute-done.4.refs_3_), channel_id=1, source_target_pairs={{0,8},{4,28},{8,16},{12,4},{16,24},{20,12},{24,0},{28,20},{1,9},{5... | collective-permute-start | bytes 786440 | tf_op jit(solution)/shard_map/ppermute | solution.py:23
  24.2 2.3 %collective-permute-done.2.far.refs_6_ = bf16[256,512]{1,0:T(8,128)(2,1)S(1)} collective-permute-done((bf16[256,512]{1,0:T(8,128)(2,1)S(1)}, bf16[256,512]{1,0:T(8,128)(2,1)S(1)}, u32[]{:S(2)}, u32[]{:S(2)}) %collective-permute-start.2) | collective-permute-done | bytes 262176 | tf_op jit(solution)/shard_map/ppermute | solution.py:23
  26.5 0.3 end_blocks.1
  26.8 1.4 %collective-permute-start.3 = (bf16[3,128,128]{2,1,0:T(8,128)(2,1)S(1)}, bf16[3,128,128]{2,1,0:T(8,128)(2,1)S(1)}, u32[]{:S(2)}, u32[]{:S(2)}) collective-permute-start(bf16[3,128,128]{2,1,0:T(8,128)(2,1)S(1)} %end_blocks.1), channel_id=1, source_target_pairs={{0,4},{4,0},{8,12},{12,8},{16,20},{20,16},{24,28},{28,24},{1,5},{5... | collective-permute-start | bytes 294920 | tf_op jit(solution)/shard_map/ppermute | solution.py:23
  28.1 0.0 collective-permute-done.6.refs_4_
  28.1 0.0 collective-permute-done.7.refs_5_
  28.1 1.8 %early_blocks.1.refs_1_ = bf16[6,22,128,128]{3,2,1,0:T(8,128)(2,1)S(1)} custom-call(bf16[768,512]{1,0:T(8,128)(2,1)S(1)} %multiply_convert_fusion.left, bf16[768,512]{1,0:T(8,128)(2,1)S(1)} %copy-done.1, bf16[256,512]{1,0:T(8,128)(2,1)S(1)} %collective-permute-done.near.refs_1_, bf16[256,512]{1,0:T(8,128)(2,1)S(1)} %collective-permute-done.1.refs_2_, ...), custom_call_target="tpu_custom_call" | custom-call | flops 20000000000 | bytes 1 | tf_op jit(solution)/shard_map/early_blocks/pallas_call | solution.py:61
  29.9 2.0 %collective-permute-done.5.refs_0_ = bf16[256,512]{1,0:T(8,128)(2,1)S(1)} collective-permute-done((bf16[256,512]{1,0:T(8,128)(2,1)S(1)}, bf16[256,512]{1,0:T(8,128)(2,1)S(1)}, u32[]{:S(2)}, u32[]{:S(2)}) %collective-permute-start.5) | collective-permute-done | bytes 262176 | tf_op jit(solution)/shard_map/ppermute | solution.py:23
  31.9 0.0 collective-permute-done.3.from_partner
  32.0 1.2 %late_blocks.1 = (bf16[6,22,128,128]{3,2,1,0:T(8,128)(2,1)S(1)}, bf16[6,3,128,128]{3,2,1,0:T(8,128)(2,1)S(1)}, bf16[6,3,128,128]{3,2,1,0:T(8,128)(2,1)S(1)}, bf1...) custom-call(s32[6,12]{1,0:T(8,128)S(1)} %add_select_fusion.after.places, ...), custom_call_target="tpu_custom_call", output_to_operand_aliasing={{0}: (4, {})} | custom-call | flops 1 | bytes 1 | tf_op jit(solution)/shard_map/late_blocks/pallas_call | solution.py:111
  33.1 0.1 collective-permute-start.9
  33.2 0.5 collective-permute-start.8
  33.7 1.5 %collective-permute-done.9 = bf16[6,3,128,128]{3,2,1,0:T(8,128)(2,1)S(1)} collective-permute-done((bf16[6,3,128,128]{3,2,1,0:T(8,128)(2,1)S(1)}, bf16[6,3,128,128]{3,2,1,0:T(8,128)(2,1)S(1)}, u32[]{:S(2)}, u32[]{:S(2)}) %collective-permute-start.9) | collective-permute-done | bytes 589856 | tf_op jit(solution)/shard_map/ppermute | solution.py:23
  35.2 0.2 add_convert_fusion.1
  35.4 1.6 %collective-permute-start.10 = (bf16[6,3,128,128]{3,2,1,0:T(8,128)(2,1)S(1)}, bf16[6,3,128,128]{3,2,1,0:T(8,128)(2,1)S(1)}, u32[]{:S(2)}, u32[]{:S(2)}) collective-permute-start(bf16[6,3,128,128]{3,2,1,0:T(8,128)(2,1)S(1)} %add_convert_fusion.1), channel_id=1, source_target_pairs={{0,2},{1,3},{2,0},{3,1},{4,6},{5,7},{6,4},{7,5},{8,10},{9,11},{10,... | collective-permute-start | bytes 1769480 | tf_op jit(solution)/shard_map/ppermute | solution.py:23
  36.9 0.0 collective-permute-done.8
  36.9 13.9 %collective-permute-done.10 = bf16[6,3,128,128]{3,2,1,0:T(8,128)(2,1)S(1)} collective-permute-done((bf16[6,3,128,128]{3,2,1,0:T(8,128)(2,1)S(1)}, bf16[6,3,128,128]{3,2,1,0:T(8,128)(2,1)S(1)}, u32[]{:S(2)}, u32[]{:S(2)}) %collective-permute-start.10) | collective-permute-done | bytes 589856 | tf_op jit(solution)/shard_map/ppermute | solution.py:23
  50.8 1.1 %add_convert_fusion = bf16[6,3,128,128]{3,2,1,0:T(8,128)(2,1)} fusion(bf16[6,3,128,128]{3,2,1,0:T(8,128)(2,1)S(1)} %collective-permute-done.10, bf16[6,3,128,128]{3,2,1,0:T(8,128)(2,1)S(1)} %collective-permute-done.8, bf16[6,3,128,128]{3,2,1,0:T(8,128)(2,1)S(1)} %get-tuple-element.9), kind=kLoop, calls=%fused_computation.3 | loop fusion | flops 1769472 | bytes 2359296 | tf_op jit(solution)/shard_map/convert_element_type | solution.py:174
  (3 shorter events, 0.1 us)
Async XLA Ops:
  0.7 1.1 %copy-start = (bf16[768,512]{1,0:T(8,128)(2,1)S(1)}, bf16[768,512]{1,0:T(8,128)(2,1)}, u32[]{:S(2)}) copy-start(bf16[768,512]{1,0:T(8,128)(2,1)} %refs_0_.1) | copy-start | bytes 2359300
  1.8 3.2 %copy-start.1 = (bf16[768,512]{1,0:T(8,128)(2,1)S(1)}, bf16[768,512]{1,0:T(8,128)(2,1)}, u32[]{:S(2)}) copy-start(bf16[768,512]{1,0:T(8,128)(2,1)} %refs_0_.1) | copy-start | bytes 2359300
  1.8 8.9 %copy-start.2 = (f32[4096]{0:T(1024)S(1)}, f32[4096]{0:T(1024)}, u32[]{:S(2)}) copy-start(f32[4096]{0:T(1024)} %param.5) | copy-start | bytes 49156
  1.8 8.9 %copy-start.3 = (s32[512]{0:T(512)S(1)}, s32[512]{0:T(512)}, u32[]{:S(2)}) copy-start(s32[512]{0:T(512)} %param.6) | copy-start | bytes 6148
  1.9 10.2 %collective-permute-start = (bf16[256,512]{1,0:T(8,128)(2,1)S(1)}, bf16[256,512]{1,0:T(8,128)(2,1)S(1)}, u32[]{:S(2)}, u32[]{:S(2)}) collective-permute-start(bf16[256,512]{1,0:T(8,128)(2,1)S(1)} %take.2), channel_id=1, source_target_pairs={{0,4},{4,0},{8,12},{12,8},{16,20},{20,16},{24,28},{28,24},{1,5},{5... | collective-permute-start | bytes 786440 | tf_op jit(solution)/shard_map/ppermute | solution.py:23
  4.9 12.7 %collective-permute-start.1 = (bf16[256,512]{1,0:T(8,128)(2,1)S(1)}, bf16[256,512]{1,0:T(8,128)(2,1)S(1)}, u32[]{:S(2)}, u32[]{:S(2)}) collective-permute-start(bf16[256,512]{1,0:T(8,128)(2,1)S(1)} %take.3), channel_id=1, source_target_pairs={{0,4},{4,0},{8,12},{12,8},{16,20},{20,16},{24,28},{28,24},{1,5},{5... | collective-permute-start | bytes 786440 | tf_op jit(solution)/shard_map/ppermute | solution.py:23
  5.1 23.1 %collective-permute-start.6 = (bf16[256,512]{1,0:T(8,128)(2,1)S(1)}, bf16[256,512]{1,0:T(8,128)(2,1)S(1)}, u32[]{:S(2)}, u32[]{:S(2)}) collective-permute-start(bf16[256,512]{1,0:T(8,128)(2,1)S(1)} %get-tuple-element.13), channel_id=1, source_target_pairs={{0,8},{4,28},{8,16},{12,4},{16,24},{20,12},{24,0},{28,20},{1,9},{5... | collective-permute-start | bytes 786440 | tf_op jit(solution)/shard_map/ppermute | solution.py:23
  7.2 15.3 %collective-permute-start.4 = (bf16[256,512]{1,0:T(8,128)(2,1)S(1)}, bf16[256,512]{1,0:T(8,128)(2,1)S(1)}, u32[]{:S(2)}, u32[]{:S(2)}) collective-permute-start(bf16[256,512]{1,0:T(8,128)(2,1)S(1)} %get-tuple-element.14), channel_id=1, source_target_pairs={{0,4},{4,0},{8,12},{12,8},{16,20},{20,16},{24,28},{28,24},{1,5},{5... | collective-permute-start | bytes 786440 | tf_op jit(solution)/shard_map/ppermute | solution.py:23
  12.0 16.1 %collective-permute-start.7 = (bf16[256,512]{1,0:T(8,128)(2,1)S(1)}, bf16[256,512]{1,0:T(8,128)(2,1)S(1)}, u32[]{:S(2)}, u32[]{:S(2)}) collective-permute-start(bf16[256,512]{1,0:T(8,128)(2,1)S(1)} %collective-permute-done.near.refs_1_), channel_id=1, source_target_pairs={{0,8},{4,28},{8,16},{12,4},{16,24},{20,12},{24,0},{28,20},{1,9},{5... | collective-permute-start | bytes 786440 | tf_op jit(solution)/shard_map/ppermute | solution.py:23
  17.6 8.8 %collective-permute-start.2 = (bf16[256,512]{1,0:T(8,128)(2,1)S(1)}, bf16[256,512]{1,0:T(8,128)(2,1)S(1)}, u32[]{:S(2)}, u32[]{:S(2)}) collective-permute-start(bf16[256,512]{1,0:T(8,128)(2,1)S(1)} %collective-permute-done.1.refs_2_), channel_id=1, source_target_pairs={{0,8},{4,28},{8,16},{12,4},{16,24},{20,12},{24,0},{28,20},{1,9},{5... | collective-permute-start | bytes 786440 | tf_op jit(solution)/shard_map/ppermute | solution.py:23
  22.4 9.5 %collective-permute-start.5 = (bf16[256,512]{1,0:T(8,128)(2,1)S(1)}, bf16[256,512]{1,0:T(8,128)(2,1)S(1)}, u32[]{:S(2)}, u32[]{:S(2)}) collective-permute-start(bf16[256,512]{1,0:T(8,128)(2,1)S(1)} %collective-permute-done.4.refs_3_), channel_id=1, source_target_pairs={{0,8},{4,28},{8,16},{12,4},{16,24},{20,12},{24,0},{28,20},{1,9},{5... | collective-permute-start | bytes 786440 | tf_op jit(solution)/shard_map/ppermute | solution.py:23
  26.8 5.2 %collective-permute-start.3 = (bf16[3,128,128]{2,1,0:T(8,128)(2,1)S(1)}, bf16[3,128,128]{2,1,0:T(8,128)(2,1)S(1)}, u32[]{:S(2)}, u32[]{:S(2)}) collective-permute-start(bf16[3,128,128]{2,1,0:T(8,128)(2,1)S(1)} %end_blocks.1), channel_id=1, source_target_pairs={{0,4},{4,0},{8,12},{12,8},{16,20},{20,16},{24,28},{28,24},{1,5},{5... | collective-permute-start | bytes 294920 | tf_op jit(solution)/shard_map/ppermute | solution.py:23
  33.1 2.1 %collective-permute-start.9 = (bf16[6,3,128,128]{3,2,1,0:T(8,128)(2,1)S(1)}, bf16[6,3,128,128]{3,2,1,0:T(8,128)(2,1)S(1)}, u32[]{:S(2)}, u32[]{:S(2)}) collective-permute-start(bf16[6,3,128,128]{3,2,1,0:T(8,128)(2,1)S(1)} %get-tuple-element.12), channel_id=1, source_target_pairs={{0,1},{1,0},{2,3},{3,2},{4,5},{5,4},{6,7},{7,6},{8,9},{9,8},{10,11... | collective-permute-start | bytes 1769480 | tf_op jit(solution)/shard_map/ppermute | solution.py:23
  33.2 3.7 %collective-permute-start.8 = (bf16[6,3,128,128]{3,2,1,0:T(8,128)(2,1)S(1)}, bf16[6,3,128,128]{3,2,1,0:T(8,128)(2,1)S(1)}, u32[]{:S(2)}, u32[]{:S(2)}) collective-permute-start(bf16[6,3,128,128]{3,2,1,0:T(8,128)(2,1)S(1)} %get-tuple-element.10), channel_id=1, source_target_pairs={{0,1},{1,0},{2,3},{3,2},{4,5},{5,4},{6,7},{7,6},{8,9},{9,8},{10,11... | collective-permute-start | bytes 1769480 | tf_op jit(solution)/shard_map/ppermute | solution.py:23
  35.4 15.4 %collective-permute-start.10 = (bf16[6,3,128,128]{3,2,1,0:T(8,128)(2,1)S(1)}, bf16[6,3,128,128]{3,2,1,0:T(8,128)(2,1)S(1)}, u32[]{:S(2)}, u32[]{:S(2)}) collective-permute-start(bf16[6,3,128,128]{3,2,1,0:T(8,128)(2,1)S(1)} %add_convert_fusion.1), channel_id=1, source_target_pairs={{0,2},{1,3},{2,0},{3,1},{4,6},{5,7},{6,4},{7,5},{8,10},{9,11},{10,... | collective-permute-start | bytes 1769480 | tf_op jit(solution)/shard_map/ppermute | solution.py:23
where the time goes:
time: 52.1 us; the launch traced here: 51.9 us
  waiting for transfers between devices  25.8 us (50%)
  starting transfers between devices  18.3 us (35%)
  other arithmetic  3.32 us (6%)
  Pallas kernels  3.23 us (6%)
  local copies, waits for them, and re-layouts  1.18 us (2%)
    ppermute x11, waiting for transfers between devices, move(): lax.ppermute(value, axis, [(s, target(s) % count) for s in range(count)])  25.8 us
    ppermute x11, starting transfers between devices, move(): lax.ppermute(value, axis, [(s, target(s) % count) for s in range(count)])  18.3 us
    pallas_call x1, Pallas kernels, early_blocks(): pl.pallas_call(functools.partial(early_kernel, list(pieces)), out_shape=j...  1.78 us
    reduce_sum x1, other arithmetic, per_device(): jnp.sum(jnp.where(picks, occupation[None, :], jnp.float32(0.0)), axis=1)  1.22 us
    pallas_call x1, Pallas kernels, late_blocks(): pl.pallas_call(functools.partial(blocks_kernel, share, list(pieces)), out...  1.15 us
    unnamed x8, local copies, waits for them, and re-layouts  1.14 us
    convert_element_type x1, other arithmetic, per_device(): return (near + got.astype(jnp.float32)).astype(jnp.bfloat16)  1.09 us
  transfers between devices with their start and end apart: 11, of which 7 were waited for; matrix products, arithmetic and copies ran while one was open for 3% of the time, Pallas kernels for 4%

commit v1 on v0

--- a/solution.py
+++ b/solution.py
@@ -120,21 +120,24 @@
     )(places, left, from_partner, *pieces.values(), dense)[1:]
 
 
-def take_kernel(near, slab, after, out):
+def take_kernel(which, slab, after, out, done):
     odd = lax.rem(lax.axis_index("wide"), 2)
-    row = (1 - odd if near else odd) * 2 * PAIR * B
-    out[...] = slab[pl.ds(pl.multiple_of(row, PAIR * B), PAIR * B), :]
+    row = {"end": odd * 2, "middle": 1, "near": (1 - odd) * 2}[which] * PAIR * B
+    copy = pltpu.make_async_copy(slab.at[pl.ds(pl.multiple_of(row, PAIR * B), PAIR * B), :], out, done)
+    copy.start()
+    copy.wait()
 
 
-def take(slab, near, after):
+def take(slab, which, after):
     return pl.pallas_call(
-        functools.partial(take_kernel, near),
+        functools.partial(take_kernel, which),
         out_shape=jax.ShapeDtypeStruct((PAIR * B, slab.shape[1]), slab.dtype),
-        in_specs=[VMEM] * 2,
+        in_specs=[pl.BlockSpec(memory_space=pl.ANY), VMEM],
         out_specs=VMEM,
+        scratch_shapes=[pltpu.SemaphoreType.DMA],
         compiler_params=pltpu.CompilerParams(vmem_limit_bytes=LIMIT),
         cost_estimate=SHORT,
-        name="take",
+        name=f"take_{which}",
     )(slab, after)
 
 
@@ -150,13 +153,15 @@
     weight = jnp.sum(jnp.where(picks, occupation[None, :], jnp.float32(0.0)), axis=1)
     scaled = (slab.astype(jnp.float32) * weight[None, :]).astype(jnp.bfloat16)
 
-    near_rows = lax.dynamic_slice_in_dim(slab, (1 - odd) * 2 * rows, rows, 0)
-    end_rows = lax.dynamic_slice_in_dim(slab, odd * 2 * rows, rows, 0)
     early = {0: slab}
-    early[-2] = move(take(slab, True, places), "wide", partner)
-    early[-6] = move(take(slab, False, places), "wide", partner)
-    early[-4] = move(slab[rows : 2 * rows], "wide", partner)
-    early[12] = move(near_rows, "wide", outward)
+    near_rows = take(slab, "near", jnp.zeros((8, 128), jnp.float32))
+    end_rows = take(slab, "end", jnp.zeros((8, 128), jnp.float32))
+    middle_rows = take(slab, "middle", places)
+    later_rows = take(slab, "near", places.astype(jnp.float32))
+    early[-2] = move(near_rows, "wide", partner)
+    early[-6] = move(end_rows, "wide", partner)
+    early[-4] = move(middle_rows, "wide", partner)
+    early[12] = move(later_rows, "wide", outward)
     early[10] = move(early[-2], "wide", outward)
     early[6] = move(early[-6], "wide", outward)
     late = {8: move(early[-4], "wide", outward)}

time: 52.1 us -> 53.3 us (1.023)
  waiting for transfers between devices: 25.8 us -> 30.8 us
  starting transfers between devices: 18.3 us -> 15.1 us
  other arithmetic: 3.32 us -> 2.63 us
    ppermute x11, waiting for transfers between devices: 25.8 us -> 30.8 us  [move(): lax.ppermute(value, axis, [(s, target(s) % count) for s in range(count)])]
    ppermute x11, starting transfers between devices: 18.3 us -> 15.1 us  [move(): lax.ppermute(value, axis, [(s, target(s) % count) for s in range(count)])]
    select_n x1 -> x0, other arithmetic: 0.7 us -> none  [per_device(): places = jnp.mod(pattern - (lax.axis_index('wide') * CL - REACH), clusters)]
    unnamed x8 -> x10, local copies, waits for them, and re-layouts: 1.14 us -> 1.16 us
  transfers between devices with their start and end apart: 11 -> 11, of which waited for: 7 -> 8; matrix products, arithmetic and copies ran while one was open for 3% -> 3% of each run, Pallas kernels for 4% -> 4%
where the time goes in v1:
time: 53.3 us; the launch traced here: 53.1 us
  waiting for transfers between devices  30.8 us (58%)
  starting transfers between devices  15.1 us (28%)
  Pallas kernels  3.31 us (6%)
  other arithmetic  2.63 us (5%)
  local copies, waits for them, and re-layouts  1.17 us (2%)
    ppermute x11, waiting for transfers between devices, move(): lax.ppermute(value, axis, [(s, target(s) % count) for s in range(count)])  30.8 us
    ppermute x11, starting transfers between devices, move(): lax.ppermute(value, axis, [(s, target(s) % count) for s in range(count)])  15.1 us
    pallas_call x1, Pallas kernels, early_blocks(): pl.pallas_call(functools.partial(early_kernel, list(pieces)), out_shape=j...  1.77 us
    reduce_sum x1, other arithmetic, per_device(): jnp.sum(jnp.where(picks, occupation[None, :], jnp.float32(0.0)), axis=1)  1.22 us
    unnamed x10, local copies, waits for them, and re-layouts  1.16 us
    pallas_call x1, Pallas kernels, late_blocks(): pl.pallas_call(functools.partial(blocks_kernel, share, list(pieces)), out...  1.15 us
    convert_element_type x1, other arithmetic, per_device(): return (near + got.astype(jnp.float32)).astype(jnp.bfloat16)  1.09 us
  transfers between devices with their start and end apart: 11, of which 8 were waited for; matrix products, arithmetic and copies ran while one was open for 3% of the time, Pallas kernels for 4%

profile of v1, /device:TPU:0, one launch (start us, length us, event | category | flops | bytes accessed | tf_op | source)
XLA Modules:
  0.0 53.1 jit_solution(7003835629232889743)
XLA Ops:
  0.0 0.0 copy-start.2
  0.0 0.0 copy-start
  0.0 1.1 %copy-done = bf16[768,512]{1,0:T(8,128)(2,1)S(1)} copy-done((bf16[768,512]{1,0:T(8,128)(2,1)S(1)}, bf16[768,512]{1,0:T(8,128)(2,1)}, u32[]{:S(2)}) %copy-start) | copy-done | bytes 786456
  1.1 0.0 copy-start.1
  1.2 0.0 copy-start.3
  1.2 0.0 copy-start.4
  1.2 3.0 %collective-permute-start = (bf16[256,512]{1,0:T(8,128)(2,1)S(1)}, bf16[256,512]{1,0:T(8,128)(2,1)S(1)}, u32[]{:S(2)}, u32[]{:S(2)}) collective-permute-start(bf16[256,512]{1,0:T(8,128)(2,1)S(1)} %take_near.2), channel_id=1, source_target_pairs={{0,4},{4,0},{8,12},{12,8},{16,20},{20,16},{24,28},{28,24},{1,5},{5... | collective-permute-start | bytes 786440 | tf_op jit(solution)/shard_map/ppermute | solution.py:23
  4.3 0.1 collective-permute-start.1
  4.4 0.0 copy-done.2
  4.4 0.0 copy-done.1
  4.4 2.1 %collective-permute-start.4 = (bf16[256,512]{1,0:T(8,128)(2,1)S(1)}, bf16[256,512]{1,0:T(8,128)(2,1)S(1)}, u32[]{:S(2)}, u32[]{:S(2)}) collective-permute-start(bf16[256,512]{1,0:T(8,128)(2,1)S(1)} %take_middle.1), channel_id=1, source_target_pairs={{0,4},{4,0},{8,12},{12,8},{16,20},{20,16},{24,28},{28,24},{1,5},{5... | collective-permute-start | bytes 786440 | tf_op jit(solution)/shard_map/ppermute | solution.py:23
  6.5 1.6 %collective-permute-start.6 = (bf16[256,512]{1,0:T(8,128)(2,1)S(1)}, bf16[256,512]{1,0:T(8,128)(2,1)S(1)}, u32[]{:S(2)}, u32[]{:S(2)}) collective-permute-start(bf16[256,512]{1,0:T(8,128)(2,1)S(1)} %take_near.3), channel_id=1, source_target_pairs={{0,8},{4,28},{8,16},{12,4},{16,24},{20,12},{24,0},{28,20},{1,9},{5... | collective-permute-start | bytes 786440 | tf_op jit(solution)/shard_map/ppermute | solution.py:23
  8.2 0.0 copy-done.3
  8.2 0.0 copy-done.4
  8.2 1.2 %select_reduce_fusion = f32[512]{0:T(512)S(1)} fusion(f32[4096]{0:T(1024)S(1)} %copy-done.3, s32[512]{0:T(512)S(1)} %copy-done.4), kind=kLoop, calls=%fused_computation | loop fusion | flops 6290944 | bytes 20480 | tf_op jit(solution)/shard_map/reduce_sum | solution.py:153
  9.4 2.0 %collective-permute-done.near.refs_1_ = bf16[256,512]{1,0:T(8,128)(2,1)S(1)} collective-permute-done((bf16[256,512]{1,0:T(8,128)(2,1)S(1)}, bf16[256,512]{1,0:T(8,128)(2,1)S(1)}, u32[]{:S(2)}, u32[]{:S(2)}) %collective-permute-start) | collective-permute-done | bytes 262176 | tf_op jit(solution)/shard_map/ppermute | solution.py:23
  11.4 2.1 %collective-permute-start.7 = (bf16[256,512]{1,0:T(8,128)(2,1)S(1)}, bf16[256,512]{1,0:T(8,128)(2,1)S(1)}, u32[]{:S(2)}, u32[]{:S(2)}) collective-permute-start(bf16[256,512]{1,0:T(8,128)(2,1)S(1)} %collective-permute-done.near.refs_1_), channel_id=1, source_target_pairs={{0,8},{4,28},{8,16},{12,4},{16,24},{20,12},{24,0},{28,20},{1,9},{5... | collective-permute-start | bytes 786440 | tf_op jit(solution)/shard_map/ppermute | solution.py:23
  13.5 3.5 %collective-permute-done.1.refs_2_ = bf16[256,512]{1,0:T(8,128)(2,1)S(1)} collective-permute-done((bf16[256,512]{1,0:T(8,128)(2,1)S(1)}, bf16[256,512]{1,0:T(8,128)(2,1)S(1)}, u32[]{:S(2)}, u32[]{:S(2)}) %collective-permute-start.1) | collective-permute-done | bytes 262176 | tf_op jit(solution)/shard_map/ppermute | solution.py:23
  17.0 2.1 %collective-permute-start.2 = (bf16[256,512]{1,0:T(8,128)(2,1)S(1)}, bf16[256,512]{1,0:T(8,128)(2,1)S(1)}, u32[]{:S(2)}, u32[]{:S(2)}) collective-permute-start(bf16[256,512]{1,0:T(8,128)(2,1)S(1)} %collective-permute-done.1.refs_2_), channel_id=1, source_target_pairs={{0,8},{4,28},{8,16},{12,4},{16,24},{20,12},{24,0},{28,20},{1,9},{5... | collective-permute-start | bytes 786440 | tf_op jit(solution)/shard_map/ppermute | solution.py:23
  19.1 0.1 multiply_convert_fusion.left
  19.3 2.5 %collective-permute-done.4.refs_3_ = bf16[256,512]{1,0:T(8,128)(2,1)S(1)} collective-permute-done((bf16[256,512]{1,0:T(8,128)(2,1)S(1)}, bf16[256,512]{1,0:T(8,128)(2,1)S(1)}, u32[]{:S(2)}, u32[]{:S(2)}) %collective-permute-start.4) | collective-permute-done | bytes 262176 | tf_op jit(solution)/shard_map/ppermute | solution.py:23
  21.8 1.8 %collective-permute-start.5 = (bf16[256,512]{1,0:T(8,128)(2,1)S(1)}, bf16[256,512]{1,0:T(8,128)(2,1)S(1)}, u32[]{:S(2)}, u32[]{:S(2)}) collective-permute-start(bf16[256,512]{1,0:T(8,128)(2,1)S(1)} %collective-permute-done.4.refs_3_), channel_id=1, source_target_pairs={{0,8},{4,28},{8,16},{12,4},{16,24},{20,12},{24,0},{28,20},{1,9},{5... | collective-permute-start | bytes 786440 | tf_op jit(solution)/shard_map/ppermute | solution.py:23
  23.6 4.7 %collective-permute-done.2.far.refs_6_ = bf16[256,512]{1,0:T(8,128)(2,1)S(1)} collective-permute-done((bf16[256,512]{1,0:T(8,128)(2,1)S(1)}, bf16[256,512]{1,0:T(8,128)(2,1)S(1)}, u32[]{:S(2)}, u32[]{:S(2)}) %collective-permute-start.2) | collective-permute-done | bytes 262176 | tf_op jit(solution)/shard_map/ppermute | solution.py:23
  28.3 0.3 end_blocks.1
  28.5 0.1 collective-permute-start.3
  28.6 0.0 collective-permute-done.6.refs_4_
  28.6 0.0 collective-permute-done.7.refs_5_
  28.6 1.8 %early_blocks.1.refs_1_ = bf16[6,22,128,128]{3,2,1,0:T(8,128)(2,1)S(1)} custom-call(bf16[768,512]{1,0:T(8,128)(2,1)S(1)} %multiply_convert_fusion.left, bf16[768,512]{1,0:T(8,128)(2,1)S(1)} %copy-done.1, bf16[256,512]{1,0:T(8,128)(2,1)S(1)} %collective-permute-done.near.refs_1_, bf16[256,512]{1,0:T(8,128)(2,1)S(1)} %collective-permute-done.1.refs_2_, ...), custom_call_target="tpu_custom_call" | custom-call | flops 20000000000 | bytes 1 | tf_op jit(solution)/shard_map/early_blocks/pallas_call | solution.py:61
  30.4 2.1 %collective-permute-done.5.refs_0_ = bf16[256,512]{1,0:T(8,128)(2,1)S(1)} collective-permute-done((bf16[256,512]{1,0:T(8,128)(2,1)S(1)}, bf16[256,512]{1,0:T(8,128)(2,1)S(1)}, u32[]{:S(2)}, u32[]{:S(2)}) %collective-permute-start.5) | collective-permute-done | bytes 262176 | tf_op jit(solution)/shard_map/ppermute | solution.py:23
  32.5 0.7 %collective-permute-done.3.from_partner = bf16[3,128,128]{2,1,0:T(8,128)(2,1)S(1)} collective-permute-done((bf16[3,128,128]{2,1,0:T(8,128)(2,1)S(1)}, bf16[3,128,128]{2,1,0:T(8,128)(2,1)S(1)}, u32[]{:S(2)}, u32[]{:S(2)}) %collective-permute-start.3) | collective-permute-done | bytes 98336 | tf_op jit(solution)/shard_map/ppermute | solution.py:23
  33.2 1.2 %late_blocks.1 = (bf16[6,22,128,128]{3,2,1,0:T(8,128)(2,1)S(1)}, bf16[6,3,128,128]{3,2,1,0:T(8,128)(2,1)S(1)}, bf16[6,3,128,128]{3,2,1,0:T(8,128)(2,1)S(1)}, bf1...) custom-call(s32[6,12]{1,0:T(8,128)S(1)} %get-tuple-element.14.after.places, ...), custom_call_target="tpu_custom_call", output_to_operand_aliasing={{0}: (4, {})} | custom-call | flops 1 | bytes 1 | tf_op jit(solution)/shard_map/late_blocks/pallas_call | solution.py:111
  34.4 0.1 collective-permute-start.9
  34.5 0.5 collective-permute-start.8
  35.0 1.5 %collective-permute-done.9 = bf16[6,3,128,128]{3,2,1,0:T(8,128)(2,1)S(1)} collective-permute-done((bf16[6,3,128,128]{3,2,1,0:T(8,128)(2,1)S(1)}, bf16[6,3,128,128]{3,2,1,0:T(8,128)(2,1)S(1)}, u32[]{:S(2)}, u32[]{:S(2)}) %collective-permute-start.9) | collective-permute-done | bytes 589856 | tf_op jit(solution)/shard_map/ppermute | solution.py:23
  36.4 0.2 add_convert_fusion.1
  36.6 1.6 %collective-permute-start.10 = (bf16[6,3,128,128]{3,2,1,0:T(8,128)(2,1)S(1)}, bf16[6,3,128,128]{3,2,1,0:T(8,128)(2,1)S(1)}, u32[]{:S(2)}, u32[]{:S(2)}) collective-permute-start(bf16[6,3,128,128]{3,2,1,0:T(8,128)(2,1)S(1)} %add_convert_fusion.1), channel_id=1, source_target_pairs={{0,2},{1,3},{2,0},{3,1},{4,6},{5,7},{6,4},{7,5},{8,10},{9,11},{10,... | collective-permute-start | bytes 1769480 | tf_op jit(solution)/shard_map/ppermute | solution.py:23
  38.2 0.0 collective-permute-done.8
  38.2 13.8 %collective-permute-done.10 = bf16[6,3,128,128]{3,2,1,0:T(8,128)(2,1)S(1)} collective-permute-done((bf16[6,3,128,128]{3,2,1,0:T(8,128)(2,1)S(1)}, bf16[6,3,128,128]{3,2,1,0:T(8,128)(2,1)S(1)}, u32[]{:S(2)}, u32[]{:S(2)}) %collective-permute-start.10) | collective-permute-done | bytes 589856 | tf_op jit(solution)/shard_map/ppermute | solution.py:23
  52.1 1.1 %add_convert_fusion = bf16[6,3,128,128]{3,2,1,0:T(8,128)(2,1)} fusion(bf16[6,3,128,128]{3,2,1,0:T(8,128)(2,1)S(1)} %collective-permute-done.10, bf16[6,3,128,128]{3,2,1,0:T(8,128)(2,1)S(1)} %collective-permute-done.8, bf16[6,3,128,128]{3,2,1,0:T(8,128)(2,1)S(1)} %get-tuple-element.9), kind=kLoop, calls=%fused_computation.3 | loop fusion | flops 1769472 | bytes 2359296 | tf_op jit(solution)/shard_map/convert_element_type | solution.py:179
  (6 shorter events, 0.1 us)
Async XLA Ops:
  0.0 4.4 %copy-start.2 = (s32[6,12]{1,0:T(8,128)S(1)}, s32[6,12]{1,0:T(8,128)}, u32[]{:S(2)}) copy-start(s32[6,12]{1,0:T(8,128)} %param.7) | copy-start | bytes 868
  0.0 1.1 %copy-start = (bf16[768,512]{1,0:T(8,128)(2,1)S(1)}, bf16[768,512]{1,0:T(8,128)(2,1)}, u32[]{:S(2)}) copy-start(bf16[768,512]{1,0:T(8,128)(2,1)} %refs_0_.1) | copy-start | bytes 2359300
  1.1 3.2 %copy-start.1 = (bf16[768,512]{1,0:T(8,128)(2,1)S(1)}, bf16[768,512]{1,0:T(8,128)(2,1)}, u32[]{:S(2)}) copy-start(bf16[768,512]{1,0:T(8,128)(2,1)} %refs_0_.1) | copy-start | bytes 2359300
  1.2 7.0 %copy-start.3 = (f32[4096]{0:T(1024)S(1)}, f32[4096]{0:T(1024)}, u32[]{:S(2)}) copy-start(f32[4096]{0:T(1024)} %param.5) | copy-start | bytes 49156
  1.2 7.0 %copy-start.4 = (s32[512]{0:T(512)S(1)}, s32[512]{0:T(512)}, u32[]{:S(2)}) copy-start(s32[512]{0:T(512)} %param.6) | copy-start | bytes 6148
  1.2 10.2 %collective-permute-start = (bf16[256,512]{1,0:T(8,128)(2,1)S(1)}, bf16[256,512]{1,0:T(8,128)(2,1)S(1)}, u32[]{:S(2)}, u32[]{:S(2)}) collective-permute-start(bf16[256,512]{1,0:T(8,128)(2,1)S(1)} %take_near.2), channel_id=1, source_target_pairs={{0,4},{4,0},{8,12},{12,8},{16,20},{20,16},{24,28},{28,24},{1,5},{5... | collective-permute-start | bytes 786440 | tf_op jit(solution)/shard_map/ppermute | solution.py:23
  4.3 12.7 %collective-permute-start.1 = (bf16[256,512]{1,0:T(8,128)(2,1)S(1)}, bf16[256,512]{1,0:T(8,128)(2,1)S(1)}, u32[]{:S(2)}, u32[]{:S(2)}) collective-permute-start(bf16[256,512]{1,0:T(8,128)(2,1)S(1)} %take_end.1), channel_id=1, source_target_pairs={{0,4},{4,0},{8,12},{12,8},{16,20},{20,16},{24,28},{28,24},{1,5},{5... | collective-permute-start | bytes 786440 | tf_op jit(solution)/shard_map/ppermute | solution.py:23
  4.4 17.3 %collective-permute-start.4 = (bf16[256,512]{1,0:T(8,128)(2,1)S(1)}, bf16[256,512]{1,0:T(8,128)(2,1)S(1)}, u32[]{:S(2)}, u32[]{:S(2)}) collective-permute-start(bf16[256,512]{1,0:T(8,128)(2,1)S(1)} %take_middle.1), channel_id=1, source_target_pairs={{0,4},{4,0},{8,12},{12,8},{16,20},{20,16},{24,28},{28,24},{1,5},{5... | collective-permute-start | bytes 786440 | tf_op jit(solution)/shard_map/ppermute | solution.py:23
  6.5 22.1 %collective-permute-start.6 = (bf16[256,512]{1,0:T(8,128)(2,1)S(1)}, bf16[256,512]{1,0:T(8,128)(2,1)S(1)}, u32[]{:S(2)}, u32[]{:S(2)}) collective-permute-start(bf16[256,512]{1,0:T(8,128)(2,1)S(1)} %take_near.3), channel_id=1, source_target_pairs={{0,8},{4,28},{8,16},{12,4},{16,24},{20,12},{24,0},{28,20},{1,9},{5... | collective-permute-start | bytes 786440 | tf_op jit(solution)/shard_map/ppermute | solution.py:23
  11.4 17.2 %collective-permute-start.7 = (bf16[256,512]{1,0:T(8,128)(2,1)S(1)}, bf16[256,512]{1,0:T(8,128)(2,1)S(1)}, u32[]{:S(2)}, u32[]{:S(2)}) collective-permute-start(bf16[256,512]{1,0:T(8,128)(2,1)S(1)} %collective-permute-done.near.refs_1_), channel_id=1, source_target_pairs={{0,8},{4,28},{8,16},{12,4},{16,24},{20,12},{24,0},{28,20},{1,9},{5... | collective-permute-start | bytes 786440 | tf_op jit(solution)/shard_map/ppermute | solution.py:23
  17.0 11.3 %collective-permute-start.2 = (bf16[256,512]{1,0:T(8,128)(2,1)S(1)}, bf16[256,512]{1,0:T(8,128)(2,1)S(1)}, u32[]{:S(2)}, u32[]{:S(2)}) collective-permute-start(bf16[256,512]{1,0:T(8,128)(2,1)S(1)} %collective-permute-done.1.refs_2_), channel_id=1, source_target_pairs={{0,8},{4,28},{8,16},{12,4},{16,24},{20,12},{24,0},{28,20},{1,9},{5... | collective-permute-start | bytes 786440 | tf_op jit(solution)/shard_map/ppermute | solution.py:23
  21.8 10.7 %collective-permute-start.5 = (bf16[256,512]{1,0:T(8,128)(2,1)S(1)}, bf16[256,512]{1,0:T(8,128)(2,1)S(1)}, u32[]{:S(2)}, u32[]{:S(2)}) collective-permute-start(bf16[256,512]{1,0:T(8,128)(2,1)S(1)} %collective-permute-done.4.refs_3_), channel_id=1, source_target_pairs={{0,8},{4,28},{8,16},{12,4},{16,24},{20,12},{24,0},{28,20},{1,9},{5... | collective-permute-start | bytes 786440 | tf_op jit(solution)/shard_map/ppermute | solution.py:23
  28.5 4.7 %collective-permute-start.3 = (bf16[3,128,128]{2,1,0:T(8,128)(2,1)S(1)}, bf16[3,128,128]{2,1,0:T(8,128)(2,1)S(1)}, u32[]{:S(2)}, u32[]{:S(2)}) collective-permute-start(bf16[3,128,128]{2,1,0:T(8,128)(2,1)S(1)} %end_blocks.1), channel_id=1, source_target_pairs={{0,4},{4,0},{8,12},{12,8},{16,20},{20,16},{24,28},{28,24},{1,5},{5... | collective-permute-start | bytes 294920 | tf_op jit(solution)/shard_map/ppermute | solution.py:23
  34.4 2.1 %collective-permute-start.9 = (bf16[6,3,128,128]{3,2,1,0:T(8,128)(2,1)S(1)}, bf16[6,3,128,128]{3,2,1,0:T(8,128)(2,1)S(1)}, u32[]{:S(2)}, u32[]{:S(2)}) collective-permute-start(bf16[6,3,128,128]{3,2,1,0:T(8,128)(2,1)S(1)} %get-tuple-element.12), channel_id=1, source_target_pairs={{0,1},{1,0},{2,3},{3,2},{4,5},{5,4},{6,7},{7,6},{8,9},{9,8},{10,11... | collective-permute-start | bytes 1769480 | tf_op jit(solution)/shard_map/ppermute | solution.py:23
  34.5 3.8 %collective-permute-start.8 = (bf16[6,3,128,128]{3,2,1,0:T(8,128)(2,1)S(1)}, bf16[6,3,128,128]{3,2,1,0:T(8,128)(2,1)S(1)}, u32[]{:S(2)}, u32[]{:S(2)}) collective-permute-start(bf16[6,3,128,128]{3,2,1,0:T(8,128)(2,1)S(1)} %get-tuple-element.10), channel_id=1, source_target_pairs={{0,1},{1,0},{2,3},{3,2},{4,5},{5,4},{6,7},{7,6},{8,9},{9,8},{10,11... | collective-permute-start | bytes 1769480 | tf_op jit(solution)/shard_map/ppermute | solution.py:23
  36.6 15.4 %collective-permute-start.10 = (bf16[6,3,128,128]{3,2,1,0:T(8,128)(2,1)S(1)}, bf16[6,3,128,128]{3,2,1,0:T(8,128)(2,1)S(1)}, u32[]{:S(2)}, u32[]{:S(2)}) collective-permute-start(bf16[6,3,128,128]{3,2,1,0:T(8,128)(2,1)S(1)} %add_convert_fusion.1), channel_id=1, source_target_pairs={{0,2},{1,3},{2,0},{3,1},{4,6},{5,7},{6,4},{7,5},{8,10},{9,11},{10,... | collective-permute-start | bytes 1769480 | tf_op jit(solution)/shard_map/ppermute | solution.py:23

commit v2 on v1

--- a/solution.py
+++ b/solution.py
@@ -53,20 +53,22 @@
                     dense[start + r, offset + REACH + h] = product[r * B : (r + 1) * B, h * B : (h + 1) * B]
 
 
-def early_kernel(marks, left, *refs):
-    add_pieces(marks, refs[:-1], left, refs[-1])
-
-
-def early_blocks(left, pieces):
-    return pl.pallas_call(
-        functools.partial(early_kernel, list(pieces)),
+def pieces_kernel(marks, left, *refs):
+    add_pieces(marks, refs[: len(marks)], left, refs[-1])
+
+
+def pieces_blocks(left, pieces, cost, dense=None):
+    held = [] if dense is None else [dense]
+    return pl.pallas_call(
+        functools.partial(pieces_kernel, list(pieces)),
         out_shape=jax.ShapeDtypeStruct((CL, CL + 2 * REACH, B, B), jnp.bfloat16),
-        in_specs=[VMEM] * (1 + len(pieces)),
-        out_specs=VMEM,
-        compiler_params=pltpu.CompilerParams(vmem_limit_bytes=LIMIT),
-        cost_estimate=LONG,
-        name="early_blocks",
-    )(left, *pieces.values())
+        in_specs=[VMEM] * (1 + len(pieces) + len(held)),
+        out_specs=VMEM,
+        input_output_aliases={1 + len(pieces): 0} if held else {},
+        compiler_params=pltpu.CompilerParams(vmem_limit_bytes=LIMIT),
+        cost_estimate=cost,
+        name="pieces_blocks",
+    )(left, *pieces.values(), *held)
 
 
 def ends_kernel(weight, near, far, out):
@@ -91,33 +93,90 @@
     )(weight[None, :], near, far)
 
 
-def blocks_kernel(share, marks, places, left, from_partner, *refs):
+def choose_kernel(share, marks, chunk, ends, places, left, from_partner, after, *refs):
     dense = refs[len(marks) + 1]
     outs = refs[len(marks) + 2 :]
     add_pieces(marks, refs[: len(marks)], left, dense)
-    for at, (c, m) in enumerate(((0, -7), (0, -8), (1, -7))):
-        dense[natural(c, c), natural(m, m) + REACH] = from_partner[at]
+    if ends:
+        for at, (c, m) in enumerate(((0, -7), (0, -8), (1, -7))):
+            dense[natural(c, c), natural(m, m) + REACH] = from_partner[at]
+    first, last = chunk
+    start = natural(first, last)
     me = lax.axis_index("narrow")
     for out, mask in zip(outs, (3, 1, 2, 0)):
         slot0 = (me ^ mask) * share
-        for c in range(CL):
+        for c in range(last - first + 1):
             for s in range(share):
-                out[c, s] = dense[c, places[c, slot0 + s]]
-
-
-def late_blocks(share, places, left, from_partner, pieces, dense):
+                out[c, s] = dense[start + c, places[start + c, slot0 + s]]
+
+
+def choose_blocks(share, chunk, ends, places, left, from_partner, after, pieces, dense):
     shapes = [jax.ShapeDtypeStruct(dense.shape, dense.dtype)]
-    shapes += [jax.ShapeDtypeStruct((CL, share, B, B), jnp.bfloat16)] * 4
-    return pl.pallas_call(
-        functools.partial(blocks_kernel, share, list(pieces)),
+    shapes += [jax.ShapeDtypeStruct((chunk[1] - chunk[0] + 1, share, B, B), jnp.bfloat16)] * 4
+    return pl.pallas_call(
+        functools.partial(choose_kernel, share, list(pieces), chunk, ends),
         out_shape=shapes,
-        in_specs=[SMEM] + [VMEM] * (3 + len(pieces)),
+        in_specs=[SMEM] + [VMEM] * (4 + len(pieces)),
         out_specs=[VMEM] * len(shapes),
-        input_output_aliases={3 + len(pieces): 0},
-        compiler_params=pltpu.CompilerParams(vmem_limit_bytes=LIMIT),
-        cost_estimate=SHORT,
-        name="late_blocks",
-    )(places, left, from_partner, *pieces.values(), dense)[1:]
+        input_output_aliases={4 + len(pieces): 0},
+        compiler_params=pltpu.CompilerParams(vmem_limit_bytes=LIMIT),
+        cost_estimate=SHORT,
+        name="choose_blocks",
+    )(places, left, from_partner, after, *pieces.values(), dense)
+
+
+def add_kernel(x, y, out):
+    out[...] = (x[...].astype(jnp.float32) + y[...].astype(jnp.float32)).astype(jnp.bfloat16)
+
+
+def add(x, y):
+    return pl.pallas_call(
+        add_kernel,
+        out_shape=jax.ShapeDtypeStruct(x.shape, x.dtype),
+        in_specs=[VMEM] * 2,
+        out_specs=VMEM,
+        compiler_params=pltpu.CompilerParams(vmem_limit_bytes=LIMIT),
+        cost_estimate=SHORT,
+        name="add",
+    )(x, y)
+
+
+def total_kernel(near, got_near, got, out):
+    total = near[...].astype(jnp.float32) + got_near[...].astype(jnp.float32) + got[...].astype(jnp.float32)
+    out[...] = total.astype(jnp.bfloat16)
+
+
+def total(near, got_near, got):
+    return pl.pallas_call(
+        total_kernel,
+        out_shape=jax.ShapeDtypeStruct(near.shape, near.dtype),
+        in_specs=[VMEM] * 3,
+        out_specs=VMEM,
+        compiler_params=pltpu.CompilerParams(vmem_limit_bytes=LIMIT),
+        cost_estimate=LONG,
+        name="total",
+    )(near, got_near, got)
+
+
+def finish_kernel(chunks, early, near, got_near, got, out):
+    start, later = [natural(first, last) for first, last in chunks]
+    for r in range(early.shape[0]):
+        out[start + r] = early[r]
+    for r in range(near.shape[0]):
+        total = near[r].astype(jnp.float32) + got_near[r].astype(jnp.float32) + got[r].astype(jnp.float32)
+        out[later + r] = total.astype(jnp.bfloat16)
+
+
+def finish(chunks, early, near, got_near, got):
+    return pl.pallas_call(
+        functools.partial(finish_kernel, chunks),
+        out_shape=jax.ShapeDtypeStruct((CL,) + near.shape[1:], near.dtype),
+        in_specs=[VMEM] * 4,
+        out_specs=VMEM,
+        compiler_params=pltpu.CompilerParams(vmem_limit_bytes=LIMIT),
+        cost_estimate=SHORT,
+        name="finish",
+    )(early, near, got_near, got)
 
 
 def take_kernel(which, slab, after, out, done):
@@ -132,7 +191,7 @@
     return pl.pallas_call(
         functools.partial(take_kernel, which),
         out_shape=jax.ShapeDtypeStruct((PAIR * B, slab.shape[1]), slab.dtype),
-        in_specs=[pl.BlockSpec(memory_space=pl.ANY), VMEM],
+        in_specs=[pl.BlockSpec(memory_space=pltpu.HBM), VMEM],
         out_specs=VMEM,
         scratch_shapes=[pltpu.SemaphoreType.DMA],
         compiler_params=pltpu.CompilerParams(vmem_limit_bytes=LIMIT),
@@ -154,29 +213,32 @@
     scaled = (slab.astype(jnp.float32) * weight[None, :]).astype(jnp.bfloat16)
 
     early = {0: slab}
-    near_rows = take(slab, "near", jnp.zeros((8, 128), jnp.float32))
     end_rows = take(slab, "end", jnp.zeros((8, 128), jnp.float32))
-    middle_rows = take(slab, "middle", places)
-    later_rows = take(slab, "near", places.astype(jnp.float32))
-    early[-2] = move(near_rows, "wide", partner)
     early[-6] = move(end_rows, "wide", partner)
-    early[-4] = move(middle_rows, "wide", partner)
-    early[12] = move(later_rows, "wide", outward)
-    early[10] = move(early[-2], "wide", outward)
+    near_rows = take(slab, "near", end_rows)
+    early[12] = move(near_rows, "wide", outward)
+    early[-4] = move(take(slab, "middle", near_rows), "wide", partner)
     early[6] = move(early[-6], "wide", outward)
-    late = {8: move(early[-4], "wide", outward)}
-    from_partner = move(end_blocks(weight, early[-2], early[6]), "wide", partner)
-
-    dense = early_blocks(scaled, early)
-    send_far, send_near, keep_far, keep_near = late_blocks(
-        share, places, scaled, from_partner, late, dense
-    )
-    got_far = move(send_far, "narrow", lambda n: n ^ 1)
-    got_near = move(send_near, "narrow", lambda n: n ^ 1)
-    far = (keep_far.astype(jnp.float32) + got_far.astype(jnp.float32)).astype(jnp.bfloat16)
-    got = move(far, "narrow", lambda n: n ^ 2)
-    near = keep_near.astype(jnp.float32) + got_near.astype(jnp.float32)
-    return (near + got.astype(jnp.float32)).astype(jnp.bfloat16)
+    middle = {-2: move(take(slab, "near", early[-6]), "wide", partner)}
+    middle[8] = move(early[-4], "wide", outward)
+    late = {10: move(middle[-2], "wide", outward)}
+    from_partner = move(end_blocks(weight, middle[-2], early[6]), "wide", partner)
+
+    dense = pieces_blocks(scaled, early, LONG)
+    dense = pieces_blocks(scaled, middle, LONG, dense)
+    chunks = ((0, 1), (2, 5))
+
+    parts = []
+    after = scaled
+    for pieces, chunk, ends in (({}, chunks[0], True), (late, chunks[1], False)):
+        dense, send_far, send_near, keep_far, keep_near = choose_blocks(
+            share, chunk, ends, places, scaled, from_partner, after, pieces, dense
+        )
+        got_far = move(send_far, "narrow", lambda n: n ^ 1)
+        got_near = move(send_near, "narrow", lambda n: n ^ 1)
+        parts.append((keep_near, got_near, move(add(keep_far, got_far), "narrow", lambda n: n ^ 2)))
+        after = got_far
+    return finish(chunks, total(*parts[0]), *parts[1])
 
 
 def solution(mesh):

time: 53.3 us -> 52.3 us (0.981)
  waiting for transfers between devices: 30.8 us -> 25 us
  Pallas kernels: 3.31 us -> 5.33 us
  starting transfers between devices: 15.1 us -> 16.5 us
  local copies, waits for them, and re-layouts: 1.17 us -> 2.27 us
    ppermute x11 -> x14, waiting for transfers between devices: 30.8 us -> 25 us  [move(): lax.ppermute(value, axis, [(s, target(s) % count) for s in range(count)])]
    pallas_call x2 -> x8, Pallas kernels: 2.92 us -> 4.95 us  [the longest x2 2.04 us: pieces_blocks(): pl.pallas_call(functools.partial(pieces_kernel, list(pieces)), out_shape=...]
    ppermute x11 -> x14, starting transfers between devices: 15.1 us -> 16.5 us  [move(): lax.ppermute(value, axis, [(s, target(s) % count) for s in range(count)])]
    convert_element_type x3 -> x0, other arithmetic: 1.27 us -> none  [the longest x1 1.09 us: per_device(): return (near + got.astype(jnp.float32)).astype(jnp.bfloat16)]
    unnamed x10 -> x6, local copies, waits for them, and re-layouts: 1.16 us -> 2.27 us
    reduce_sum x1, other arithmetic: 1.22 us -> 1.94 us  [per_device(): jnp.sum(jnp.where(picks, occupation[None, :], jnp.float32(0.0)), axis=1)]
    select_n x0 -> x1, other arithmetic: none -> 0.7 us  [per_device(): places = jnp.mod(pattern - (lax.axis_index('wide') * CL - REACH), clusters)]
  transfers between devices with their start and end apart: 11 -> 14, of which waited for: 8 -> 9; matrix products, arithmetic and copies ran while one was open for 3% -> 5% of each run, Pallas kernels for 4% -> 6%
where the time goes in v2:
time: 52.3 us; the launch traced here: 52 us
  waiting for transfers between devices  25 us (48%)
  starting transfers between devices  16.5 us (32%)
  Pallas kernels  5.33 us (10%)
  other arithmetic  2.78 us (5%)
  local copies, waits for them, and re-layouts  2.27 us (4%)
    ppermute x14, waiting for transfers between devices, move(): lax.ppermute(value, axis, [(s, target(s) % count) for s in range(count)])  25 us
    ppermute x14, starting transfers between devices, move(): lax.ppermute(value, axis, [(s, target(s) % count) for s in range(count)])  16.5 us
    unnamed x6, local copies, waits for them, and re-layouts  2.27 us
    pallas_call x2, Pallas kernels, pieces_blocks(): pl.pallas_call(functools.partial(pieces_kernel, list(pieces)), out_shape=...  2.04 us
    reduce_sum x1, other arithmetic, per_device(): jnp.sum(jnp.where(picks, occupation[None, :], jnp.float32(0.0)), axis=1)  1.94 us
    pallas_call x2, Pallas kernels, choose_blocks(): pl.pallas_call(functools.partial(choose_kernel, share, list(pieces), chun...  1.72 us
  transfers between devices with their start and end apart: 14, of which 9 were waited for; matrix products, arithmetic and copies ran while one was open for 5% of the time, Pallas kernels for 6%

profile of v2, /device:TPU:0, one launch (start us, length us, event | category | flops | bytes accessed | tf_op | source)
XLA Modules:
  0.0 52.0 jit_solution(13743221790762375791)
XLA Ops:
  0.0 0.0 copy-start
  0.0 1.1 %copy-done = bf16[768,512]{1,0:T(8,128)(2,1)S(1)} copy-done((bf16[768,512]{1,0:T(8,128)(2,1)S(1)}, bf16[768,512]{1,0:T(8,128)(2,1)}, u32[]{:S(2)}) %copy-start) | copy-done | bytes 786456
  1.1 0.0 copy-start.2
  1.2 3.0 %collective-permute-start = (bf16[256,512]{1,0:T(8,128)(2,1)S(1)}, bf16[256,512]{1,0:T(8,128)(2,1)S(1)}, u32[]{:S(2)}, u32[]{:S(2)}) collective-permute-start(bf16[256,512]{1,0:T(8,128)(2,1)S(1)} %take_end.1.after), channel_id=1, source_target_pairs={{0,4},{4,0},{8,12},{12,8},{16,20},{20,16},{24,28},{28,24},{1,5},{5... | collective-permute-start | bytes 786440 | tf_op jit(solution)/shard_map/ppermute | solution.py:23
  4.2 1.6 %collective-permute-start.6 = (bf16[256,512]{1,0:T(8,128)(2,1)S(1)}, bf16[256,512]{1,0:T(8,128)(2,1)S(1)}, u32[]{:S(2)}, u32[]{:S(2)}) collective-permute-start(bf16[256,512]{1,0:T(8,128)(2,1)S(1)} %take_near.3.after), channel_id=1, source_target_pairs={{0,8},{4,28},{8,16},{12,4},{16,24},{20,12},{24,0},{28,20},{1,9},{5... | collective-permute-start | bytes 786440 | tf_op jit(solution)/shard_map/ppermute | solution.py:23
  5.9 2.6 %collective-permute-start.4 = (bf16[256,512]{1,0:T(8,128)(2,1)S(1)}, bf16[256,512]{1,0:T(8,128)(2,1)S(1)}, u32[]{:S(2)}, u32[]{:S(2)}) collective-permute-start(bf16[256,512]{1,0:T(8,128)(2,1)S(1)} %take_middle.1), channel_id=1, source_target_pairs={{0,4},{4,0},{8,12},{12,8},{16,20},{20,16},{24,28},{28,24},{1,5},{5... | collective-permute-start | bytes 786440 | tf_op jit(solution)/shard_map/ppermute | solution.py:23
  8.5 1.9 %select_reduce_fusion = f32[512]{0:T(512)S(1)} fusion(f32[4096]{0:T(1024)} %param.5, s32[512]{0:T(512)} %param.6), kind=kLoop, calls=%fused_computation | loop fusion | flops 6290944 | bytes 20480 | tf_op jit(solution)/shard_map/reduce_sum | solution.py:212
  10.5 0.7 %add_select_fusion.places = s32[6,12]{1,0:T(8,128)S(1)} fusion(s32[6,12]{1,0:T(8,128)} %param.7, s32[]{:T(128)S(6)} %sub.9), kind=kLoop, calls=%fused_computation.3 | loop fusion | flops 504 | bytes 580 | tf_op jit(solution)/shard_map/jit(remainder)/select_n | solution.py:210
  11.2 0.2 collective-permute-done.after.refs_1_
  11.3 0.0 copy-start.1
  11.3 1.1 %copy-done.1 = bf16[768,512]{1,0:T(8,128)(2,1)S(1)} copy-done((bf16[768,512]{1,0:T(8,128)(2,1)S(1)}, bf16[768,512]{1,0:T(8,128)(2,1)}, u32[]{:S(2)}) %copy-start.1) | copy-done | bytes 786456
  12.5 2.1 %collective-permute-start.1 = (bf16[256,512]{1,0:T(8,128)(2,1)S(1)}, bf16[256,512]{1,0:T(8,128)(2,1)S(1)}, u32[]{:S(2)}, u32[]{:S(2)}) collective-permute-start(bf16[256,512]{1,0:T(8,128)(2,1)S(1)} %take_near.2), channel_id=1, source_target_pairs={{0,4},{4,0},{8,12},{12,8},{16,20},{20,16},{24,28},{28,24},{1,5},{5... | collective-permute-start | bytes 786440 | tf_op jit(solution)/shard_map/ppermute | solution.py:23
  14.6 1.6 %collective-permute-start.2 = (bf16[256,512]{1,0:T(8,128)(2,1)S(1)}, bf16[256,512]{1,0:T(8,128)(2,1)S(1)}, u32[]{:S(2)}, u32[]{:S(2)}) collective-permute-start(bf16[256,512]{1,0:T(8,128)(2,1)S(1)} %collective-permute-done.after.refs_1_), channel_id=1, source_target_pairs={{0,8},{4,28},{8,16},{12,4},{16,24},{20,12},{24,0},{28,20},{1,9},{5... | collective-permute-start | bytes 786440 | tf_op jit(solution)/shard_map/ppermute | solution.py:23
  16.2 0.1 multiply_convert_fusion.left.after
  16.4 0.6 %collective-permute-done.4.refs_3_ = bf16[256,512]{1,0:T(8,128)(2,1)S(1)} collective-permute-done((bf16[256,512]{1,0:T(8,128)(2,1)S(1)}, bf16[256,512]{1,0:T(8,128)(2,1)S(1)}, u32[]{:S(2)}, u32[]{:S(2)}) %collective-permute-start.4) | collective-permute-done | bytes 262176 | tf_op jit(solution)/shard_map/ppermute | solution.py:23
  17.0 2.1 %collective-permute-start.5 = (bf16[256,512]{1,0:T(8,128)(2,1)S(1)}, bf16[256,512]{1,0:T(8,128)(2,1)S(1)}, u32[]{:S(2)}, u32[]{:S(2)}) collective-permute-start(bf16[256,512]{1,0:T(8,128)(2,1)S(1)} %collective-permute-done.4.refs_3_), channel_id=1, source_target_pairs={{0,8},{4,28},{8,16},{12,4},{16,24},{20,12},{24,0},{28,20},{1,9},{5... | collective-permute-start | bytes 786440 | tf_op jit(solution)/shard_map/ppermute | solution.py:23
  19.1 2.7 %collective-permute-done.1.near.refs_0_ = bf16[256,512]{1,0:T(8,128)(2,1)S(1)} collective-permute-done((bf16[256,512]{1,0:T(8,128)(2,1)S(1)}, bf16[256,512]{1,0:T(8,128)(2,1)S(1)}, u32[]{:S(2)}, u32[]{:S(2)}) %collective-permute-start.1) | collective-permute-done | bytes 262176 | tf_op jit(solution)/shard_map/ppermute | solution.py:23
  21.7 3.7 %collective-permute-done.2.far.refs_4_ = bf16[256,512]{1,0:T(8,128)(2,1)S(1)} collective-permute-done((bf16[256,512]{1,0:T(8,128)(2,1)S(1)}, bf16[256,512]{1,0:T(8,128)(2,1)S(1)}, u32[]{:S(2)}, u32[]{:S(2)}) %collective-permute-start.2) | collective-permute-done | bytes 262176 | tf_op jit(solution)/shard_map/ppermute | solution.py:23
  25.4 0.3 end_blocks.1
  25.7 0.1 collective-permute-start.3
  25.8 0.1 collective-permute-start.10
  25.8 0.0 collective-permute-done.6.refs_2_
  25.9 0.0 copy-done.2
  25.9 1.4 %pieces_blocks.2.refs_2_ = bf16[6,22,128,128]{3,2,1,0:T(8,128)(2,1)S(1)} custom-call(bf16[768,512]{1,0:T(8,128)(2,1)S(1)} %multiply_convert_fusion.left.after, bf16[768,512]{1,0:T(8,128)(2,1)S(1)} %copy-done.2, bf16[256,512]{1,0:T(8,128)(2,1)S(1)} %collective-permute-done.after.refs_1_, bf16[256,512]{1,0:T(8,128)(2,1)S(1)} %collective-permute-done.6.refs_2_, ...), custom_call_target="tpu_custom_call" | custom-call | flops 20000000000 | bytes 1 | tf_op jit(solution)/shard_map/pieces_blocks/pallas_call | solution.py:62
  27.3 2.1 %collective-permute-done.5.refs_1_ = bf16[256,512]{1,0:T(8,128)(2,1)S(1)} collective-permute-done((bf16[256,512]{1,0:T(8,128)(2,1)S(1)}, bf16[256,512]{1,0:T(8,128)(2,1)S(1)}, u32[]{:S(2)}, u32[]{:S(2)}) %collective-permute-start.5) | collective-permute-done | bytes 262176 | tf_op jit(solution)/shard_map/ppermute | solution.py:23
  29.4 0.6 %pieces_blocks.3.refs_0_ = bf16[6,22,128,128]{3,2,1,0:T(8,128)(2,1)S(1)} custom-call(bf16[768,512]{1,0:T(8,128)(2,1)S(1)} %multiply_convert_fusion.left.after, bf16[256,512]{1,0:T(8,128)(2,1)S(1)} %collective-permute-done.1.near.refs_0_, bf16[256,512]{1,0:T(8,128)(2,1)S(1)} %collective-permute-done.5.refs_1_, ...), custom_call_target="tpu_custom_call", output_to_operand_aliasing={{}: (3, {})} | custom-call | flops 20000000000 | bytes 1 | tf_op jit(solution)/shard_map/pieces_blocks/pallas_call | solution.py:62
  30.0 0.3 collective-permute-done.3.from_partner
  30.4 0.7 %choose_blocks.2 = (bf16[6,22,128,128]{3,2,1,0:T(8,128)(2,1)S(1)}, bf16[2,3,128,128]{3,2,1,0:T(8,128)(2,1)S(1)}, bf16[2,3,128,128]{3,2,1,0:T(8,128)(2,1)S(1)}, b...) custom-call(s32[6,12]{1,0:T(8,128)S(1)} %add_select_fusion.places, ...), custom_call_target="tpu_custom_call", output_to_operand_aliasing={{0}: (4, {})} | custom-call | flops 1 | bytes 1 | tf_op jit(solution)/shard_map/choose_blocks/pallas_call | solution.py:116
  31.1 0.1 collective-permute-start.8
  31.2 2.8 %collective-permute-done.10.refs_0_ = bf16[256,512]{1,0:T(8,128)(2,1)S(1)} collective-permute-done((bf16[256,512]{1,0:T(8,128)(2,1)S(1)}, bf16[256,512]{1,0:T(8,128)(2,1)S(1)}, u32[]{:S(2)}, u32[]{:S(2)}) %collective-permute-start.10) | collective-permute-done | bytes 262176 | tf_op jit(solution)/shard_map/ppermute | solution.py:23
  34.0 0.0 collective-permute-done.8.y.after
  34.0 1.0 %choose_blocks.3 = (bf16[6,22,128,128]{3,2,1,0:T(8,128)(2,1)S(1)}, bf16[4,3,128,128]{3,2,1,0:T(8,128)(2,1)S(1)}, bf16[4,3,128,128]{3,2,1,0:T(8,128)(2,1)S(1)}, b...) custom-call(s32[6,12]{1,0:T(8,128)S(1)} %add_select_fusion.places, ...), custom_call_target="tpu_custom_call", output_to_operand_aliasing={{0}: (5, {})} | custom-call | flops 1 | bytes 1 | tf_op jit(solution)/shard_map/choose_blocks/pallas_call | solution.py:116
  35.0 0.1 collective-permute-start.12
  35.1 0.5 collective-permute-start.7
  35.7 1.5 %collective-permute-start.9 = (bf16[2,3,128,128]{3,2,1,0:T(8,128)(2,1)S(1)}, bf16[2,3,128,128]{3,2,1,0:T(8,128)(2,1)S(1)}, u32[]{:S(2)}, u32[]{:S(2)}) collective-permute-start(bf16[2,3,128,128]{3,2,1,0:T(8,128)(2,1)S(1)} %add.11), channel_id=1, source_target_pairs={{0,2},{1,3},{2,0},{3,1},{4,6},{5,7},{6,4},{7,5},{8,10},{9,11},{10,... | collective-permute-start | bytes 589832 | tf_op jit(solution)/shard_map/ppermute | solution.py:23
  37.2 0.0 collective-permute-start.11
  37.2 0.0 collective-permute-done.12.y
  37.2 0.1 add.12
  37.3 1.2 %collective-permute-start.13 = (bf16[4,3,128,128]{3,2,1,0:T(8,128)(2,1)S(1)}, bf16[4,3,128,128]{3,2,1,0:T(8,128)(2,1)S(1)}, u32[]{:S(2)}, u32[]{:S(2)}) collective-permute-start(bf16[4,3,128,128]{3,2,1,0:T(8,128)(2,1)S(1)} %add.12), channel_id=1, source_target_pairs={{0,2},{1,3},{2,0},{3,1},{4,6},{5,7},{6,4},{7,5},{8,10},{9,11},{10,... | collective-permute-start | bytes 1179656 | tf_op jit(solution)/shard_map/ppermute | solution.py:23
  38.4 0.0 collective-permute-done.7.got_near
  38.4 5.0 %collective-permute-done.9.got = bf16[2,3,128,128]{3,2,1,0:T(8,128)(2,1)S(1)} collective-permute-done((bf16[2,3,128,128]{3,2,1,0:T(8,128)(2,1)S(1)}, bf16[2,3,128,128]{3,2,1,0:T(8,128)(2,1)S(1)}, u32[]{:S(2)}, u32[]{:S(2)}) %collective-permute-start.9) | collective-permute-done | bytes 196640 | tf_op jit(solution)/shard_map/ppermute | solution.py:23
  43.5 0.1 total.1.early
  43.6 0.0 collective-permute-done.11.got_near
  43.6 7.5 %collective-permute-done.13.got = bf16[4,3,128,128]{3,2,1,0:T(8,128)(2,1)S(1)} collective-permute-done((bf16[4,3,128,128]{3,2,1,0:T(8,128)(2,1)S(1)}, bf16[4,3,128,128]{3,2,1,0:T(8,128)(2,1)S(1)}, u32[]{:S(2)}, u32[]{:S(2)}) %collective-permute-start.13) | collective-permute-done | bytes 393248 | tf_op jit(solution)/shard_map/ppermute | solution.py:23
  51.0 1.0 %finish.1 = bf16[6,3,128,128]{3,2,1,0:T(8,128)(2,1)} custom-call(bf16[2,3,128,128]{3,2,1,0:T(8,128)(2,1)S(1)} %total.1.early, bf16[4,3,128,128]{3,2,1,0:T(8,128)(2,1)S(1)} %get-tuple-element.19.near, bf16[4,3,128,128]{3,2,1,0:T(8,128)(2,1)S(1)} %collective-permute-done.11.got_near, bf16[4,3,128,128]{3,2,1,0:T(8,128)(2,1)S(1)} %collective-permute-done.13.got), custom_call_target="tpu_custom_call" | custom-call | flops 1 | bytes 1 | tf_op jit(solution)/shard_map/finish/pallas_call | solution.py:171
  (6 shorter events, 0.2 us)
Async XLA Ops:
  0.0 1.1 %copy-start = (bf16[768,512]{1,0:T(8,128)(2,1)S(1)}, bf16[768,512]{1,0:T(8,128)(2,1)}, u32[]{:S(2)}) copy-start(bf16[768,512]{1,0:T(8,128)(2,1)} %refs_0_.1) | copy-start | bytes 2359300
  1.1 24.7 %copy-start.2 = (bf16[768,512]{1,0:T(8,128)(2,1)S(1)}, bf16[768,512]{1,0:T(8,128)(2,1)}, u32[]{:S(2)}) copy-start(bf16[768,512]{1,0:T(8,128)(2,1)} %refs_0_.1) | copy-start | bytes 2359300
  1.2 10.2 %collective-permute-start = (bf16[256,512]{1,0:T(8,128)(2,1)S(1)}, bf16[256,512]{1,0:T(8,128)(2,1)S(1)}, u32[]{:S(2)}, u32[]{:S(2)}) collective-permute-start(bf16[256,512]{1,0:T(8,128)(2,1)S(1)} %take_end.1.after), channel_id=1, source_target_pairs={{0,4},{4,0},{8,12},{12,8},{16,20},{20,16},{24,28},{28,24},{1,5},{5... | collective-permute-start | bytes 786440 | tf_op jit(solution)/shard_map/ppermute | solution.py:23
  4.2 21.6 %collective-permute-start.6 = (bf16[256,512]{1,0:T(8,128)(2,1)S(1)}, bf16[256,512]{1,0:T(8,128)(2,1)S(1)}, u32[]{:S(2)}, u32[]{:S(2)}) collective-permute-start(bf16[256,512]{1,0:T(8,128)(2,1)S(1)} %take_near.3.after), channel_id=1, source_target_pairs={{0,8},{4,28},{8,16},{12,4},{16,24},{20,12},{24,0},{28,20},{1,9},{5... | collective-permute-start | bytes 786440 | tf_op jit(solution)/shard_map/ppermute | solution.py:23
  5.9 11.0 %collective-permute-start.4 = (bf16[256,512]{1,0:T(8,128)(2,1)S(1)}, bf16[256,512]{1,0:T(8,128)(2,1)S(1)}, u32[]{:S(2)}, u32[]{:S(2)}) collective-permute-start(bf16[256,512]{1,0:T(8,128)(2,1)S(1)} %take_middle.1), channel_id=1, source_target_pairs={{0,4},{4,0},{8,12},{12,8},{16,20},{20,16},{24,28},{28,24},{1,5},{5... | collective-permute-start | bytes 786440 | tf_op jit(solution)/shard_map/ppermute | solution.py:23
  11.3 1.1 %copy-start.1 = (bf16[768,512]{1,0:T(8,128)(2,1)S(1)}, bf16[768,512]{1,0:T(8,128)(2,1)}, u32[]{:S(2)}) copy-start(bf16[768,512]{1,0:T(8,128)(2,1)} %refs_0_.1) | copy-start | bytes 2359300
  12.5 9.2 %collective-permute-start.1 = (bf16[256,512]{1,0:T(8,128)(2,1)S(1)}, bf16[256,512]{1,0:T(8,128)(2,1)S(1)}, u32[]{:S(2)}, u32[]{:S(2)}) collective-permute-start(bf16[256,512]{1,0:T(8,128)(2,1)S(1)} %take_near.2), channel_id=1, source_target_pairs={{0,4},{4,0},{8,12},{12,8},{16,20},{20,16},{24,28},{28,24},{1,5},{5... | collective-permute-start | bytes 786440 | tf_op jit(solution)/shard_map/ppermute | solution.py:23
  14.6 10.8 %collective-permute-start.2 = (bf16[256,512]{1,0:T(8,128)(2,1)S(1)}, bf16[256,512]{1,0:T(8,128)(2,1)S(1)}, u32[]{:S(2)}, u32[]{:S(2)}) collective-permute-start(bf16[256,512]{1,0:T(8,128)(2,1)S(1)} %collective-permute-done.after.refs_1_), channel_id=1, source_target_pairs={{0,8},{4,28},{8,16},{12,4},{16,24},{20,12},{24,0},{28,20},{1,9},{5... | collective-permute-start | bytes 786440 | tf_op jit(solution)/shard_map/ppermute | solution.py:23
  17.0 12.5 %collective-permute-start.5 = (bf16[256,512]{1,0:T(8,128)(2,1)S(1)}, bf16[256,512]{1,0:T(8,128)(2,1)S(1)}, u32[]{:S(2)}, u32[]{:S(2)}) collective-permute-start(bf16[256,512]{1,0:T(8,128)(2,1)S(1)} %collective-permute-done.4.refs_3_), channel_id=1, source_target_pairs={{0,8},{4,28},{8,16},{12,4},{16,24},{20,12},{24,0},{28,20},{1,9},{5... | collective-permute-start | bytes 786440 | tf_op jit(solution)/shard_map/ppermute | solution.py:23
  25.7 4.7 %collective-permute-start.3 = (bf16[3,128,128]{2,1,0:T(8,128)(2,1)S(1)}, bf16[3,128,128]{2,1,0:T(8,128)(2,1)S(1)}, u32[]{:S(2)}, u32[]{:S(2)}) collective-permute-start(bf16[3,128,128]{2,1,0:T(8,128)(2,1)S(1)} %end_blocks.1), channel_id=1, source_target_pairs={{0,4},{4,0},{8,12},{12,8},{16,20},{20,16},{24,28},{28,24},{1,5},{5... | collective-permute-start | bytes 294920 | tf_op jit(solution)/shard_map/ppermute | solution.py:23
  25.8 8.2 %collective-permute-start.10 = (bf16[256,512]{1,0:T(8,128)(2,1)S(1)}, bf16[256,512]{1,0:T(8,128)(2,1)S(1)}, u32[]{:S(2)}, u32[]{:S(2)}) collective-permute-start(bf16[256,512]{1,0:T(8,128)(2,1)S(1)} %collective-permute-done.1.near.refs_0_), channel_id=1, source_target_pairs={{0,8},{4,28},{8,16},{12,4},{16,24},{20,12},{24,0},{28,20},{1,9},{5... | collective-permute-start | bytes 786440 | tf_op jit(solution)/shard_map/ppermute | solution.py:23
  31.1 2.9 %collective-permute-start.8 = (bf16[2,3,128,128]{3,2,1,0:T(8,128)(2,1)S(1)}, bf16[2,3,128,128]{3,2,1,0:T(8,128)(2,1)S(1)}, u32[]{:S(2)}, u32[]{:S(2)}) collective-permute-start(bf16[2,3,128,128]{3,2,1,0:T(8,128)(2,1)S(1)} %get-tuple-element.17), channel_id=1, source_target_pairs={{0,1},{1,0},{2,3},{3,2},{4,5},{5,4},{6,7},{7,6},{8,9},{9,8},{10,11... | collective-permute-start | bytes 589832 | tf_op jit(solution)/shard_map/ppermute | solution.py:23
  35.0 2.1 %collective-permute-start.12 = (bf16[4,3,128,128]{3,2,1,0:T(8,128)(2,1)S(1)}, bf16[4,3,128,128]{3,2,1,0:T(8,128)(2,1)S(1)}, u32[]{:S(2)}, u32[]{:S(2)}) collective-permute-start(bf16[4,3,128,128]{3,2,1,0:T(8,128)(2,1)S(1)} %get-tuple-element.22), channel_id=1, source_target_pairs={{0,1},{1,0},{2,3},{3,2},{4,5},{5,4},{6,7},{7,6},{8,9},{9,8},{10,11... | collective-permute-start | bytes 1179656 | tf_op jit(solution)/shard_map/ppermute | solution.py:23
  35.1 3.3 %collective-permute-start.7 = (bf16[2,3,128,128]{3,2,1,0:T(8,128)(2,1)S(1)}, bf16[2,3,128,128]{3,2,1,0:T(8,128)(2,1)S(1)}, u32[]{:S(2)}, u32[]{:S(2)}) collective-permute-start(bf16[2,3,128,128]{3,2,1,0:T(8,128)(2,1)S(1)} %get-tuple-element.15), channel_id=1, source_target_pairs={{0,1},{1,0},{2,3},{3,2},{4,5},{5,4},{6,7},{7,6},{8,9},{9,8},{10,11... | collective-permute-start | bytes 589832 | tf_op jit(solution)/shard_map/ppermute | solution.py:23
  35.7 7.8 %collective-permute-start.9 = (bf16[2,3,128,128]{3,2,1,0:T(8,128)(2,1)S(1)}, bf16[2,3,128,128]{3,2,1,0:T(8,128)(2,1)S(1)}, u32[]{:S(2)}, u32[]{:S(2)}) collective-permute-start(bf16[2,3,128,128]{3,2,1,0:T(8,128)(2,1)S(1)} %add.11), channel_id=1, source_target_pairs={{0,2},{1,3},{2,0},{3,1},{4,6},{5,7},{6,4},{7,5},{8,10},{9,11},{10,... | collective-permute-start | bytes 589832 | tf_op jit(solution)/shard_map/ppermute | solution.py:23
  37.2 6.4 %collective-permute-start.11 = (bf16[4,3,128,128]{3,2,1,0:T(8,128)(2,1)S(1)}, bf16[4,3,128,128]{3,2,1,0:T(8,128)(2,1)S(1)}, u32[]{:S(2)}, u32[]{:S(2)}) collective-permute-start(bf16[4,3,128,128]{3,2,1,0:T(8,128)(2,1)S(1)} %get-tuple-element.20), channel_id=1, source_target_pairs={{0,1},{1,0},{2,3},{3,2},{4,5},{5,4},{6,7},{7,6},{8,9},{9,8},{10,11... | collective-permute-start | bytes 1179656 | tf_op jit(solution)/shard_map/ppermute | solution.py:23
  37.3 13.8 %collective-permute-start.13 = (bf16[4,3,128,128]{3,2,1,0:T(8,128)(2,1)S(1)}, bf16[4,3,128,128]{3,2,1,0:T(8,128)(2,1)S(1)}, u32[]{:S(2)}, u32[]{:S(2)}) collective-permute-start(bf16[4,3,128,128]{3,2,1,0:T(8,128)(2,1)S(1)} %add.12), channel_id=1, source_target_pairs={{0,2},{1,3},{2,0},{3,1},{4,6},{5,7},{6,4},{7,5},{8,10},{9,11},{10,... | collective-permute-start | bytes 1179656 | tf_op jit(solution)/shard_map/ppermute | solution.py:23

commit v3 on v2

--- a/solution.py
+++ b/solution.py
@@ -213,19 +213,21 @@
     scaled = (slab.astype(jnp.float32) * weight[None, :]).astype(jnp.bfloat16)
 
     early = {0: slab}
+    middle_rows = take(slab, "middle", jnp.zeros((8, 128), jnp.float32))
     end_rows = take(slab, "end", jnp.zeros((8, 128), jnp.float32))
+    later_rows = take(slab, "near", places)
+    near_rows = take(slab, "near", places.astype(jnp.float32))
+    early[-4] = move(middle_rows, "wide", partner)
     early[-6] = move(end_rows, "wide", partner)
-    near_rows = take(slab, "near", end_rows)
-    early[12] = move(near_rows, "wide", outward)
-    early[-4] = move(take(slab, "middle", near_rows), "wide", partner)
+    early[12] = move(later_rows, "wide", outward)
+    near = move(near_rows, "wide", partner)
+    early[8] = move(early[-4], "wide", outward)
     early[6] = move(early[-6], "wide", outward)
-    middle = {-2: move(take(slab, "near", early[-6]), "wide", partner)}
-    middle[8] = move(early[-4], "wide", outward)
-    late = {10: move(middle[-2], "wide", outward)}
-    from_partner = move(end_blocks(weight, middle[-2], early[6]), "wide", partner)
+    early[-2] = near
+    late = {10: move(near, "wide", outward)}
+    from_partner = move(end_blocks(weight, near, early[6]), "wide", partner)
 
     dense = pieces_blocks(scaled, early, LONG)
-    dense = pieces_blocks(scaled, middle, LONG, dense)
     chunks = ((0, 1), (2, 5))
 
     parts = []

time: 52.3 us -> 53.1 us (1.015)
  starting transfers between devices: 16.5 us -> 18.3 us
  waiting for transfers between devices: 25 us -> 24.1 us
    ppermute x14, starting transfers between devices: 16.5 us -> 18.3 us  [move(): lax.ppermute(value, axis, [(s, target(s) % count) for s in range(count)])]
    ppermute x14, waiting for transfers between devices: 25 us -> 24.1 us  [move(): lax.ppermute(value, axis, [(s, target(s) % count) for s in range(count)])]
    convert_element_type x0 -> x1, other arithmetic: none -> 0.7 us  [per_device(): near_rows = take(slab, 'near', places.astype(jnp.float32))]
    select_n x1 -> x0, other arithmetic: 0.7 us -> none  [per_device(): places = jnp.mod(pattern - (lax.axis_index('wide') * CL - REACH), clusters)]
    pallas_call x2 -> x1, Pallas kernels: 2.04 us -> 1.84 us  [pieces_blocks(): pl.pallas_call(functools.partial(pieces_kernel, list(pieces)), out_shape=...]
  transfers between devices with their start and end apart: 14 -> 14, of which waited for: 9 -> 8; matrix products, arithmetic and copies ran while one was open for 5% -> 5% of each run, Pallas kernels for 6% -> 6%
where the time goes in v3:
time: 53.1 us; the launch traced here: 52.8 us
  waiting for transfers between devices  24.1 us (45%)
  starting transfers between devices  18.3 us (34%)
  Pallas kernels  5.15 us (10%)
  other arithmetic  2.78 us (5%)
  local copies, waits for them, and re-layouts  2.27 us (4%)
    ppermute x14, waiting for transfers between devices, move(): lax.ppermute(value, axis, [(s, target(s) % count) for s in range(count)])  24.1 us
    ppermute x14, starting transfers between devices, move(): lax.ppermute(value, axis, [(s, target(s) % count) for s in range(count)])  18.3 us
    unnamed x6, local copies, waits for them, and re-layouts  2.27 us
    reduce_sum x1, other arithmetic, per_device(): jnp.sum(jnp.where(picks, occupation[None, :], jnp.float32(0.0)), axis=1)  1.94 us
    pallas_call x1, Pallas kernels, pieces_blocks(): pl.pallas_call(functools.partial(pieces_kernel, list(pieces)), out_shape=...  1.84 us
    pallas_call x2, Pallas kernels, choose_blocks(): pl.pallas_call(functools.partial(choose_kernel, share, list(pieces), chun...  1.73 us
  transfers between devices with their start and end apart: 14, of which 8 were waited for; matrix products, arithmetic and copies ran while one was open for 5% of the time, Pallas kernels for 6%

profile of v3, /device:TPU:0, one launch (start us, length us, event | category | flops | bytes accessed | tf_op | source)
XLA Modules:
  0.0 52.8 jit_solution(1194415909372593479)
XLA Ops:
  0.0 0.0 copy-start
  0.0 1.1 %copy-done = bf16[768,512]{1,0:T(8,128)(2,1)S(1)} copy-done((bf16[768,512]{1,0:T(8,128)(2,1)S(1)}, bf16[768,512]{1,0:T(8,128)(2,1)}, u32[]{:S(2)}) %copy-start) | copy-done | bytes 786456
  1.1 0.0 copy-start.2
  1.2 3.0 %collective-permute-start.1 = (bf16[256,512]{1,0:T(8,128)(2,1)S(1)}, bf16[256,512]{1,0:T(8,128)(2,1)S(1)}, u32[]{:S(2)}, u32[]{:S(2)}) collective-permute-start(bf16[256,512]{1,0:T(8,128)(2,1)S(1)} %take_end.1), channel_id=1, source_target_pairs={{0,4},{4,0},{8,12},{12,8},{16,20},{20,16},{24,28},{28,24},{1,5},{5... | collective-permute-start | bytes 786440 | tf_op jit(solution)/shard_map/ppermute | solution.py:23
  4.2 0.1 collective-permute-start.4
  4.3 0.7 %fusion = (f32[6,12]{1,0:T(8,128)S(1)}, s32[6,12]{1,0:T(8,128)S(1)}) fusion(s32[6,12]{1,0:T(8,128)} %param.7, s32[]{:T(128)S(6)} %sub.9), kind=kLoop, calls=%fused_computation.5 | loop fusion | flops 576 | bytes 868 | tf_op jit(solution)/shard_map/convert_element_type | solution.py:219
  5.0 0.0 copy-start.1
  5.0 1.1 %copy-done.1 = bf16[768,512]{1,0:T(8,128)(2,1)S(1)} copy-done((bf16[768,512]{1,0:T(8,128)(2,1)S(1)}, bf16[768,512]{1,0:T(8,128)(2,1)}, u32[]{:S(2)}) %copy-start.1) | copy-done | bytes 786456
  6.2 2.1 %collective-permute-start.5 = (bf16[256,512]{1,0:T(8,128)(2,1)S(1)}, bf16[256,512]{1,0:T(8,128)(2,1)S(1)}, u32[]{:S(2)}, u32[]{:S(2)}) collective-permute-start(bf16[256,512]{1,0:T(8,128)(2,1)S(1)} %take_near.3), channel_id=1, source_target_pairs={{0,8},{4,28},{8,16},{12,4},{16,24},{20,12},{24,0},{28,20},{1,9},{5... | collective-permute-start | bytes 786440 | tf_op jit(solution)/shard_map/ppermute | solution.py:23
  8.4 3.6 %collective-permute-start = (bf16[256,512]{1,0:T(8,128)(2,1)S(1)}, bf16[256,512]{1,0:T(8,128)(2,1)S(1)}, u32[]{:S(2)}, u32[]{:S(2)}) collective-permute-start(bf16[256,512]{1,0:T(8,128)(2,1)S(1)} %take_near.2), channel_id=1, source_target_pairs={{0,4},{4,0},{8,12},{12,8},{16,20},{20,16},{24,28},{28,24},{1,5},{5... | collective-permute-start | bytes 786440 | tf_op jit(solution)/shard_map/ppermute | solution.py:23
  12.0 1.9 %select_reduce_fusion = f32[512]{0:T(512)S(1)} fusion(f32[4096]{0:T(1024)} %param.5, s32[512]{0:T(512)} %param.6), kind=kLoop, calls=%fused_computation | loop fusion | flops 6290944 | bytes 20480 | tf_op jit(solution)/shard_map/reduce_sum | solution.py:212
  13.9 0.0 collective-permute-done.1.refs_2_
  13.9 0.1 collective-permute-start.2
  14.0 3.0 %collective-permute-done.4.refs_1_ = bf16[256,512]{1,0:T(8,128)(2,1)S(1)} collective-permute-done((bf16[256,512]{1,0:T(8,128)(2,1)S(1)}, bf16[256,512]{1,0:T(8,128)(2,1)S(1)}, u32[]{:S(2)}, u32[]{:S(2)}) %collective-permute-start.4) | collective-permute-done | bytes 262176 | tf_op jit(solution)/shard_map/ppermute | solution.py:23
  17.0 2.1 %collective-permute-start.6 = (bf16[256,512]{1,0:T(8,128)(2,1)S(1)}, bf16[256,512]{1,0:T(8,128)(2,1)S(1)}, u32[]{:S(2)}, u32[]{:S(2)}) collective-permute-start(bf16[256,512]{1,0:T(8,128)(2,1)S(1)} %collective-permute-done.4.refs_1_), channel_id=1, source_target_pairs={{0,8},{4,28},{8,16},{12,4},{16,24},{20,12},{24,0},{28,20},{1,9},{5... | collective-permute-start | bytes 786440 | tf_op jit(solution)/shard_map/ppermute | solution.py:23
  19.1 0.1 multiply_convert_fusion.left.after
  19.2 2.5 %collective-permute-done.near.refs_6_ = bf16[256,512]{1,0:T(8,128)(2,1)S(1)} collective-permute-done((bf16[256,512]{1,0:T(8,128)(2,1)S(1)}, bf16[256,512]{1,0:T(8,128)(2,1)S(1)}, u32[]{:S(2)}, u32[]{:S(2)}) %collective-permute-start) | collective-permute-done | bytes 262176 | tf_op jit(solution)/shard_map/ppermute | solution.py:23
  21.7 1.8 %collective-permute-start.10 = (bf16[256,512]{1,0:T(8,128)(2,1)S(1)}, bf16[256,512]{1,0:T(8,128)(2,1)S(1)}, u32[]{:S(2)}, u32[]{:S(2)}) collective-permute-start(bf16[256,512]{1,0:T(8,128)(2,1)S(1)} %collective-permute-done.near.refs_6_), channel_id=1, source_target_pairs={{0,8},{4,28},{8,16},{12,4},{16,24},{20,12},{24,0},{28,20},{1,9},{5... | collective-permute-start | bytes 786440 | tf_op jit(solution)/shard_map/ppermute | solution.py:23
  23.5 1.5 %collective-permute-done.2.far.refs_5_ = bf16[256,512]{1,0:T(8,128)(2,1)S(1)} collective-permute-done((bf16[256,512]{1,0:T(8,128)(2,1)S(1)}, bf16[256,512]{1,0:T(8,128)(2,1)S(1)}, u32[]{:S(2)}, u32[]{:S(2)}) %collective-permute-start.2) | collective-permute-done | bytes 262176 | tf_op jit(solution)/shard_map/ppermute | solution.py:23
  25.0 0.3 end_blocks.1
  25.3 2.1 %collective-permute-start.3 = (bf16[3,128,128]{2,1,0:T(8,128)(2,1)S(1)}, bf16[3,128,128]{2,1,0:T(8,128)(2,1)S(1)}, u32[]{:S(2)}, u32[]{:S(2)}) collective-permute-start(bf16[3,128,128]{2,1,0:T(8,128)(2,1)S(1)} %end_blocks.1), channel_id=1, source_target_pairs={{0,4},{4,0},{8,12},{12,8},{16,20},{20,16},{24,28},{28,24},{1,5},{5... | collective-permute-start | bytes 294920 | tf_op jit(solution)/shard_map/ppermute | solution.py:23
  27.4 0.0 collective-permute-done.5.refs_3_
  27.4 3.2 %collective-permute-done.6.refs_4_ = bf16[256,512]{1,0:T(8,128)(2,1)S(1)} collective-permute-done((bf16[256,512]{1,0:T(8,128)(2,1)S(1)}, bf16[256,512]{1,0:T(8,128)(2,1)S(1)}, u32[]{:S(2)}, u32[]{:S(2)}) %collective-permute-start.6) | collective-permute-done | bytes 262176 | tf_op jit(solution)/shard_map/ppermute | solution.py:23
  30.6 0.0 copy-done.2
  30.6 1.8 %pieces_blocks.1.refs_0_ = bf16[6,22,128,128]{3,2,1,0:T(8,128)(2,1)S(1)} custom-call(bf16[768,512]{1,0:T(8,128)(2,1)S(1)} %multiply_convert_fusion.left.after, bf16[768,512]{1,0:T(8,128)(2,1)S(1)} %copy-done.2, bf16[256,512]{1,0:T(8,128)(2,1)S(1)} %collective-permute-done.4.refs_1_, bf16[256,512]{1,0:T(8,128)(2,1)S(1)} %collective-permute-done.1.refs_2_, ...), custom_call_target="tpu_custom_call" | custom-call | flops 20000000000 | bytes 1 | tf_op jit(solution)/shard_map/pieces_blocks/pallas_call | solution.py:62
  32.5 0.0 collective-permute-done.3.from_partner
  32.5 0.7 %choose_blocks.2 = (bf16[6,22,128,128]{3,2,1,0:T(8,128)(2,1)S(1)}, bf16[2,3,128,128]{3,2,1,0:T(8,128)(2,1)S(1)}, bf16[2,3,128,128]{3,2,1,0:T(8,128)(2,1)S(1)}, b...) custom-call(s32[6,12]{1,0:T(8,128)S(1)} %get-tuple-element.24.after.places, ...), custom_call_target="tpu_custom_call", output_to_operand_aliasing={{0}: (4, {})} | custom-call | flops 1 | bytes 1 | tf_op jit(solution)/shard_map/choose_blocks/pallas_call | solution.py:116
  33.2 0.1 collective-permute-start.8
  33.3 0.7 %collective-permute-done.10.refs_0_ = bf16[256,512]{1,0:T(8,128)(2,1)S(1)} collective-permute-done((bf16[256,512]{1,0:T(8,128)(2,1)S(1)}, bf16[256,512]{1,0:T(8,128)(2,1)S(1)}, u32[]{:S(2)}, u32[]{:S(2)}) %collective-permute-start.10) | collective-permute-done | bytes 262176 | tf_op jit(solution)/shard_map/ppermute | solution.py:23
  33.9 0.8 %collective-permute-done.8.y.after = bf16[2,3,128,128]{3,2,1,0:T(8,128)(2,1)S(1)} collective-permute-done((bf16[2,3,128,128]{3,2,1,0:T(8,128)(2,1)S(1)}, bf16[2,3,128,128]{3,2,1,0:T(8,128)(2,1)S(1)}, u32[]{:S(2)}, u32[]{:S(2)}) %collective-permute-start.8) | collective-permute-done | bytes 196640 | tf_op jit(solution)/shard_map/ppermute | solution.py:23
  34.7 1.0 %choose_blocks.3 = (bf16[6,22,128,128]{3,2,1,0:T(8,128)(2,1)S(1)}, bf16[4,3,128,128]{3,2,1,0:T(8,128)(2,1)S(1)}, bf16[4,3,128,128]{3,2,1,0:T(8,128)(2,1)S(1)}, b...) custom-call(s32[6,12]{1,0:T(8,128)S(1)} %get-tuple-element.24.after.places, ...), custom_call_target="tpu_custom_call", output_to_operand_aliasing={{0}: (5, {})} | custom-call | flops 1 | bytes 1 | tf_op jit(solution)/shard_map/choose_blocks/pallas_call | solution.py:116
  35.7 0.2 collective-permute-start.12
  35.9 0.4 collective-permute-start.7
  36.4 1.5 %collective-permute-start.9 = (bf16[2,3,128,128]{3,2,1,0:T(8,128)(2,1)S(1)}, bf16[2,3,128,128]{3,2,1,0:T(8,128)(2,1)S(1)}, u32[]{:S(2)}, u32[]{:S(2)}) collective-permute-start(bf16[2,3,128,128]{3,2,1,0:T(8,128)(2,1)S(1)} %add.12), channel_id=1, source_target_pairs={{0,2},{1,3},{2,0},{3,1},{4,6},{5,7},{6,4},{7,5},{8,10},{9,11},{10,... | collective-permute-start | bytes 589832 | tf_op jit(solution)/shard_map/ppermute | solution.py:23
  37.9 0.0 collective-permute-start.11
  37.9 0.0 collective-permute-done.12.y
  37.9 0.1 add.13
  38.0 1.2 %collective-permute-start.13 = (bf16[4,3,128,128]{3,2,1,0:T(8,128)(2,1)S(1)}, bf16[4,3,128,128]{3,2,1,0:T(8,128)(2,1)S(1)}, u32[]{:S(2)}, u32[]{:S(2)}) collective-permute-start(bf16[4,3,128,128]{3,2,1,0:T(8,128)(2,1)S(1)} %add.13), channel_id=1, source_target_pairs={{0,2},{1,3},{2,0},{3,1},{4,6},{5,7},{6,4},{7,5},{8,10},{9,11},{10,... | collective-permute-start | bytes 1179656 | tf_op jit(solution)/shard_map/ppermute | solution.py:23
  39.2 0.0 collective-permute-done.7.got_near
  39.2 5.0 %collective-permute-done.9.got = bf16[2,3,128,128]{3,2,1,0:T(8,128)(2,1)S(1)} collective-permute-done((bf16[2,3,128,128]{3,2,1,0:T(8,128)(2,1)S(1)}, bf16[2,3,128,128]{3,2,1,0:T(8,128)(2,1)S(1)}, u32[]{:S(2)}, u32[]{:S(2)}) %collective-permute-start.9) | collective-permute-done | bytes 196640 | tf_op jit(solution)/shard_map/ppermute | solution.py:23
  44.2 0.1 total.1.early
  44.3 0.0 collective-permute-done.11.got_near
  44.3 7.5 %collective-permute-done.13.got = bf16[4,3,128,128]{3,2,1,0:T(8,128)(2,1)S(1)} collective-permute-done((bf16[4,3,128,128]{3,2,1,0:T(8,128)(2,1)S(1)}, bf16[4,3,128,128]{3,2,1,0:T(8,128)(2,1)S(1)}, u32[]{:S(2)}, u32[]{:S(2)}) %collective-permute-start.13) | collective-permute-done | bytes 393248 | tf_op jit(solution)/shard_map/ppermute | solution.py:23
  51.8 1.0 %finish.1 = bf16[6,3,128,128]{3,2,1,0:T(8,128)(2,1)} custom-call(bf16[2,3,128,128]{3,2,1,0:T(8,128)(2,1)S(1)} %total.1.early, bf16[4,3,128,128]{3,2,1,0:T(8,128)(2,1)S(1)} %get-tuple-element.19.near, bf16[4,3,128,128]{3,2,1,0:T(8,128)(2,1)S(1)} %collective-permute-done.11.got_near, bf16[4,3,128,128]{3,2,1,0:T(8,128)(2,1)S(1)} %collective-permute-done.13.got), custom_call_target="tpu_custom_call" | custom-call | flops 1 | bytes 1 | tf_op jit(solution)/shard_map/finish/pallas_call | solution.py:171
  (6 shorter events, 0.2 us)
Async XLA Ops:
  0.0 1.1 %copy-start = (bf16[768,512]{1,0:T(8,128)(2,1)S(1)}, bf16[768,512]{1,0:T(8,128)(2,1)}, u32[]{:S(2)}) copy-start(bf16[768,512]{1,0:T(8,128)(2,1)} %refs_0_.1) | copy-start | bytes 2359300
  1.1 29.5 %copy-start.2 = (bf16[768,512]{1,0:T(8,128)(2,1)S(1)}, bf16[768,512]{1,0:T(8,128)(2,1)}, u32[]{:S(2)}) copy-start(bf16[768,512]{1,0:T(8,128)(2,1)} %refs_0_.1) | copy-start | bytes 2359300
  1.2 12.7 %collective-permute-start.1 = (bf16[256,512]{1,0:T(8,128)(2,1)S(1)}, bf16[256,512]{1,0:T(8,128)(2,1)S(1)}, u32[]{:S(2)}, u32[]{:S(2)}) collective-permute-start(bf16[256,512]{1,0:T(8,128)(2,1)S(1)} %take_end.1), channel_id=1, source_target_pairs={{0,4},{4,0},{8,12},{12,8},{16,20},{20,16},{24,28},{28,24},{1,5},{5... | collective-permute-start | bytes 786440 | tf_op jit(solution)/shard_map/ppermute | solution.py:23
  4.2 12.7 %collective-permute-start.4 = (bf16[256,512]{1,0:T(8,128)(2,1)S(1)}, bf16[256,512]{1,0:T(8,128)(2,1)S(1)}, u32[]{:S(2)}, u32[]{:S(2)}) collective-permute-start(bf16[256,512]{1,0:T(8,128)(2,1)S(1)} %take_middle.1), channel_id=1, source_target_pairs={{0,4},{4,0},{8,12},{12,8},{16,20},{20,16},{24,28},{28,24},{1,5},{5... | collective-permute-start | bytes 786440 | tf_op jit(solution)/shard_map/ppermute | solution.py:23
  5.0 1.1 %copy-start.1 = (bf16[768,512]{1,0:T(8,128)(2,1)S(1)}, bf16[768,512]{1,0:T(8,128)(2,1)}, u32[]{:S(2)}) copy-start(bf16[768,512]{1,0:T(8,128)(2,1)} %refs_0_.1) | copy-start | bytes 2359300
  6.2 21.2 %collective-permute-start.5 = (bf16[256,512]{1,0:T(8,128)(2,1)S(1)}, bf16[256,512]{1,0:T(8,128)(2,1)S(1)}, u32[]{:S(2)}, u32[]{:S(2)}) collective-permute-start(bf16[256,512]{1,0:T(8,128)(2,1)S(1)} %take_near.3), channel_id=1, source_target_pairs={{0,8},{4,28},{8,16},{12,4},{16,24},{20,12},{24,0},{28,20},{1,9},{5... | collective-permute-start | bytes 786440 | tf_op jit(solution)/shard_map/ppermute | solution.py:23
  8.4 13.4 %collective-permute-start = (bf16[256,512]{1,0:T(8,128)(2,1)S(1)}, bf16[256,512]{1,0:T(8,128)(2,1)S(1)}, u32[]{:S(2)}, u32[]{:S(2)}) collective-permute-start(bf16[256,512]{1,0:T(8,128)(2,1)S(1)} %take_near.2), channel_id=1, source_target_pairs={{0,4},{4,0},{8,12},{12,8},{16,20},{20,16},{24,28},{28,24},{1,5},{5... | collective-permute-start | bytes 786440 | tf_op jit(solution)/shard_map/ppermute | solution.py:23
  13.9 11.1 %collective-permute-start.2 = (bf16[256,512]{1,0:T(8,128)(2,1)S(1)}, bf16[256,512]{1,0:T(8,128)(2,1)S(1)}, u32[]{:S(2)}, u32[]{:S(2)}) collective-permute-start(bf16[256,512]{1,0:T(8,128)(2,1)S(1)} %collective-permute-done.1.refs_2_), channel_id=1, source_target_pairs={{0,8},{4,28},{8,16},{12,4},{16,24},{20,12},{24,0},{28,20},{1,9},{5... | collective-permute-start | bytes 786440 | tf_op jit(solution)/shard_map/ppermute | solution.py:23
  17.0 13.7 %collective-permute-start.6 = (bf16[256,512]{1,0:T(8,128)(2,1)S(1)}, bf16[256,512]{1,0:T(8,128)(2,1)S(1)}, u32[]{:S(2)}, u32[]{:S(2)}) collective-permute-start(bf16[256,512]{1,0:T(8,128)(2,1)S(1)} %collective-permute-done.4.refs_1_), channel_id=1, source_target_pairs={{0,8},{4,28},{8,16},{12,4},{16,24},{20,12},{24,0},{28,20},{1,9},{5... | collective-permute-start | bytes 786440 | tf_op jit(solution)/shard_map/ppermute | solution.py:23
  21.7 12.2 %collective-permute-start.10 = (bf16[256,512]{1,0:T(8,128)(2,1)S(1)}, bf16[256,512]{1,0:T(8,128)(2,1)S(1)}, u32[]{:S(2)}, u32[]{:S(2)}) collective-permute-start(bf16[256,512]{1,0:T(8,128)(2,1)S(1)} %collective-permute-done.near.refs_6_), channel_id=1, source_target_pairs={{0,8},{4,28},{8,16},{12,4},{16,24},{20,12},{24,0},{28,20},{1,9},{5... | collective-permute-start | bytes 786440 | tf_op jit(solution)/shard_map/ppermute | solution.py:23
  25.3 7.2 %collective-permute-start.3 = (bf16[3,128,128]{2,1,0:T(8,128)(2,1)S(1)}, bf16[3,128,128]{2,1,0:T(8,128)(2,1)S(1)}, u32[]{:S(2)}, u32[]{:S(2)}) collective-permute-start(bf16[3,128,128]{2,1,0:T(8,128)(2,1)S(1)} %end_blocks.1), channel_id=1, source_target_pairs={{0,4},{4,0},{8,12},{12,8},{16,20},{20,16},{24,28},{28,24},{1,5},{5... | collective-permute-start | bytes 294920 | tf_op jit(solution)/shard_map/ppermute | solution.py:23
  33.2 1.5 %collective-permute-start.8 = (bf16[2,3,128,128]{3,2,1,0:T(8,128)(2,1)S(1)}, bf16[2,3,128,128]{3,2,1,0:T(8,128)(2,1)S(1)}, u32[]{:S(2)}, u32[]{:S(2)}) collective-permute-start(bf16[2,3,128,128]{3,2,1,0:T(8,128)(2,1)S(1)} %get-tuple-element.17), channel_id=1, source_target_pairs={{0,1},{1,0},{2,3},{3,2},{4,5},{5,4},{6,7},{7,6},{8,9},{9,8},{10,11... | collective-permute-start | bytes 589832 | tf_op jit(solution)/shard_map/ppermute | solution.py:23
  35.7 2.2 %collective-permute-start.12 = (bf16[4,3,128,128]{3,2,1,0:T(8,128)(2,1)S(1)}, bf16[4,3,128,128]{3,2,1,0:T(8,128)(2,1)S(1)}, u32[]{:S(2)}, u32[]{:S(2)}) collective-permute-start(bf16[4,3,128,128]{3,2,1,0:T(8,128)(2,1)S(1)} %get-tuple-element.22), channel_id=1, source_target_pairs={{0,1},{1,0},{2,3},{3,2},{4,5},{5,4},{6,7},{7,6},{8,9},{9,8},{10,11... | collective-permute-start | bytes 1179656 | tf_op jit(solution)/shard_map/ppermute | solution.py:23
  35.9 3.2 %collective-permute-start.7 = (bf16[2,3,128,128]{3,2,1,0:T(8,128)(2,1)S(1)}, bf16[2,3,128,128]{3,2,1,0:T(8,128)(2,1)S(1)}, u32[]{:S(2)}, u32[]{:S(2)}) collective-permute-start(bf16[2,3,128,128]{3,2,1,0:T(8,128)(2,1)S(1)} %get-tuple-element.15), channel_id=1, source_target_pairs={{0,1},{1,0},{2,3},{3,2},{4,5},{5,4},{6,7},{7,6},{8,9},{9,8},{10,11... | collective-permute-start | bytes 589832 | tf_op jit(solution)/shard_map/ppermute | solution.py:23
  36.4 7.8 %collective-permute-start.9 = (bf16[2,3,128,128]{3,2,1,0:T(8,128)(2,1)S(1)}, bf16[2,3,128,128]{3,2,1,0:T(8,128)(2,1)S(1)}, u32[]{:S(2)}, u32[]{:S(2)}) collective-permute-start(bf16[2,3,128,128]{3,2,1,0:T(8,128)(2,1)S(1)} %add.12), channel_id=1, source_target_pairs={{0,2},{1,3},{2,0},{3,1},{4,6},{5,7},{6,4},{7,5},{8,10},{9,11},{10,... | collective-permute-start | bytes 589832 | tf_op jit(solution)/shard_map/ppermute | solution.py:23
  37.9 6.3 %collective-permute-start.11 = (bf16[4,3,128,128]{3,2,1,0:T(8,128)(2,1)S(1)}, bf16[4,3,128,128]{3,2,1,0:T(8,128)(2,1)S(1)}, u32[]{:S(2)}, u32[]{:S(2)}) collective-permute-start(bf16[4,3,128,128]{3,2,1,0:T(8,128)(2,1)S(1)} %get-tuple-element.20), channel_id=1, source_target_pairs={{0,1},{1,0},{2,3},{3,2},{4,5},{5,4},{6,7},{7,6},{8,9},{9,8},{10,11... | collective-permute-start | bytes 1179656 | tf_op jit(solution)/shard_map/ppermute | solution.py:23
  38.0 13.8 %collective-permute-start.13 = (bf16[4,3,128,128]{3,2,1,0:T(8,128)(2,1)S(1)}, bf16[4,3,128,128]{3,2,1,0:T(8,128)(2,1)S(1)}, u32[]{:S(2)}, u32[]{:S(2)}) collective-permute-start(bf16[4,3,128,128]{3,2,1,0:T(8,128)(2,1)S(1)} %add.13), channel_id=1, source_target_pairs={{0,2},{1,3},{2,0},{3,1},{4,6},{5,7},{6,4},{7,5},{8,10},{9,11},{10,... | collective-permute-start | bytes 1179656 | tf_op jit(solution)/shard_map/ppermute | solution.py:23

commit v4 on v3

--- a/solution.py
+++ b/solution.py
@@ -215,8 +215,8 @@
     early = {0: slab}
     middle_rows = take(slab, "middle", jnp.zeros((8, 128), jnp.float32))
     end_rows = take(slab, "end", jnp.zeros((8, 128), jnp.float32))
-    later_rows = take(slab, "near", places)
-    near_rows = take(slab, "near", places.astype(jnp.float32))
+    later_rows = take(slab, "near", jnp.zeros((8, 128), jnp.float32))
+    near_rows = take(slab, "near", later_rows)
     early[-4] = move(middle_rows, "wide", partner)
     early[-6] = move(end_rows, "wide", partner)
     early[12] = move(later_rows, "wide", outward)

time: 53.1 us -> 50.5 us (0.951)
  starting transfers between devices: 18.3 us -> 21.8 us
  waiting for transfers between devices: 24.1 us -> 20.7 us
  other arithmetic: 2.78 us -> 1.37 us
  local copies, waits for them, and re-layouts: 2.27 us -> 1.16 us
    ppermute x14, starting transfers between devices: 18.3 us -> 21.8 us  [move(): lax.ppermute(value, axis, [(s, target(s) % count) for s in range(count)])]
    ppermute x14, waiting for transfers between devices: 24.1 us -> 20.7 us  [move(): lax.ppermute(value, axis, [(s, target(s) % count) for s in range(count)])]
    unnamed x6 -> x10, local copies, waits for them, and re-layouts: 2.27 us -> 1.16 us
    reduce_sum x1, other arithmetic: 1.94 us -> 1.22 us  [per_device(): jnp.sum(jnp.where(picks, occupation[None, :], jnp.float32(0.0)), axis=1)]
    convert_element_type x1 -> x0, other arithmetic: 0.7 us -> none  [per_device(): near_rows = take(slab, 'near', places.astype(jnp.float32))]
  transfers between devices with their start and end apart: 14 -> 14, of which waited for: 8 -> 7; matrix products, arithmetic and copies ran while one was open for 5% -> 3% of each run, Pallas kernels for 6% -> 6%
where the time goes in v4:
time: 50.5 us; the launch traced here: 50.3 us
  starting transfers between devices  21.8 us (43%)
  waiting for transfers between devices  20.7 us (41%)
  Pallas kernels  5.17 us (10%)
  other arithmetic  1.37 us (3%)
  local copies, waits for them, and re-layouts  1.16 us (2%)
    ppermute x14, starting transfers between devices, move(): lax.ppermute(value, axis, [(s, target(s) % count) for s in range(count)])  21.8 us
    ppermute x14, waiting for transfers between devices, move(): lax.ppermute(value, axis, [(s, target(s) % count) for s in range(count)])  20.7 us
    pallas_call x1, Pallas kernels, pieces_blocks(): pl.pallas_call(functools.partial(pieces_kernel, list(pieces)), out_shape=...  1.86 us
    pallas_call x2, Pallas kernels, choose_blocks(): pl.pallas_call(functools.partial(choose_kernel, share, list(pieces), chun...  1.72 us
    reduce_sum x1, other arithmetic, per_device(): jnp.sum(jnp.where(picks, occupation[None, :], jnp.float32(0.0)), axis=1)  1.22 us
    unnamed x10, local copies, waits for them, and re-layouts  1.16 us
  transfers between devices with their start and end apart: 14, of which 7 were waited for; matrix products, arithmetic and copies ran while one was open for 3% of the time, Pallas kernels for 6%

profile of v4, /device:TPU:0, one launch (start us, length us, event | category | flops | bytes accessed | tf_op | source)
XLA Modules:
  0.0 50.3 jit_solution(5961674252126296260)
XLA Ops:
  0.0 0.0 copy-start.2
  0.0 0.0 copy-start
  0.0 1.1 %copy-done = bf16[768,512]{1,0:T(8,128)(2,1)S(1)} copy-done((bf16[768,512]{1,0:T(8,128)(2,1)S(1)}, bf16[768,512]{1,0:T(8,128)(2,1)}, u32[]{:S(2)}) %copy-start) | copy-done | bytes 786456
  1.1 0.0 copy-start.3
  1.2 0.0 copy-start.4
  1.2 0.0 copy-start.1
  1.2 3.0 %collective-permute-start.1 = (bf16[256,512]{1,0:T(8,128)(2,1)S(1)}, bf16[256,512]{1,0:T(8,128)(2,1)S(1)}, u32[]{:S(2)}, u32[]{:S(2)}) collective-permute-start(bf16[256,512]{1,0:T(8,128)(2,1)S(1)} %take_end.1), channel_id=1, source_target_pairs={{0,4},{4,0},{8,12},{12,8},{16,20},{20,16},{24,28},{28,24},{1,5},{5... | collective-permute-start | bytes 786440 | tf_op jit(solution)/shard_map/ppermute | solution.py:23
  4.3 0.1 collective-permute-start.4
  4.4 2.1 %collective-permute-start.5 = (bf16[256,512]{1,0:T(8,128)(2,1)S(1)}, bf16[256,512]{1,0:T(8,128)(2,1)S(1)}, u32[]{:S(2)}, u32[]{:S(2)}) collective-permute-start(bf16[256,512]{1,0:T(8,128)(2,1)S(1)} %take_near.2.after), channel_id=1, source_target_pairs={{0,8},{4,28},{8,16},{12,4},{16,24},{20,12},{24,0},{28,20},{1,9},{5... | collective-permute-start | bytes 786440 | tf_op jit(solution)/shard_map/ppermute | solution.py:23
  6.5 3.6 %collective-permute-start = (bf16[256,512]{1,0:T(8,128)(2,1)S(1)}, bf16[256,512]{1,0:T(8,128)(2,1)S(1)}, u32[]{:S(2)}, u32[]{:S(2)}) collective-permute-start(bf16[256,512]{1,0:T(8,128)(2,1)S(1)} %take_near.3), channel_id=1, source_target_pairs={{0,4},{4,0},{8,12},{12,8},{16,20},{20,16},{24,28},{28,24},{1,5},{5... | collective-permute-start | bytes 786440 | tf_op jit(solution)/shard_map/ppermute | solution.py:23
  10.1 0.0 copy-done.3
  10.1 0.0 copy-done.4
  10.2 1.2 %select_reduce_fusion = f32[512]{0:T(512)S(1)} fusion(f32[4096]{0:T(1024)S(1)} %copy-done.3, s32[512]{0:T(512)S(1)} %copy-done.4), kind=kLoop, calls=%fused_computation | loop fusion | flops 6290944 | bytes 20480 | tf_op jit(solution)/shard_map/reduce_sum | solution.py:212
  11.4 0.0 copy-done.2
  11.4 0.0 collective-permute-done.1.refs_2_
  11.4 2.1 %collective-permute-start.2 = (bf16[256,512]{1,0:T(8,128)(2,1)S(1)}, bf16[256,512]{1,0:T(8,128)(2,1)S(1)}, u32[]{:S(2)}, u32[]{:S(2)}) collective-permute-start(bf16[256,512]{1,0:T(8,128)(2,1)S(1)} %collective-permute-done.1.refs_2_), channel_id=1, source_target_pairs={{0,8},{4,28},{8,16},{12,4},{16,24},{20,12},{24,0},{28,20},{1,9},{5... | collective-permute-start | bytes 786440 | tf_op jit(solution)/shard_map/ppermute | solution.py:23
  13.5 3.5 %collective-permute-done.4.refs_1_ = bf16[256,512]{1,0:T(8,128)(2,1)S(1)} collective-permute-done((bf16[256,512]{1,0:T(8,128)(2,1)S(1)}, bf16[256,512]{1,0:T(8,128)(2,1)S(1)}, u32[]{:S(2)}, u32[]{:S(2)}) %collective-permute-start.4) | collective-permute-done | bytes 262176 | tf_op jit(solution)/shard_map/ppermute | solution.py:23
  17.0 2.1 %collective-permute-start.6 = (bf16[256,512]{1,0:T(8,128)(2,1)S(1)}, bf16[256,512]{1,0:T(8,128)(2,1)S(1)}, u32[]{:S(2)}, u32[]{:S(2)}) collective-permute-start(bf16[256,512]{1,0:T(8,128)(2,1)S(1)} %collective-permute-done.4.refs_1_), channel_id=1, source_target_pairs={{0,8},{4,28},{8,16},{12,4},{16,24},{20,12},{24,0},{28,20},{1,9},{5... | collective-permute-start | bytes 786440 | tf_op jit(solution)/shard_map/ppermute | solution.py:23
  19.1 0.0 copy-done.1
  19.1 0.1 multiply_convert_fusion.left.after
  19.2 2.5 %collective-permute-done.near.refs_6_ = bf16[256,512]{1,0:T(8,128)(2,1)S(1)} collective-permute-done((bf16[256,512]{1,0:T(8,128)(2,1)S(1)}, bf16[256,512]{1,0:T(8,128)(2,1)S(1)}, u32[]{:S(2)}, u32[]{:S(2)}) %collective-permute-start) | collective-permute-done | bytes 262176 | tf_op jit(solution)/shard_map/ppermute | solution.py:23
  21.8 1.8 %collective-permute-start.10 = (bf16[256,512]{1,0:T(8,128)(2,1)S(1)}, bf16[256,512]{1,0:T(8,128)(2,1)S(1)}, u32[]{:S(2)}, u32[]{:S(2)}) collective-permute-start(bf16[256,512]{1,0:T(8,128)(2,1)S(1)} %collective-permute-done.near.refs_6_), channel_id=1, source_target_pairs={{0,8},{4,28},{8,16},{12,4},{16,24},{20,12},{24,0},{28,20},{1,9},{5... | collective-permute-start | bytes 786440 | tf_op jit(solution)/shard_map/ppermute | solution.py:23
  23.6 0.0 collective-permute-done.2.far.refs_5_
  23.6 0.3 end_blocks.1
  23.9 3.6 %collective-permute-start.3 = (bf16[3,128,128]{2,1,0:T(8,128)(2,1)S(1)}, bf16[3,128,128]{2,1,0:T(8,128)(2,1)S(1)}, u32[]{:S(2)}, u32[]{:S(2)}) collective-permute-start(bf16[3,128,128]{2,1,0:T(8,128)(2,1)S(1)} %end_blocks.1), channel_id=1, source_target_pairs={{0,4},{4,0},{8,12},{12,8},{16,20},{20,16},{24,28},{28,24},{1,5},{5... | collective-permute-start | bytes 294920 | tf_op jit(solution)/shard_map/ppermute | solution.py:23
  27.5 0.0 collective-permute-done.5.refs_3_
  27.5 0.0 collective-permute-done.6.refs_4_
  27.5 1.9 %pieces_blocks.1.refs_0_ = bf16[6,22,128,128]{3,2,1,0:T(8,128)(2,1)S(1)} custom-call(bf16[768,512]{1,0:T(8,128)(2,1)S(1)} %multiply_convert_fusion.left.after, bf16[768,512]{1,0:T(8,128)(2,1)S(1)} %copy-done.1, bf16[256,512]{1,0:T(8,128)(2,1)S(1)} %collective-permute-done.4.refs_1_, bf16[256,512]{1,0:T(8,128)(2,1)S(1)} %collective-permute-done.1.refs_2_, ...), custom_call_target="tpu_custom_call" | custom-call | flops 20000000000 | bytes 1 | tf_op jit(solution)/shard_map/pieces_blocks/pallas_call | solution.py:62
  29.3 0.7 %collective-permute-done.3.from_partner = bf16[3,128,128]{2,1,0:T(8,128)(2,1)S(1)} collective-permute-done((bf16[3,128,128]{2,1,0:T(8,128)(2,1)S(1)}, bf16[3,128,128]{2,1,0:T(8,128)(2,1)S(1)}, u32[]{:S(2)}, u32[]{:S(2)}) %collective-permute-start.3) | collective-permute-done | bytes 98336 | tf_op jit(solution)/shard_map/ppermute | solution.py:23
  30.1 0.7 %choose_blocks.2 = (bf16[6,22,128,128]{3,2,1,0:T(8,128)(2,1)S(1)}, bf16[2,3,128,128]{3,2,1,0:T(8,128)(2,1)S(1)}, bf16[2,3,128,128]{3,2,1,0:T(8,128)(2,1)S(1)}, b...) custom-call(s32[6,12]{1,0:T(8,128)S(1)} %add_select_fusion.places, ...), custom_call_target="tpu_custom_call", output_to_operand_aliasing={{0}: (4, {})} | custom-call | flops 1 | bytes 1 | tf_op jit(solution)/shard_map/choose_blocks/pallas_call | solution.py:116
  30.7 0.1 collective-permute-start.8
  30.8 0.6 %collective-permute-done.10.refs_0_ = bf16[256,512]{1,0:T(8,128)(2,1)S(1)} collective-permute-done((bf16[256,512]{1,0:T(8,128)(2,1)S(1)}, bf16[256,512]{1,0:T(8,128)(2,1)S(1)}, u32[]{:S(2)}, u32[]{:S(2)}) %collective-permute-start.10) | collective-permute-done | bytes 262176 | tf_op jit(solution)/shard_map/ppermute | solution.py:23
  31.4 0.8 %collective-permute-done.8.y.after = bf16[2,3,128,128]{3,2,1,0:T(8,128)(2,1)S(1)} collective-permute-done((bf16[2,3,128,128]{3,2,1,0:T(8,128)(2,1)S(1)}, bf16[2,3,128,128]{3,2,1,0:T(8,128)(2,1)S(1)}, u32[]{:S(2)}, u32[]{:S(2)}) %collective-permute-start.8) | collective-permute-done | bytes 196640 | tf_op jit(solution)/shard_map/ppermute | solution.py:23
  32.3 1.0 %choose_blocks.3 = (bf16[6,22,128,128]{3,2,1,0:T(8,128)(2,1)S(1)}, bf16[4,3,128,128]{3,2,1,0:T(8,128)(2,1)S(1)}, bf16[4,3,128,128]{3,2,1,0:T(8,128)(2,1)S(1)}, b...) custom-call(s32[6,12]{1,0:T(8,128)S(1)} %add_select_fusion.places, ...), custom_call_target="tpu_custom_call", output_to_operand_aliasing={{0}: (5, {})} | custom-call | flops 1 | bytes 1 | tf_op jit(solution)/shard_map/choose_blocks/pallas_call | solution.py:116
  33.3 0.2 collective-permute-start.12
  33.5 0.4 collective-permute-start.7
  33.9 1.5 %collective-permute-start.9 = (bf16[2,3,128,128]{3,2,1,0:T(8,128)(2,1)S(1)}, bf16[2,3,128,128]{3,2,1,0:T(8,128)(2,1)S(1)}, u32[]{:S(2)}, u32[]{:S(2)}) collective-permute-start(bf16[2,3,128,128]{3,2,1,0:T(8,128)(2,1)S(1)} %add.11), channel_id=1, source_target_pairs={{0,2},{1,3},{2,0},{3,1},{4,6},{5,7},{6,4},{7,5},{8,10},{9,11},{10,... | collective-permute-start | bytes 589832 | tf_op jit(solution)/shard_map/ppermute | solution.py:23
  35.5 0.0 collective-permute-start.11
  35.5 0.0 collective-permute-done.12.y
  35.5 0.1 add.12
  35.6 1.2 %collective-permute-start.13 = (bf16[4,3,128,128]{3,2,1,0:T(8,128)(2,1)S(1)}, bf16[4,3,128,128]{3,2,1,0:T(8,128)(2,1)S(1)}, u32[]{:S(2)}, u32[]{:S(2)}) collective-permute-start(bf16[4,3,128,128]{3,2,1,0:T(8,128)(2,1)S(1)} %add.12), channel_id=1, source_target_pairs={{0,2},{1,3},{2,0},{3,1},{4,6},{5,7},{6,4},{7,5},{8,10},{9,11},{10,... | collective-permute-start | bytes 1179656 | tf_op jit(solution)/shard_map/ppermute | solution.py:23
  36.7 0.0 collective-permute-done.7.got_near
  36.7 5.0 %collective-permute-done.9.got = bf16[2,3,128,128]{3,2,1,0:T(8,128)(2,1)S(1)} collective-permute-done((bf16[2,3,128,128]{3,2,1,0:T(8,128)(2,1)S(1)}, bf16[2,3,128,128]{3,2,1,0:T(8,128)(2,1)S(1)}, u32[]{:S(2)}, u32[]{:S(2)}) %collective-permute-start.9) | collective-permute-done | bytes 196640 | tf_op jit(solution)/shard_map/ppermute | solution.py:23
  41.7 0.1 total.1.early
  41.8 0.0 collective-permute-done.11.got_near
  41.8 7.5 %collective-permute-done.13.got = bf16[4,3,128,128]{3,2,1,0:T(8,128)(2,1)S(1)} collective-permute-done((bf16[4,3,128,128]{3,2,1,0:T(8,128)(2,1)S(1)}, bf16[4,3,128,128]{3,2,1,0:T(8,128)(2,1)S(1)}, u32[]{:S(2)}, u32[]{:S(2)}) %collective-permute-start.13) | collective-permute-done | bytes 393248 | tf_op jit(solution)/shard_map/ppermute | solution.py:23
  49.4 1.0 %finish.1 = bf16[6,3,128,128]{3,2,1,0:T(8,128)(2,1)} custom-call(bf16[2,3,128,128]{3,2,1,0:T(8,128)(2,1)S(1)} %total.1.early, bf16[4,3,128,128]{3,2,1,0:T(8,128)(2,1)S(1)} %get-tuple-element.19.near, bf16[4,3,128,128]{3,2,1,0:T(8,128)(2,1)S(1)} %collective-permute-done.11.got_near, bf16[4,3,128,128]{3,2,1,0:T(8,128)(2,1)S(1)} %collective-permute-done.13.got), custom_call_target="tpu_custom_call" | custom-call | flops 1 | bytes 1 | tf_op jit(solution)/shard_map/finish/pallas_call | solution.py:171
  (7 shorter events, 0.2 us)
Async XLA Ops:
  0.0 11.4 %copy-start.2 = (s32[6,12]{1,0:T(8,128)S(1)}, s32[6,12]{1,0:T(8,128)}, u32[]{:S(2)}) copy-start(s32[6,12]{1,0:T(8,128)} %param.7) | copy-start | bytes 868
  0.0 1.1 %copy-start = (bf16[768,512]{1,0:T(8,128)(2,1)S(1)}, bf16[768,512]{1,0:T(8,128)(2,1)}, u32[]{:S(2)}) copy-start(bf16[768,512]{1,0:T(8,128)(2,1)} %refs_0_.1) | copy-start | bytes 2359300
  1.1 9.0 %copy-start.3 = (f32[4096]{0:T(1024)S(1)}, f32[4096]{0:T(1024)}, u32[]{:S(2)}) copy-start(f32[4096]{0:T(1024)} %param.5) | copy-start | bytes 49156
  1.2 9.0 %copy-start.4 = (s32[512]{0:T(512)S(1)}, s32[512]{0:T(512)}, u32[]{:S(2)}) copy-start(s32[512]{0:T(512)} %param.6) | copy-start | bytes 6148
  1.2 17.9 %copy-start.1 = (bf16[768,512]{1,0:T(8,128)(2,1)S(1)}, bf16[768,512]{1,0:T(8,128)(2,1)}, u32[]{:S(2)}) copy-start(bf16[768,512]{1,0:T(8,128)(2,1)} %refs_0_.1) | copy-start | bytes 2359300
  1.2 10.2 %collective-permute-start.1 = (bf16[256,512]{1,0:T(8,128)(2,1)S(1)}, bf16[256,512]{1,0:T(8,128)(2,1)S(1)}, u32[]{:S(2)}, u32[]{:S(2)}) collective-permute-start(bf16[256,512]{1,0:T(8,128)(2,1)S(1)} %take_end.1), channel_id=1, source_target_pairs={{0,4},{4,0},{8,12},{12,8},{16,20},{20,16},{24,28},{28,24},{1,5},{5... | collective-permute-start | bytes 786440 | tf_op jit(solution)/shard_map/ppermute | solution.py:23
  4.3 12.7 %collective-permute-start.4 = (bf16[256,512]{1,0:T(8,128)(2,1)S(1)}, bf16[256,512]{1,0:T(8,128)(2,1)S(1)}, u32[]{:S(2)}, u32[]{:S(2)}) collective-permute-start(bf16[256,512]{1,0:T(8,128)(2,1)S(1)} %take_middle.1), channel_id=1, source_target_pairs={{0,4},{4,0},{8,12},{12,8},{16,20},{20,16},{24,28},{28,24},{1,5},{5... | collective-permute-start | bytes 786440 | tf_op jit(solution)/shard_map/ppermute | solution.py:23
  4.4 23.1 %collective-permute-start.5 = (bf16[256,512]{1,0:T(8,128)(2,1)S(1)}, bf16[256,512]{1,0:T(8,128)(2,1)S(1)}, u32[]{:S(2)}, u32[]{:S(2)}) collective-permute-start(bf16[256,512]{1,0:T(8,128)(2,1)S(1)} %take_near.2.after), channel_id=1, source_target_pairs={{0,8},{4,28},{8,16},{12,4},{16,24},{20,12},{24,0},{28,20},{1,9},{5... | collective-permute-start | bytes 786440 | tf_op jit(solution)/shard_map/ppermute | solution.py:23
  6.5 15.2 %collective-permute-start = (bf16[256,512]{1,0:T(8,128)(2,1)S(1)}, bf16[256,512]{1,0:T(8,128)(2,1)S(1)}, u32[]{:S(2)}, u32[]{:S(2)}) collective-permute-start(bf16[256,512]{1,0:T(8,128)(2,1)S(1)} %take_near.3), channel_id=1, source_target_pairs={{0,4},{4,0},{8,12},{12,8},{16,20},{20,16},{24,28},{28,24},{1,5},{5... | collective-permute-start | bytes 786440 | tf_op jit(solution)/shard_map/ppermute | solution.py:23
  11.4 12.2 %collective-permute-start.2 = (bf16[256,512]{1,0:T(8,128)(2,1)S(1)}, bf16[256,512]{1,0:T(8,128)(2,1)S(1)}, u32[]{:S(2)}, u32[]{:S(2)}) collective-permute-start(bf16[256,512]{1,0:T(8,128)(2,1)S(1)} %collective-permute-done.1.refs_2_), channel_id=1, source_target_pairs={{0,8},{4,28},{8,16},{12,4},{16,24},{20,12},{24,0},{28,20},{1,9},{5... | collective-permute-start | bytes 786440 | tf_op jit(solution)/shard_map/ppermute | solution.py:23
  17.0 10.5 %collective-permute-start.6 = (bf16[256,512]{1,0:T(8,128)(2,1)S(1)}, bf16[256,512]{1,0:T(8,128)(2,1)S(1)}, u32[]{:S(2)}, u32[]{:S(2)}) collective-permute-start(bf16[256,512]{1,0:T(8,128)(2,1)S(1)} %collective-permute-done.4.refs_1_), channel_id=1, source_target_pairs={{0,8},{4,28},{8,16},{12,4},{16,24},{20,12},{24,0},{28,20},{1,9},{5... | collective-permute-start | bytes 786440 | tf_op jit(solution)/shard_map/ppermute | solution.py:23
  21.8 9.7 %collective-permute-start.10 = (bf16[256,512]{1,0:T(8,128)(2,1)S(1)}, bf16[256,512]{1,0:T(8,128)(2,1)S(1)}, u32[]{:S(2)}, u32[]{:S(2)}) collective-permute-start(bf16[256,512]{1,0:T(8,128)(2,1)S(1)} %collective-permute-done.near.refs_6_), channel_id=1, source_target_pairs={{0,8},{4,28},{8,16},{12,4},{16,24},{20,12},{24,0},{28,20},{1,9},{5... | collective-permute-start | bytes 786440 | tf_op jit(solution)/shard_map/ppermute | solution.py:23
  23.9 6.2 %collective-permute-start.3 = (bf16[3,128,128]{2,1,0:T(8,128)(2,1)S(1)}, bf16[3,128,128]{2,1,0:T(8,128)(2,1)S(1)}, u32[]{:S(2)}, u32[]{:S(2)}) collective-permute-start(bf16[3,128,128]{2,1,0:T(8,128)(2,1)S(1)} %end_blocks.1), channel_id=1, source_target_pairs={{0,4},{4,0},{8,12},{12,8},{16,20},{20,16},{24,28},{28,24},{1,5},{5... | collective-permute-start | bytes 294920 | tf_op jit(solution)/shard_map/ppermute | solution.py:23
  30.7 1.5 %collective-permute-start.8 = (bf16[2,3,128,128]{3,2,1,0:T(8,128)(2,1)S(1)}, bf16[2,3,128,128]{3,2,1,0:T(8,128)(2,1)S(1)}, u32[]{:S(2)}, u32[]{:S(2)}) collective-permute-start(bf16[2,3,128,128]{3,2,1,0:T(8,128)(2,1)S(1)} %get-tuple-element.17), channel_id=1, source_target_pairs={{0,1},{1,0},{2,3},{3,2},{4,5},{5,4},{6,7},{7,6},{8,9},{9,8},{10,11... | collective-permute-start | bytes 589832 | tf_op jit(solution)/shard_map/ppermute | solution.py:23
  33.3 2.2 %collective-permute-start.12 = (bf16[4,3,128,128]{3,2,1,0:T(8,128)(2,1)S(1)}, bf16[4,3,128,128]{3,2,1,0:T(8,128)(2,1)S(1)}, u32[]{:S(2)}, u32[]{:S(2)}) collective-permute-start(bf16[4,3,128,128]{3,2,1,0:T(8,128)(2,1)S(1)} %get-tuple-element.22), channel_id=1, source_target_pairs={{0,1},{1,0},{2,3},{3,2},{4,5},{5,4},{6,7},{7,6},{8,9},{9,8},{10,11... | collective-permute-start | bytes 1179656 | tf_op jit(solution)/shard_map/ppermute | solution.py:23
  33.5 3.2 %collective-permute-start.7 = (bf16[2,3,128,128]{3,2,1,0:T(8,128)(2,1)S(1)}, bf16[2,3,128,128]{3,2,1,0:T(8,128)(2,1)S(1)}, u32[]{:S(2)}, u32[]{:S(2)}) collective-permute-start(bf16[2,3,128,128]{3,2,1,0:T(8,128)(2,1)S(1)} %get-tuple-element.15), channel_id=1, source_target_pairs={{0,1},{1,0},{2,3},{3,2},{4,5},{5,4},{6,7},{7,6},{8,9},{9,8},{10,11... | collective-permute-start | bytes 589832 | tf_op jit(solution)/shard_map/ppermute | solution.py:23
  33.9 7.8 %collective-permute-start.9 = (bf16[2,3,128,128]{3,2,1,0:T(8,128)(2,1)S(1)}, bf16[2,3,128,128]{3,2,1,0:T(8,128)(2,1)S(1)}, u32[]{:S(2)}, u32[]{:S(2)}) collective-permute-start(bf16[2,3,128,128]{3,2,1,0:T(8,128)(2,1)S(1)} %add.11), channel_id=1, source_target_pairs={{0,2},{1,3},{2,0},{3,1},{4,6},{5,7},{6,4},{7,5},{8,10},{9,11},{10,... | collective-permute-start | bytes 589832 | tf_op jit(solution)/shard_map/ppermute | solution.py:23
  35.5 6.3 %collective-permute-start.11 = (bf16[4,3,128,128]{3,2,1,0:T(8,128)(2,1)S(1)}, bf16[4,3,128,128]{3,2,1,0:T(8,128)(2,1)S(1)}, u32[]{:S(2)}, u32[]{:S(2)}) collective-permute-start(bf16[4,3,128,128]{3,2,1,0:T(8,128)(2,1)S(1)} %get-tuple-element.20), channel_id=1, source_target_pairs={{0,1},{1,0},{2,3},{3,2},{4,5},{5,4},{6,7},{7,6},{8,9},{9,8},{10,11... | collective-permute-start | bytes 1179656 | tf_op jit(solution)/shard_map/ppermute | solution.py:23
  35.6 13.8 %collective-permute-start.13 = (bf16[4,3,128,128]{3,2,1,0:T(8,128)(2,1)S(1)}, bf16[4,3,128,128]{3,2,1,0:T(8,128)(2,1)S(1)}, u32[]{:S(2)}, u32[]{:S(2)}) collective-permute-start(bf16[4,3,128,128]{3,2,1,0:T(8,128)(2,1)S(1)} %add.12), channel_id=1, source_target_pairs={{0,2},{1,3},{2,0},{3,1},{4,6},{5,7},{6,4},{7,5},{8,10},{9,11},{10,... | collective-permute-start | bytes 1179656 | tf_op jit(solution)/shard_map/ppermute | solution.py:23

commit v5 on v4

--- a/solution.py
+++ b/solution.py
@@ -11,6 +11,10 @@
 REACH = 8
 CL = 6
 PAIR = 2
+ENDS = [(0, -7), (0, -8), (1, -7)]
+LATE = [(2, 10), (3, 10), (3, 11), (4, 10), (4, 11), (5, 10), (5, 11)]
+LATE_PLACES = (10, 11)
+MASKS = (3, 1, 2, 0)
 VMEM = pl.BlockSpec(memory_space=pltpu.VMEM)
 SMEM = pl.BlockSpec(memory_space=pltpu.SMEM)
 LIMIT = 40 * 1024 * 1024
@@ -53,22 +57,126 @@
                     dense[start + r, offset + REACH + h] = product[r * B : (r + 1) * B, h * B : (h + 1) * B]
 
 
-def pieces_kernel(marks, left, *refs):
-    add_pieces(marks, refs[: len(marks)], left, refs[-1])
-
-
-def pieces_blocks(left, pieces, cost, dense=None):
-    held = [] if dense is None else [dense]
-    return pl.pallas_call(
-        functools.partial(pieces_kernel, list(pieces)),
-        out_shape=jax.ShapeDtypeStruct((CL, CL + 2 * REACH, B, B), jnp.bfloat16),
-        in_specs=[VMEM] * (1 + len(pieces) + len(held)),
-        out_specs=VMEM,
-        input_output_aliases={1 + len(pieces): 0} if held else {},
-        compiler_params=pltpu.CompilerParams(vmem_limit_bytes=LIMIT),
-        cost_estimate=cost,
-        name="pieces_blocks",
-    )(left, *pieces.values(), *held)
+def choose(share, chunk, places, dense, outs):
+    first, last = chunk
+    start = natural(first, last)
+    me = lax.axis_index("narrow")
+    for out, mask in zip(outs, MASKS):
+        slot0 = (me ^ mask) * share
+        for r in range(last - first + 1):
+            for s in range(share):
+                out[r, s] = dense[start + r, places[start + r, slot0 + s]]
+
+
+def put(spot, row, block, outs):
+    for out, mask in zip(outs, MASKS):
+
+        @pl.when(spot[0] == mask)
+        def _(out=out):
+            out[row, spot[1]] = block()
+
+
+def chosen_shapes(chunk, share):
+    return [jax.ShapeDtypeStruct((chunk[1] - chunk[0] + 1, share, B, B), jnp.bfloat16)] * 4
+
+
+def early_kernel(share, marks, chunk, places, left, *refs):
+    dense, spots = refs[len(marks) : len(marks) + 2]
+    add_pieces(marks, refs[: len(marks)], left, dense)
+    choose(share, chunk, places, dense, refs[len(marks) + 2 :])
+    me = lax.axis_index("narrow")
+    for at, (c, m) in enumerate(ENDS + LATE):
+        row, place = natural(c, c), natural(m, m) + REACH
+        slot = jnp.int32(-1)
+        for s in range(places.shape[1]):
+            slot = jnp.where(places[row, s] == place, s, slot)
+        spots[at, 0] = jnp.where(slot < 0, -1, lax.div(slot, share) ^ me)
+        spots[at, 1] = lax.rem(slot, share)
+
+
+def early_blocks(share, chunk, places, left, pieces):
+    shapes = [
+        jax.ShapeDtypeStruct((CL, CL + 2 * REACH, B, B), jnp.bfloat16),
+        jax.ShapeDtypeStruct((len(ENDS + LATE), 2), jnp.int32),
+    ] + chosen_shapes(chunk, share)
+    return pl.pallas_call(
+        functools.partial(early_kernel, share, list(pieces), chunk),
+        out_shape=shapes,
+        in_specs=[SMEM] + [VMEM] * (1 + len(pieces)),
+        out_specs=[VMEM, SMEM] + [VMEM] * 4,
+        compiler_params=pltpu.CompilerParams(vmem_limit_bytes=LIMIT),
+        cost_estimate=LONG,
+        name="early_blocks",
+    )(places, left, *pieces.values())
+
+
+def ends_put_kernel(chunk, spots, from_partner, *refs):
+    outs = refs[4:]
+    for at, (c, m) in enumerate(ENDS):
+        row = natural(c, c) - natural(*chunk)
+        put([spots[at, k] for k in range(2)], row, lambda at=at: from_partner[at], outs)
+
+
+def ends_put(chunk, spots, from_partner, chosen):
+    return pl.pallas_call(
+        functools.partial(ends_put_kernel, chunk),
+        out_shape=[jax.ShapeDtypeStruct(x.shape, x.dtype) for x in chosen],
+        in_specs=[SMEM] + [VMEM] * 5,
+        out_specs=[VMEM] * 4,
+        input_output_aliases={2 + k: k for k in range(4)},
+        compiler_params=pltpu.CompilerParams(vmem_limit_bytes=LIMIT),
+        cost_estimate=SHORT,
+        name="ends_put",
+    )(spots, from_partner, *chosen)
+
+
+def choose_kernel(share, chunk, places, dense, after, *outs):
+    choose(share, chunk, places, dense, outs)
+
+
+def choose_blocks(share, chunk, places, dense, after):
+    shapes = chosen_shapes(chunk, share)
+    return pl.pallas_call(
+        functools.partial(choose_kernel, share, chunk),
+        out_shape=shapes,
+        in_specs=[SMEM] + [VMEM] * 2,
+        out_specs=[VMEM] * 4,
+        compiler_params=pltpu.CompilerParams(vmem_limit_bytes=LIMIT),
+        cost_estimate=SHORT,
+        name="choose_blocks",
+    )(places, dense, after)
+
+
+def late_kernel(chunk, spots, left, piece, after, *refs):
+    outs, late = refs[4:8], refs[8]
+    first, last = chunk
+    start, rows = natural(first, last), (last - first + 1) * B
+    product = multiply(left[pl.ds(pl.multiple_of(start * B, B), rows), :], piece[...])
+    for r in range(last - first + 1):
+        for h in range(PAIR):
+            late[r, h] = product[r * B : (r + 1) * B, h * B : (h + 1) * B]
+    for at, (c, m) in enumerate(LATE):
+        row, column = natural(c, c) - start, natural(m, m) - natural(*LATE_PLACES)
+        put(
+            [spots[len(ENDS) + at, k] for k in range(2)],
+            row,
+            lambda row=row, column=column: late[row, column],
+            outs,
+        )
+
+
+def late_put(chunk, spots, left, piece, after, chosen):
+    return pl.pallas_call(
+        functools.partial(late_kernel, chunk),
+        out_shape=[jax.ShapeDtypeStruct(x.shape, x.dtype) for x in chosen],
+        in_specs=[SMEM] + [VMEM] * 7,
+        out_specs=[VMEM] * 4,
+        scratch_shapes=[pltpu.VMEM((chunk[1] - chunk[0] + 1, PAIR, B, B), jnp.bfloat16)],
+        input_output_aliases={4 + k: k for k in range(4)},
+        compiler_params=pltpu.CompilerParams(vmem_limit_bytes=LIMIT),
+        cost_estimate=SHORT,
+        name="late_put",
+    )(spots, left, piece, after, *chosen)
 
 
 def ends_kernel(weight, near, far, out):
@@ -93,38 +201,6 @@
     )(weight[None, :], near, far)
 
 
-def choose_kernel(share, marks, chunk, ends, places, left, from_partner, after, *refs):
-    dense = refs[len(marks) + 1]
-    outs = refs[len(marks) + 2 :]
-    add_pieces(marks, refs[: len(marks)], left, dense)
-    if ends:
-        for at, (c, m) in enumerate(((0, -7), (0, -8), (1, -7))):
-            dense[natural(c, c), natural(m, m) + REACH] = from_partner[at]
-    first, last = chunk
-    start = natural(first, last)
-    me = lax.axis_index("narrow")
-    for out, mask in zip(outs, (3, 1, 2, 0)):
-        slot0 = (me ^ mask) * share
-        for c in range(last - first + 1):
-            for s in range(share):
-                out[c, s] = dense[start + c, places[start + c, slot0 + s]]
-
-
-def choose_blocks(share, chunk, ends, places, left, from_partner, after, pieces, dense):
-    shapes = [jax.ShapeDtypeStruct(dense.shape, dense.dtype)]
-    shapes += [jax.ShapeDtypeStruct((chunk[1] - chunk[0] + 1, share, B, B), jnp.bfloat16)] * 4
-    return pl.pallas_call(
-        functools.partial(choose_kernel, share, list(pieces), chunk, ends),
-        out_shape=shapes,
-        in_specs=[SMEM] + [VMEM] * (4 + len(pieces)),
-        out_specs=[VMEM] * len(shapes),
-        input_output_aliases={4 + len(pieces): 0},
-        compiler_params=pltpu.CompilerParams(vmem_limit_bytes=LIMIT),
-        cost_estimate=SHORT,
-        name="choose_blocks",
-    )(places, left, from_partner, after, *pieces.values(), dense)
-
-
 def add_kernel(x, y, out):
     out[...] = (x[...].astype(jnp.float32) + y[...].astype(jnp.float32)).astype(jnp.bfloat16)
 
@@ -158,13 +234,19 @@
     )(near, got_near, got)
 
 
-def finish_kernel(chunks, early, near, got_near, got, out):
+def finish_kernel(chunks, early, near, got_near, got, out, rows, done):
     start, later = [natural(first, last) for first, last in chunks]
+    copies = []
     for r in range(early.shape[0]):
-        out[start + r] = early[r]
+        copies.append(pltpu.make_async_copy(early.at[r], out.at[start + r], done.at[r]))
+        copies[-1].start()
     for r in range(near.shape[0]):
         total = near[r].astype(jnp.float32) + got_near[r].astype(jnp.float32) + got[r].astype(jnp.float32)
-        out[later + r] = total.astype(jnp.bfloat16)
+        rows[r] = total.astype(jnp.bfloat16)
+        copies.append(pltpu.make_async_copy(rows.at[r], out.at[later + r], done.at[early.shape[0] + r]))
+        copies[-1].start()
+    for copy in copies:
+        copy.wait()
 
 
 def finish(chunks, early, near, got_near, got):
@@ -172,7 +254,8 @@
         functools.partial(finish_kernel, chunks),
         out_shape=jax.ShapeDtypeStruct((CL,) + near.shape[1:], near.dtype),
         in_specs=[VMEM] * 4,
-        out_specs=VMEM,
+        out_specs=pl.BlockSpec(memory_space=pl.ANY),
+        scratch_shapes=[pltpu.VMEM(near.shape, near.dtype), pltpu.SemaphoreType.DMA((CL,))],
         compiler_params=pltpu.CompilerParams(vmem_limit_bytes=LIMIT),
         cost_estimate=SHORT,
         name="finish",
@@ -213,34 +296,35 @@
     scaled = (slab.astype(jnp.float32) * weight[None, :]).astype(jnp.bfloat16)
 
     early = {0: slab}
-    middle_rows = take(slab, "middle", jnp.zeros((8, 128), jnp.float32))
     end_rows = take(slab, "end", jnp.zeros((8, 128), jnp.float32))
     later_rows = take(slab, "near", jnp.zeros((8, 128), jnp.float32))
+    middle_rows = take(slab, "middle", jnp.zeros((8, 128), jnp.float32))
     near_rows = take(slab, "near", later_rows)
-    early[-4] = move(middle_rows, "wide", partner)
     early[-6] = move(end_rows, "wide", partner)
     early[12] = move(later_rows, "wide", outward)
+    early[-4] = move(middle_rows, "wide", partner)
     near = move(near_rows, "wide", partner)
+    early[6] = move(early[-6], "wide", outward)
     early[8] = move(early[-4], "wide", outward)
-    early[6] = move(early[-6], "wide", outward)
     early[-2] = near
     late = {10: move(near, "wide", outward)}
     from_partner = move(end_blocks(weight, near, early[6]), "wide", partner)
 
-    dense = pieces_blocks(scaled, early, LONG)
     chunks = ((0, 1), (2, 5))
 
-    parts = []
-    after = scaled
-    for pieces, chunk, ends in (({}, chunks[0], True), (late, chunks[1], False)):
-        dense, send_far, send_near, keep_far, keep_near = choose_blocks(
-            share, chunk, ends, places, scaled, from_partner, after, pieces, dense
-        )
+    def swapped(chosen):
+        send_far, send_near, keep_far, keep_near = chosen
         got_far = move(send_far, "narrow", lambda n: n ^ 1)
         got_near = move(send_near, "narrow", lambda n: n ^ 1)
-        parts.append((keep_near, got_near, move(add(keep_far, got_far), "narrow", lambda n: n ^ 2)))
-        after = got_far
-    return finish(chunks, total(*parts[0]), *parts[1])
+        return got_far, (keep_near, got_near, move(add(keep_far, got_far), "narrow", lambda n: n ^ 2))
+
+    dense, spots, *chosen = early_blocks(share, chunks[0], places, scaled, early)
+    chosen = ends_put(chunks[0], spots, from_partner, chosen)
+    after, first_parts = swapped(chosen)
+    chosen = choose_blocks(share, chunks[1], places, dense, chosen[2])
+    chosen = late_put(chunks[1], spots, scaled, late[LATE_PLACES[0]], after, chosen)
+    _, parts = swapped(chosen)
+    return finish(chunks, total(*first_parts), *parts)
 
 
 def solution(mesh):

time: 50.5 us -> 51.3 us (1.016)
  Pallas kernels: 5.17 us -> 7.47 us
  starting transfers between devices: 21.8 us -> 20.3 us
    pallas_call x3 -> x4, Pallas kernels: 3.59 us -> 5.99 us  [the longest x1 3.34 us: early_blocks(): pl.pallas_call(functools.partial(early_kernel, share, list(pieces), chunk...]
    ppermute x14, starting transfers between devices: 21.8 us -> 20.3 us  [move(): lax.ppermute(value, axis, [(s, target(s) % count) for s in range(count)])]
  transfers between devices with their start and end apart: 14 -> 14, of which waited for: 7 -> 6; matrix products, arithmetic and copies ran while one was open for 3% -> 3% of each run, Pallas kernels for 6% -> 11%
where the time goes in v5:
time: 51.3 us; the launch traced here: 51.2 us
  waiting for transfers between devices  20.7 us (40%)
  starting transfers between devices  20.3 us (40%)
  Pallas kernels  7.47 us (15%)
  other arithmetic  1.37 us (3%)
  local copies, waits for them, and re-layouts  1.16 us (2%)
    ppermute x14, waiting for transfers between devices, move(): lax.ppermute(value, axis, [(s, target(s) % count) for s in range(count)])  20.7 us
    ppermute x14, starting transfers between devices, move(): lax.ppermute(value, axis, [(s, target(s) % count) for s in range(count)])  20.3 us
    pallas_call x1, Pallas kernels, early_blocks(): pl.pallas_call(functools.partial(early_kernel, share, list(pieces), chunk...  3.34 us
    reduce_sum x1, other arithmetic, per_device(): jnp.sum(jnp.where(picks, occupation[None, :], jnp.float32(0.0)), axis=1)  1.22 us
    pallas_call x1, Pallas kernels, late_put(): pl.pallas_call(functools.partial(late_kernel, chunk), out_shape=[jax.Shap...  1.16 us
    unnamed x10, local copies, waits for them, and re-layouts  1.16 us
  transfers between devices with their start and end apart: 14, of which 6 were waited for; matrix products, arithmetic and copies ran while one was open for 3% of the time, Pallas kernels for 11%

profile of v5, /device:TPU:0, one launch (start us, length us, event | category | flops | bytes accessed | tf_op | source)
XLA Modules:
  0.0 51.2 jit_solution(15127206725954651164)
XLA Ops:
  0.0 0.0 copy-start.2
  0.0 0.0 copy-start
  0.0 1.1 %copy-done = bf16[768,512]{1,0:T(8,128)(2,1)S(1)} copy-done((bf16[768,512]{1,0:T(8,128)(2,1)S(1)}, bf16[768,512]{1,0:T(8,128)(2,1)}, u32[]{:S(2)}) %copy-start) | copy-done | bytes 786456
  1.1 0.0 copy-start.3
  1.2 0.0 copy-start.4
  1.2 3.0 %collective-permute-start = (bf16[256,512]{1,0:T(8,128)(2,1)S(1)}, bf16[256,512]{1,0:T(8,128)(2,1)S(1)}, u32[]{:S(2)}, u32[]{:S(2)}) collective-permute-start(bf16[256,512]{1,0:T(8,128)(2,1)S(1)} %take_end.1), channel_id=1, source_target_pairs={{0,4},{4,0},{8,12},{12,8},{16,20},{20,16},{24,28},{28,24},{1,5},{5... | collective-permute-start | bytes 786440 | tf_op jit(solution)/shard_map/ppermute | solution.py:27
  4.3 1.6 %collective-permute-start.1 = (bf16[256,512]{1,0:T(8,128)(2,1)S(1)}, bf16[256,512]{1,0:T(8,128)(2,1)S(1)}, u32[]{:S(2)}, u32[]{:S(2)}) collective-permute-start(bf16[256,512]{1,0:T(8,128)(2,1)S(1)} %take_near.2.after), channel_id=1, source_target_pairs={{0,8},{4,28},{8,16},{12,4},{16,24},{20,12},{24,0},{28,20},{1,9},{5... | collective-permute-start | bytes 786440 | tf_op jit(solution)/shard_map/ppermute | solution.py:27
  5.9 2.6 %collective-permute-start.2 = (bf16[256,512]{1,0:T(8,128)(2,1)S(1)}, bf16[256,512]{1,0:T(8,128)(2,1)S(1)}, u32[]{:S(2)}, u32[]{:S(2)}) collective-permute-start(bf16[256,512]{1,0:T(8,128)(2,1)S(1)} %take_middle.1), channel_id=1, source_target_pairs={{0,4},{4,0},{8,12},{12,8},{16,20},{20,16},{24,28},{28,24},{1,5},{5... | collective-permute-start | bytes 786440 | tf_op jit(solution)/shard_map/ppermute | solution.py:27
  8.6 0.1 collective-permute-start.5
  8.7 0.0 copy-done.3
  8.7 0.0 copy-done.4
  8.7 1.2 %select_reduce_fusion = f32[512]{0:T(512)S(1)} fusion(f32[4096]{0:T(1024)S(1)} %copy-done.3, s32[512]{0:T(512)S(1)} %copy-done.4), kind=kLoop, calls=%fused_computation | loop fusion | flops 6290944 | bytes 20480 | tf_op jit(solution)/shard_map/reduce_sum | solution.py:295
  9.9 0.0 copy-done.2
  9.9 1.4 %collective-permute-done.refs_1_ = bf16[256,512]{1,0:T(8,128)(2,1)S(1)} collective-permute-done((bf16[256,512]{1,0:T(8,128)(2,1)S(1)}, bf16[256,512]{1,0:T(8,128)(2,1)S(1)}, u32[]{:S(2)}, u32[]{:S(2)}) %collective-permute-start) | collective-permute-done | bytes 262176 | tf_op jit(solution)/shard_map/ppermute | solution.py:27
  11.4 2.1 %collective-permute-start.3 = (bf16[256,512]{1,0:T(8,128)(2,1)S(1)}, bf16[256,512]{1,0:T(8,128)(2,1)S(1)}, u32[]{:S(2)}, u32[]{:S(2)}) collective-permute-start(bf16[256,512]{1,0:T(8,128)(2,1)S(1)} %collective-permute-done.refs_1_), channel_id=1, source_target_pairs={{0,8},{4,28},{8,16},{12,4},{16,24},{20,12},{24,0},{28,20},{1,9},{5... | collective-permute-start | bytes 786440 | tf_op jit(solution)/shard_map/ppermute | solution.py:27
  13.5 3.5 %collective-permute-done.2.refs_3_ = bf16[256,512]{1,0:T(8,128)(2,1)S(1)} collective-permute-done((bf16[256,512]{1,0:T(8,128)(2,1)S(1)}, bf16[256,512]{1,0:T(8,128)(2,1)S(1)}, u32[]{:S(2)}, u32[]{:S(2)}) %collective-permute-start.2) | collective-permute-done | bytes 262176 | tf_op jit(solution)/shard_map/ppermute | solution.py:27
  17.0 2.1 %collective-permute-start.4 = (bf16[256,512]{1,0:T(8,128)(2,1)S(1)}, bf16[256,512]{1,0:T(8,128)(2,1)S(1)}, u32[]{:S(2)}, u32[]{:S(2)}) collective-permute-start(bf16[256,512]{1,0:T(8,128)(2,1)S(1)} %collective-permute-done.2.refs_3_), channel_id=1, source_target_pairs={{0,8},{4,28},{8,16},{12,4},{16,24},{20,12},{24,0},{28,20},{1,9},{5... | collective-permute-start | bytes 786440 | tf_op jit(solution)/shard_map/ppermute | solution.py:27
  19.1 0.0 copy-done.1
  19.1 0.1 multiply_convert_fusion.left
  19.2 2.5 %collective-permute-done.5.refs_6_.near = bf16[256,512]{1,0:T(8,128)(2,1)S(1)} collective-permute-done((bf16[256,512]{1,0:T(8,128)(2,1)S(1)}, bf16[256,512]{1,0:T(8,128)(2,1)S(1)}, u32[]{:S(2)}, u32[]{:S(2)}) %collective-permute-start.5) | collective-permute-done | bytes 262176 | tf_op jit(solution)/shard_map/ppermute | solution.py:27
  21.8 1.8 %collective-permute-start.10 = (bf16[256,512]{1,0:T(8,128)(2,1)S(1)}, bf16[256,512]{1,0:T(8,128)(2,1)S(1)}, u32[]{:S(2)}, u32[]{:S(2)}) collective-permute-start(bf16[256,512]{1,0:T(8,128)(2,1)S(1)} %collective-permute-done.5.refs_6_.near), channel_id=1, source_target_pairs={{0,8},{4,28},{8,16},{12,4},{16,24},{20,12},{24,0},{28,20},{1,9},{5... | collective-permute-start | bytes 786440 | tf_op jit(solution)/shard_map/ppermute | solution.py:27
  23.6 0.0 collective-permute-done.3.refs_4_.far
  23.6 0.3 end_blocks.1
  23.8 3.6 %collective-permute-start.6 = (bf16[3,128,128]{2,1,0:T(8,128)(2,1)S(1)}, bf16[3,128,128]{2,1,0:T(8,128)(2,1)S(1)}, u32[]{:S(2)}, u32[]{:S(2)}) collective-permute-start(bf16[3,128,128]{2,1,0:T(8,128)(2,1)S(1)} %end_blocks.1), channel_id=1, source_target_pairs={{0,4},{4,0},{8,12},{12,8},{16,20},{20,16},{24,28},{28,24},{1,5},{5... | collective-permute-start | bytes 294920 | tf_op jit(solution)/shard_map/ppermute | solution.py:27
  27.5 0.0 collective-permute-done.1.refs_2_
  27.5 0.0 collective-permute-done.4.refs_5_
  27.5 3.3 %early_blocks.1 = (bf16[6,22,128,128]{3,2,1,0:T(8,128)(2,1)S(1)}, s32[10,2]{1,0:T(8,128)S(1)}, bf16[2,3,128,128]{3,2,1,0:T(8,128)(2,1)S(1)}, bf16[2,3,128,128]{3...) custom-call(s32[6,12]{1,0:T(8,128)S(1)} %add_select_fusion.places, ...), custom_call_target="tpu_custom_call" | custom-call | flops 20000000000 | bytes 1 | tf_op jit(solution)/shard_map/early_blocks/pallas_call | solution.py:102
  30.8 0.0 collective-permute-done.6.from_partner
  30.8 0.8 %ends_put.1 = (bf16[2,3,128,128]{3,2,1,0:T(8,128)(2,1)S(1)}, bf16[2,3,128,128]{3,2,1,0:T(8,128)(2,1)S(1)}, bf16[2,3,128,128]{3,2,1,0:T(8,128)(2,1)S(1)}, bf16[2,3,128,128]{3,2,1,0:T(8,128)(2,1)S(1)}) custom-call(s32[10,2]{1,0:T(8,128)S(1)} %get-tuple-element.23.spots, ...), custom_call_target="tpu_custom_call", output_to_operand_aliasing={{0}: (2, {}), {1}: (3, {}), {2}: (4, {}), {3}: (5, {})} | custom-call | flops 1 | bytes 1 | tf_op jit(solution)/shard_map/ends_put/pallas_call | solution.py:121
  31.6 0.1 collective-permute-start.8
  31.7 0.7 %choose_blocks.1 = (bf16[4,3,128,128]{3,2,1,0:T(8,128)(2,1)S(1)}, bf16[4,3,128,128]{3,2,1,0:T(8,128)(2,1)S(1)}, bf16[4,3,128,128]{3,2,1,0:T(8,128)(2,1)S(1)}, bf16[4,3,128,128]{3,2,1,0:T(8,128)(2,1)S(1)}) custom-call(s32[6,12]{1,0:T(8,128)S(1)} %add_select_fusion.places, bf16[6,22,128,128]{3,2,1,0:T(8,128)(2,1)S(1)} %get-tuple-element.32.dense, ...), custom_call_target="tpu_custom_call" | custom-call | flops 1 | bytes 1 | tf_op jit(solution)/shard_map/choose_blocks/pallas_call | solution.py:139
  32.4 0.0 collective-permute-done.10.piece
  32.4 0.7 %collective-permute-done.8.y.after = bf16[2,3,128,128]{3,2,1,0:T(8,128)(2,1)S(1)} collective-permute-done((bf16[2,3,128,128]{3,2,1,0:T(8,128)(2,1)S(1)}, bf16[2,3,128,128]{3,2,1,0:T(8,128)(2,1)S(1)}, u32[]{:S(2)}, u32[]{:S(2)}) %collective-permute-start.8) | collective-permute-done | bytes 196640 | tf_op jit(solution)/shard_map/ppermute | solution.py:27
  33.1 1.2 %late_put.1 = (bf16[4,3,128,128]{3,2,1,0:T(8,128)(2,1)S(1)}, bf16[4,3,128,128]{3,2,1,0:T(8,128)(2,1)S(1)}, bf16[4,3,128,128]{3,2,1,0:T(8,128)(2,1)S(1)}, bf16[4,3,128,128]{3,2,1,0:T(8,128)(2,1)S(1)}) custom-call(s32[10,2]{1,0:T(8,128)S(1)} %get-tuple-element.23.spots, ...), custom_call_target="tpu_custom_call", output_to_operand_aliasing={{0}: (4, {}), {1}: (5, {}), {2}: (6, {}), {3}: (7, {})} | custom-call | flops 1 | bytes 1 | tf_op jit(solution)/shard_map/late_put/pallas_call | solution.py:169
  34.3 0.2 collective-permute-start.12
  34.5 0.4 collective-permute-start.7
  34.8 0.1 add.11
  34.9 1.6 %collective-permute-start.9 = (bf16[2,3,128,128]{3,2,1,0:T(8,128)(2,1)S(1)}, bf16[2,3,128,128]{3,2,1,0:T(8,128)(2,1)S(1)}, u32[]{:S(2)}, u32[]{:S(2)}) collective-permute-start(bf16[2,3,128,128]{3,2,1,0:T(8,128)(2,1)S(1)} %add.11), channel_id=1, source_target_pairs={{0,2},{1,3},{2,0},{3,1},{4,6},{5,7},{6,4},{7,5},{8,10},{9,11},{10,... | collective-permute-start | bytes 589832 | tf_op jit(solution)/shard_map/ppermute | solution.py:27
  36.4 0.0 collective-permute-start.11
  36.5 0.0 collective-permute-done.12.y
  36.5 0.1 add.12
  36.5 1.1 %collective-permute-start.13 = (bf16[4,3,128,128]{3,2,1,0:T(8,128)(2,1)S(1)}, bf16[4,3,128,128]{3,2,1,0:T(8,128)(2,1)S(1)}, u32[]{:S(2)}, u32[]{:S(2)}) collective-permute-start(bf16[4,3,128,128]{3,2,1,0:T(8,128)(2,1)S(1)} %add.12), channel_id=1, source_target_pairs={{0,2},{1,3},{2,0},{3,1},{4,6},{5,7},{6,4},{7,5},{8,10},{9,11},{10,... | collective-permute-start | bytes 1179656 | tf_op jit(solution)/shard_map/ppermute | solution.py:27
  37.7 0.0 collective-permute-done.7.got_near
  37.7 5.0 %collective-permute-done.9.got = bf16[2,3,128,128]{3,2,1,0:T(8,128)(2,1)S(1)} collective-permute-done((bf16[2,3,128,128]{3,2,1,0:T(8,128)(2,1)S(1)}, bf16[2,3,128,128]{3,2,1,0:T(8,128)(2,1)S(1)}, u32[]{:S(2)}, u32[]{:S(2)}) %collective-permute-start.9) | collective-permute-done | bytes 196640 | tf_op jit(solution)/shard_map/ppermute | solution.py:27
  42.7 0.1 total.1.early
  42.8 0.0 collective-permute-done.11.got_near
  42.8 7.5 %collective-permute-done.13.got = bf16[4,3,128,128]{3,2,1,0:T(8,128)(2,1)S(1)} collective-permute-done((bf16[4,3,128,128]{3,2,1,0:T(8,128)(2,1)S(1)}, bf16[4,3,128,128]{3,2,1,0:T(8,128)(2,1)S(1)}, u32[]{:S(2)}, u32[]{:S(2)}) %collective-permute-start.13) | collective-permute-done | bytes 393248 | tf_op jit(solution)/shard_map/ppermute | solution.py:27
  50.3 0.9 %finish.1 = bf16[6,3,128,128]{3,2,1,0:T(8,128)(2,1)} custom-call(bf16[2,3,128,128]{3,2,1,0:T(8,128)(2,1)S(1)} %total.1.early, bf16[4,3,128,128]{3,2,1,0:T(8,128)(2,1)S(1)} %get-tuple-element.37.near, bf16[4,3,128,128]{3,2,1,0:T(8,128)(2,1)S(1)} %collective-permute-done.11.got_near, bf16[4,3,128,128]{3,2,1,0:T(8,128)(2,1)S(1)} %collective-permute-done.13.got), custom_call_target="tpu_custom_call" | custom-call | flops 1 | bytes 1 | tf_op jit(solution)/shard_map/finish/pallas_call | solution.py:253
  (7 shorter events, 0.1 us)
Async XLA Ops:
  0.0 9.9 %copy-start.2 = (s32[6,12]{1,0:T(8,128)S(1)}, s32[6,12]{1,0:T(8,128)}, u32[]{:S(2)}) copy-start(s32[6,12]{1,0:T(8,128)} %param.7) | copy-start | bytes 868
  0.0 1.1 %copy-start = (bf16[768,512]{1,0:T(8,128)(2,1)S(1)}, bf16[768,512]{1,0:T(8,128)(2,1)}, u32[]{:S(2)}) copy-start(bf16[768,512]{1,0:T(8,128)(2,1)} %refs_0_.1) | copy-start | bytes 2359300
  1.1 7.5 %copy-start.3 = (f32[4096]{0:T(1024)S(1)}, f32[4096]{0:T(1024)}, u32[]{:S(2)}) copy-start(f32[4096]{0:T(1024)} %param.5) | copy-start | bytes 49156
  1.2 7.5 %copy-start.4 = (s32[512]{0:T(512)S(1)}, s32[512]{0:T(512)}, u32[]{:S(2)}) copy-start(s32[512]{0:T(512)} %param.6) | copy-start | bytes 6148
  1.2 17.9 %copy-start.1 = (bf16[768,512]{1,0:T(8,128)(2,1)S(1)}, bf16[768,512]{1,0:T(8,128)(2,1)}, u32[]{:S(2)}) copy-start(bf16[768,512]{1,0:T(8,128)(2,1)} %refs_0_.1) | copy-start | bytes 2359300
  1.2 10.2 %collective-permute-start = (bf16[256,512]{1,0:T(8,128)(2,1)S(1)}, bf16[256,512]{1,0:T(8,128)(2,1)S(1)}, u32[]{:S(2)}, u32[]{:S(2)}) collective-permute-start(bf16[256,512]{1,0:T(8,128)(2,1)S(1)} %take_end.1), channel_id=1, source_target_pairs={{0,4},{4,0},{8,12},{12,8},{16,20},{20,16},{24,28},{28,24},{1,5},{5... | collective-permute-start | bytes 786440 | tf_op jit(solution)/shard_map/ppermute | solution.py:27
  4.3 23.2 %collective-permute-start.1 = (bf16[256,512]{1,0:T(8,128)(2,1)S(1)}, bf16[256,512]{1,0:T(8,128)(2,1)S(1)}, u32[]{:S(2)}, u32[]{:S(2)}) collective-permute-start(bf16[256,512]{1,0:T(8,128)(2,1)S(1)} %take_near.2.after), channel_id=1, source_target_pairs={{0,8},{4,28},{8,16},{12,4},{16,24},{20,12},{24,0},{28,20},{1,9},{5... | collective-permute-start | bytes 786440 | tf_op jit(solution)/shard_map/ppermute | solution.py:27
  5.9 11.0 %collective-permute-start.2 = (bf16[256,512]{1,0:T(8,128)(2,1)S(1)}, bf16[256,512]{1,0:T(8,128)(2,1)S(1)}, u32[]{:S(2)}, u32[]{:S(2)}) collective-permute-start(bf16[256,512]{1,0:T(8,128)(2,1)S(1)} %take_middle.1), channel_id=1, source_target_pairs={{0,4},{4,0},{8,12},{12,8},{16,20},{20,16},{24,28},{28,24},{1,5},{5... | collective-permute-start | bytes 786440 | tf_op jit(solution)/shard_map/ppermute | solution.py:27
  8.6 13.2 %collective-permute-start.5 = (bf16[256,512]{1,0:T(8,128)(2,1)S(1)}, bf16[256,512]{1,0:T(8,128)(2,1)S(1)}, u32[]{:S(2)}, u32[]{:S(2)}) collective-permute-start(bf16[256,512]{1,0:T(8,128)(2,1)S(1)} %take_near.3), channel_id=1, source_target_pairs={{0,4},{4,0},{8,12},{12,8},{16,20},{20,16},{24,28},{28,24},{1,5},{5... | collective-permute-start | bytes 786440 | tf_op jit(solution)/shard_map/ppermute | solution.py:27
  11.4 12.2 %collective-permute-start.3 = (bf16[256,512]{1,0:T(8,128)(2,1)S(1)}, bf16[256,512]{1,0:T(8,128)(2,1)S(1)}, u32[]{:S(2)}, u32[]{:S(2)}) collective-permute-start(bf16[256,512]{1,0:T(8,128)(2,1)S(1)} %collective-permute-done.refs_1_), channel_id=1, source_target_pairs={{0,8},{4,28},{8,16},{12,4},{16,24},{20,12},{24,0},{28,20},{1,9},{5... | collective-permute-start | bytes 786440 | tf_op jit(solution)/shard_map/ppermute | solution.py:27
  17.0 10.5 %collective-permute-start.4 = (bf16[256,512]{1,0:T(8,128)(2,1)S(1)}, bf16[256,512]{1,0:T(8,128)(2,1)S(1)}, u32[]{:S(2)}, u32[]{:S(2)}) collective-permute-start(bf16[256,512]{1,0:T(8,128)(2,1)S(1)} %collective-permute-done.2.refs_3_), channel_id=1, source_target_pairs={{0,8},{4,28},{8,16},{12,4},{16,24},{20,12},{24,0},{28,20},{1,9},{5... | collective-permute-start | bytes 786440 | tf_op jit(solution)/shard_map/ppermute | solution.py:27
  21.8 10.6 %collective-permute-start.10 = (bf16[256,512]{1,0:T(8,128)(2,1)S(1)}, bf16[256,512]{1,0:T(8,128)(2,1)S(1)}, u32[]{:S(2)}, u32[]{:S(2)}) collective-permute-start(bf16[256,512]{1,0:T(8,128)(2,1)S(1)} %collective-permute-done.5.refs_6_.near), channel_id=1, source_target_pairs={{0,8},{4,28},{8,16},{12,4},{16,24},{20,12},{24,0},{28,20},{1,9},{5... | collective-permute-start | bytes 786440 | tf_op jit(solution)/shard_map/ppermute | solution.py:27
  23.8 7.0 %collective-permute-start.6 = (bf16[3,128,128]{2,1,0:T(8,128)(2,1)S(1)}, bf16[3,128,128]{2,1,0:T(8,128)(2,1)S(1)}, u32[]{:S(2)}, u32[]{:S(2)}) collective-permute-start(bf16[3,128,128]{2,1,0:T(8,128)(2,1)S(1)} %end_blocks.1), channel_id=1, source_target_pairs={{0,4},{4,0},{8,12},{12,8},{16,20},{20,16},{24,28},{28,24},{1,5},{5... | collective-permute-start | bytes 294920 | tf_op jit(solution)/shard_map/ppermute | solution.py:27
  31.6 1.5 %collective-permute-start.8 = (bf16[2,3,128,128]{3,2,1,0:T(8,128)(2,1)S(1)}, bf16[2,3,128,128]{3,2,1,0:T(8,128)(2,1)S(1)}, u32[]{:S(2)}, u32[]{:S(2)}) collective-permute-start(bf16[2,3,128,128]{3,2,1,0:T(8,128)(2,1)S(1)} %get-tuple-element.31), channel_id=1, source_target_pairs={{0,1},{1,0},{2,3},{3,2},{4,5},{5,4},{6,7},{7,6},{8,9},{9,8},{10,11... | collective-permute-start | bytes 589832 | tf_op jit(solution)/shard_map/ppermute | solution.py:27
  34.3 2.2 %collective-permute-start.12 = (bf16[4,3,128,128]{3,2,1,0:T(8,128)(2,1)S(1)}, bf16[4,3,128,128]{3,2,1,0:T(8,128)(2,1)S(1)}, u32[]{:S(2)}, u32[]{:S(2)}) collective-permute-start(bf16[4,3,128,128]{3,2,1,0:T(8,128)(2,1)S(1)} %get-tuple-element.40), channel_id=1, source_target_pairs={{0,1},{1,0},{2,3},{3,2},{4,5},{5,4},{6,7},{7,6},{8,9},{9,8},{10,11... | collective-permute-start | bytes 1179656 | tf_op jit(solution)/shard_map/ppermute | solution.py:27
  34.5 3.2 %collective-permute-start.7 = (bf16[2,3,128,128]{3,2,1,0:T(8,128)(2,1)S(1)}, bf16[2,3,128,128]{3,2,1,0:T(8,128)(2,1)S(1)}, u32[]{:S(2)}, u32[]{:S(2)}) collective-permute-start(bf16[2,3,128,128]{3,2,1,0:T(8,128)(2,1)S(1)} %get-tuple-element.29), channel_id=1, source_target_pairs={{0,1},{1,0},{2,3},{3,2},{4,5},{5,4},{6,7},{7,6},{8,9},{9,8},{10,11... | collective-permute-start | bytes 589832 | tf_op jit(solution)/shard_map/ppermute | solution.py:27
  34.9 7.8 %collective-permute-start.9 = (bf16[2,3,128,128]{3,2,1,0:T(8,128)(2,1)S(1)}, bf16[2,3,128,128]{3,2,1,0:T(8,128)(2,1)S(1)}, u32[]{:S(2)}, u32[]{:S(2)}) collective-permute-start(bf16[2,3,128,128]{3,2,1,0:T(8,128)(2,1)S(1)} %add.11), channel_id=1, source_target_pairs={{0,2},{1,3},{2,0},{3,1},{4,6},{5,7},{6,4},{7,5},{8,10},{9,11},{10,... | collective-permute-start | bytes 589832 | tf_op jit(solution)/shard_map/ppermute | solution.py:27
  36.4 6.3 %collective-permute-start.11 = (bf16[4,3,128,128]{3,2,1,0:T(8,128)(2,1)S(1)}, bf16[4,3,128,128]{3,2,1,0:T(8,128)(2,1)S(1)}, u32[]{:S(2)}, u32[]{:S(2)}) collective-permute-start(bf16[4,3,128,128]{3,2,1,0:T(8,128)(2,1)S(1)} %get-tuple-element.38), channel_id=1, source_target_pairs={{0,1},{1,0},{2,3},{3,2},{4,5},{5,4},{6,7},{7,6},{8,9},{9,8},{10,11... | collective-permute-start | bytes 1179656 | tf_op jit(solution)/shard_map/ppermute | solution.py:27
  36.5 13.8 %collective-permute-start.13 = (bf16[4,3,128,128]{3,2,1,0:T(8,128)(2,1)S(1)}, bf16[4,3,128,128]{3,2,1,0:T(8,128)(2,1)S(1)}, u32[]{:S(2)}, u32[]{:S(2)}) collective-permute-start(bf16[4,3,128,128]{3,2,1,0:T(8,128)(2,1)S(1)} %add.12), channel_id=1, source_target_pairs={{0,2},{1,3},{2,0},{3,1},{4,6},{5,7},{6,4},{7,5},{8,10},{9,11},{10,... | collective-permute-start | bytes 1179656 | tf_op jit(solution)/shard_map/ppermute | solution.py:27

commit v6 on v4

--- a/solution.py
+++ b/solution.py
@@ -14,6 +14,7 @@
 VMEM = pl.BlockSpec(memory_space=pltpu.VMEM)
 SMEM = pl.BlockSpec(memory_space=pltpu.SMEM)
 LIMIT = 40 * 1024 * 1024
+WHOLE = 65280 * 1024
 LONG = pl.CostEstimate(flops=20 * 10**9, bytes_accessed=1, transcendentals=0)
 SHORT = pl.CostEstimate(flops=1, bytes_accessed=1, transcendentals=0)
 
@@ -158,13 +159,19 @@
     )(near, got_near, got)
 
 
-def finish_kernel(chunks, early, near, got_near, got, out):
+def finish_kernel(chunks, early, near, got_near, got, out, rows, done):
     start, later = [natural(first, last) for first, last in chunks]
+    copies = []
     for r in range(early.shape[0]):
-        out[start + r] = early[r]
+        copies.append(pltpu.make_async_copy(early.at[r], out.at[start + r], done.at[r]))
+        copies[-1].start()
     for r in range(near.shape[0]):
         total = near[r].astype(jnp.float32) + got_near[r].astype(jnp.float32) + got[r].astype(jnp.float32)
-        out[later + r] = total.astype(jnp.bfloat16)
+        rows[r] = total.astype(jnp.bfloat16)
+        copies.append(pltpu.make_async_copy(rows.at[r], out.at[later + r], done.at[early.shape[0] + r]))
+        copies[-1].start()
+    for copy in copies:
+        copy.wait()
 
 
 def finish(chunks, early, near, got_near, got):
@@ -172,7 +179,8 @@
         functools.partial(finish_kernel, chunks),
         out_shape=jax.ShapeDtypeStruct((CL,) + near.shape[1:], near.dtype),
         in_specs=[VMEM] * 4,
-        out_specs=VMEM,
+        out_specs=pl.BlockSpec(memory_space=pl.ANY),
+        scratch_shapes=[pltpu.VMEM(near.shape, near.dtype), pltpu.SemaphoreType.DMA((CL,))],
         compiler_params=pltpu.CompilerParams(vmem_limit_bytes=LIMIT),
         cost_estimate=SHORT,
         name="finish",
@@ -187,6 +195,27 @@
     copy.wait()
 
 
+def first_take_kernel(slab, out, done):
+    odd = lax.rem(lax.axis_index("wide"), 2)
+    copy = pltpu.make_async_copy(slab.at[pl.ds(pl.multiple_of(odd * 2 * PAIR * B, PAIR * B), PAIR * B), :], out, done)
+    copy.start()
+    copy.wait()
+
+
+def first_take(slab):
+    hbm = pl.BlockSpec(memory_space=pl.ANY)
+    return pl.pallas_call(
+        first_take_kernel,
+        out_shape=jax.ShapeDtypeStruct((PAIR * B, slab.shape[1]), slab.dtype),
+        in_specs=[hbm],
+        out_specs=hbm,
+        scratch_shapes=[pltpu.SemaphoreType.DMA],
+        compiler_params=pltpu.CompilerParams(vmem_limit_bytes=WHOLE),
+        cost_estimate=SHORT,
+        name="take_end",
+    )(slab)
+
+
 def take(slab, which, after):
     return pl.pallas_call(
         functools.partial(take_kernel, which),
@@ -213,16 +242,16 @@
     scaled = (slab.astype(jnp.float32) * weight[None, :]).astype(jnp.bfloat16)
 
     early = {0: slab}
-    middle_rows = take(slab, "middle", jnp.zeros((8, 128), jnp.float32))
-    end_rows = take(slab, "end", jnp.zeros((8, 128), jnp.float32))
+    end_rows = first_take(slab)
     later_rows = take(slab, "near", jnp.zeros((8, 128), jnp.float32))
-    near_rows = take(slab, "near", later_rows)
-    early[-4] = move(middle_rows, "wide", partner)
+    middle_rows = take(slab, "middle", later_rows)
+    near_rows = take(slab, "near", middle_rows)
     early[-6] = move(end_rows, "wide", partner)
     early[12] = move(later_rows, "wide", outward)
+    early[-4] = move(middle_rows, "wide", partner)
     near = move(near_rows, "wide", partner)
+    early[6] = move(early[-6], "wide", outward)
     early[8] = move(early[-4], "wide", outward)
-    early[6] = move(early[-6], "wide", outward)
     early[-2] = near
     late = {10: move(near, "wide", outward)}
     from_partner = move(end_blocks(weight, near, early[6]), "wide", partner)
@@ -237,8 +266,9 @@
             share, chunk, ends, places, scaled, from_partner, after, pieces, dense
         )
         got_far = move(send_far, "narrow", lambda n: n ^ 1)
+        got = move(add(keep_far, got_far), "narrow", lambda n: n ^ 2)
         got_near = move(send_near, "narrow", lambda n: n ^ 1)
-        parts.append((keep_near, got_near, move(add(keep_far, got_far), "narrow", lambda n: n ^ 2)))
+        parts.append((keep_near, got_near, got))
         after = got_far
     return finish(chunks, total(*parts[0]), *parts[1])
 

time: 50.5 us -> 58.5 us (1.16)
  Pallas kernels: 5.17 us -> 14.1 us
  starting transfers between devices: 21.8 us -> 20.4 us
  other arithmetic: 1.37 us -> 2.51 us
  waiting for transfers between devices: 20.7 us -> 20.1 us
    pallas_call x0 -> x1, Pallas kernels: none -> 9.05 us  [first_take(): pl.pallas_call(first_take_kernel, out_shape=jax.ShapeDtypeStruct((PAIR *...]
    ppermute x14, starting transfers between devices: 21.8 us -> 20.4 us  [move(): lax.ppermute(value, axis, [(s, target(s) % count) for s in range(count)])]
    convert_element_type x1, other arithmetic: 0.14 us -> 1.27 us  [per_device(): scaled = (slab.astype(jnp.float32) * weight[None, :]).astype(jnp.bfloat16)]
    ppermute x14, waiting for transfers between devices: 20.7 us -> 20.1 us  [move(): lax.ppermute(value, axis, [(s, target(s) % count) for s in range(count)])]
  transfers between devices with their start and end apart: 14 -> 14, of which waited for: 7 -> 8; matrix products, arithmetic and copies ran while one was open for 3% -> 4% of each run, Pallas kernels for 6% -> 5%
where the time goes in v6:
time: 58.5 us; the launch traced here: 58.3 us
  starting transfers between devices  20.4 us (35%)
  waiting for transfers between devices  20.1 us (34%)
  Pallas kernels  14.1 us (24%)
  other arithmetic  2.51 us (4%)
  local copies, waits for them, and re-layouts  1.15 us (2%)
    ppermute x14, starting transfers between devices, move(): lax.ppermute(value, axis, [(s, target(s) % count) for s in range(count)])  20.4 us
    ppermute x14, waiting for transfers between devices, move(): lax.ppermute(value, axis, [(s, target(s) % count) for s in range(count)])  20.1 us
    pallas_call x1, Pallas kernels, first_take(): pl.pallas_call(first_take_kernel, out_shape=jax.ShapeDtypeStruct((PAIR *...  9.05 us
    pallas_call x1, Pallas kernels, pieces_blocks(): pl.pallas_call(functools.partial(pieces_kernel, list(pieces)), out_shape=...  1.85 us
    pallas_call x2, Pallas kernels, choose_blocks(): pl.pallas_call(functools.partial(choose_kernel, share, list(pieces), chun...  1.72 us
    convert_element_type x1, other arithmetic, per_device(): scaled = (slab.astype(jnp.float32) * weight[None, :]).astype(jnp.bfloat16)  1.27 us
    reduce_sum x1, other arithmetic, per_device(): jnp.sum(jnp.where(picks, occupation[None, :], jnp.float32(0.0)), axis=1)  1.22 us
  transfers between devices with their start and end apart: 14, of which 8 were waited for; matrix products, arithmetic and copies ran while one was open for 4% of the time, Pallas kernels for 5%

profile of v6, /device:TPU:0, one launch (start us, length us, event | category | flops | bytes accessed | tf_op | source)
XLA Modules:
  0.0 58.3 jit_solution(13161993979481794164)
XLA Ops:
  0.0 0.0 copy-start.4
  0.0 0.0 copy-start.3
  0.0 0.0 copy-start.2
  0.0 9.0 %take_end.1 = bf16[256,512]{1,0:T(8,128)(2,1)} custom-call(bf16[768,512]{1,0:T(8,128)(2,1)} %refs_0_.1), custom_call_target="tpu_custom_call" | custom-call | flops 1 | bytes 1 | tf_op jit(solution)/shard_map/take_end/pallas_call | solution.py:207
  9.1 3.1 %collective-permute-start.1 = (bf16[256,512]{1,0:T(8,128)(2,1)}, bf16[256,512]{1,0:T(8,128)(2,1)S(1)}, u32[]{:S(2)}, u32[]{:S(2)}) collective-permute-start(bf16[256,512]{1,0:T(8,128)(2,1)} %take_end.1), channel_id=1, source_target_pairs={{0,4},{4,0},{8,12},{12,8},{16,20},{20,16},{24,28},{28,24},{1,5},{5... | collective-permute-start | bytes 786440 | tf_op jit(solution)/shard_map/ppermute | solution.py:24
  12.1 0.0 copy-start
  12.1 1.1 %copy-done = bf16[768,512]{1,0:T(8,128)(2,1)S(1)} copy-done((bf16[768,512]{1,0:T(8,128)(2,1)S(1)}, bf16[768,512]{1,0:T(8,128)(2,1)}, u32[]{:S(2)}) %copy-start) | copy-done | bytes 786456
  13.2 0.0 copy-start.1
  13.3 1.6 %collective-permute-start.4 = (bf16[256,512]{1,0:T(8,128)(2,1)S(1)}, bf16[256,512]{1,0:T(8,128)(2,1)S(1)}, u32[]{:S(2)}, u32[]{:S(2)}) collective-permute-start(bf16[256,512]{1,0:T(8,128)(2,1)S(1)} %take_near.2.after), channel_id=1, source_target_pairs={{0,8},{4,28},{8,16},{12,4},{16,24},{20,12},{24,0},{28,20},{1,9},{5... | collective-permute-start | bytes 786440 | tf_op jit(solution)/shard_map/ppermute | solution.py:24
  15.0 2.6 %collective-permute-start.5 = (bf16[256,512]{1,0:T(8,128)(2,1)S(1)}, bf16[256,512]{1,0:T(8,128)(2,1)S(1)}, u32[]{:S(2)}, u32[]{:S(2)}) collective-permute-start(bf16[256,512]{1,0:T(8,128)(2,1)S(1)} %take_middle.1.after), channel_id=1, source_target_pairs={{0,4},{4,0},{8,12},{12,8},{16,20},{20,16},{24,28},{28,24},{1,5},{5... | collective-permute-start | bytes 786440 | tf_op jit(solution)/shard_map/ppermute | solution.py:24
  17.6 0.1 collective-permute-start
  17.7 0.0 copy-done.4
  17.7 0.0 copy-done.3
  17.7 1.2 %select_reduce_fusion = f32[512]{0:T(512)S(1)} fusion(f32[4096]{0:T(1024)S(1)} %copy-done.3, s32[512]{0:T(512)S(1)} %copy-done.4), kind=kLoop, calls=%fused_computation | loop fusion | flops 6290944 | bytes 20480 | tf_op jit(solution)/shard_map/reduce_sum | solution.py:241
  18.9 0.0 copy-done.2
  18.9 0.5 collective-permute-done.1.refs_1_
  19.5 2.1 %collective-permute-start.2 = (bf16[256,512]{1,0:T(8,128)(2,1)S(1)}, bf16[256,512]{1,0:T(8,128)(2,1)S(1)}, u32[]{:S(2)}, u32[]{:S(2)}) collective-permute-start(bf16[256,512]{1,0:T(8,128)(2,1)S(1)} %collective-permute-done.1.refs_1_), channel_id=1, source_target_pairs={{0,8},{4,28},{8,16},{12,4},{16,24},{20,12},{24,0},{28,20},{1,9},{5... | collective-permute-start | bytes 786440 | tf_op jit(solution)/shard_map/ppermute | solution.py:24
  21.6 3.5 %collective-permute-done.5.refs_3_ = bf16[256,512]{1,0:T(8,128)(2,1)S(1)} collective-permute-done((bf16[256,512]{1,0:T(8,128)(2,1)S(1)}, bf16[256,512]{1,0:T(8,128)(2,1)S(1)}, u32[]{:S(2)}, u32[]{:S(2)}) %collective-permute-start.5) | collective-permute-done | bytes 262176 | tf_op jit(solution)/shard_map/ppermute | solution.py:24
  25.1 2.1 %collective-permute-start.6 = (bf16[256,512]{1,0:T(8,128)(2,1)S(1)}, bf16[256,512]{1,0:T(8,128)(2,1)S(1)}, u32[]{:S(2)}, u32[]{:S(2)}) collective-permute-start(bf16[256,512]{1,0:T(8,128)(2,1)S(1)} %collective-permute-done.5.refs_3_), channel_id=1, source_target_pairs={{0,8},{4,28},{8,16},{12,4},{16,24},{20,12},{24,0},{28,20},{1,9},{5... | collective-permute-start | bytes 786440 | tf_op jit(solution)/shard_map/ppermute | solution.py:24
  27.2 1.3 %multiply_convert_fusion.left.after = bf16[768,512]{1,0:T(8,128)(2,1)S(1)} fusion(bf16[768,512]{1,0:T(8,128)(2,1)} %refs_0_.1, f32[512]{0:T(512)S(1)} %select_reduce_fusion), kind=kLoop, calls=%fused_computation.2 | loop fusion | flops 1179648 | bytes 1574912 | tf_op jit(solution)/shard_map/convert_element_type | solution.py:242
  28.5 1.4 %collective-permute-done.near.refs_6_ = bf16[256,512]{1,0:T(8,128)(2,1)S(1)} collective-permute-done((bf16[256,512]{1,0:T(8,128)(2,1)S(1)}, bf16[256,512]{1,0:T(8,128)(2,1)S(1)}, u32[]{:S(2)}, u32[]{:S(2)}) %collective-permute-start) | collective-permute-done | bytes 262176 | tf_op jit(solution)/shard_map/ppermute | solution.py:24
  29.9 1.8 %collective-permute-start.10 = (bf16[256,512]{1,0:T(8,128)(2,1)S(1)}, bf16[256,512]{1,0:T(8,128)(2,1)S(1)}, u32[]{:S(2)}, u32[]{:S(2)}) collective-permute-start(bf16[256,512]{1,0:T(8,128)(2,1)S(1)} %collective-permute-done.near.refs_6_), channel_id=1, source_target_pairs={{0,8},{4,28},{8,16},{12,4},{16,24},{20,12},{24,0},{28,20},{1,9},{5... | collective-permute-start | bytes 786440 | tf_op jit(solution)/shard_map/ppermute | solution.py:24
  31.7 0.0 collective-permute-done.2.far.refs_4_
  31.7 0.3 end_blocks.1
  31.9 3.6 %collective-permute-start.3 = (bf16[3,128,128]{2,1,0:T(8,128)(2,1)S(1)}, bf16[3,128,128]{2,1,0:T(8,128)(2,1)S(1)}, u32[]{:S(2)}, u32[]{:S(2)}) collective-permute-start(bf16[3,128,128]{2,1,0:T(8,128)(2,1)S(1)} %end_blocks.1), channel_id=1, source_target_pairs={{0,4},{4,0},{8,12},{12,8},{16,20},{20,16},{24,28},{28,24},{1,5},{5... | collective-permute-start | bytes 294920 | tf_op jit(solution)/shard_map/ppermute | solution.py:24
  35.6 0.0 collective-permute-done.4.refs_2_
  35.6 0.0 collective-permute-done.6.refs_5_
  35.6 0.0 copy-done.1
  35.6 1.8 %pieces_blocks.1.refs_0_ = bf16[6,22,128,128]{3,2,1,0:T(8,128)(2,1)S(1)} custom-call(bf16[768,512]{1,0:T(8,128)(2,1)S(1)} %multiply_convert_fusion.left.after, bf16[768,512]{1,0:T(8,128)(2,1)S(1)} %copy-done.1, bf16[256,512]{1,0:T(8,128)(2,1)S(1)} %collective-permute-done.1.refs_1_, bf16[256,512]{1,0:T(8,128)(2,1)S(1)} %collective-permute-done.4.refs_2_, ...), custom_call_target="tpu_custom_call" | custom-call | flops 20000000000 | bytes 1 | tf_op jit(solution)/shard_map/pieces_blocks/pallas_call | solution.py:63
  37.4 0.7 %collective-permute-done.3.from_partner = bf16[3,128,128]{2,1,0:T(8,128)(2,1)S(1)} collective-permute-done((bf16[3,128,128]{2,1,0:T(8,128)(2,1)S(1)}, bf16[3,128,128]{2,1,0:T(8,128)(2,1)S(1)}, u32[]{:S(2)}, u32[]{:S(2)}) %collective-permute-start.3) | collective-permute-done | bytes 98336 | tf_op jit(solution)/shard_map/ppermute | solution.py:24
  38.1 0.7 %choose_blocks.2 = (bf16[6,22,128,128]{3,2,1,0:T(8,128)(2,1)S(1)}, bf16[2,3,128,128]{3,2,1,0:T(8,128)(2,1)S(1)}, bf16[2,3,128,128]{3,2,1,0:T(8,128)(2,1)S(1)}, b...) custom-call(s32[6,12]{1,0:T(8,128)S(1)} %add_select_fusion.places, ...), custom_call_target="tpu_custom_call", output_to_operand_aliasing={{0}: (4, {})} | custom-call | flops 1 | bytes 1 | tf_op jit(solution)/shard_map/choose_blocks/pallas_call | solution.py:117
  38.8 0.1 collective-permute-start.8
  38.9 0.9 %collective-permute-done.10.refs_0_ = bf16[256,512]{1,0:T(8,128)(2,1)S(1)} collective-permute-done((bf16[256,512]{1,0:T(8,128)(2,1)S(1)}, bf16[256,512]{1,0:T(8,128)(2,1)S(1)}, u32[]{:S(2)}, u32[]{:S(2)}) %collective-permute-start.10) | collective-permute-done | bytes 262176 | tf_op jit(solution)/shard_map/ppermute | solution.py:24
  39.8 0.5 collective-permute-done.8.y.after
  40.4 1.0 %choose_blocks.3 = (bf16[6,22,128,128]{3,2,1,0:T(8,128)(2,1)S(1)}, bf16[4,3,128,128]{3,2,1,0:T(8,128)(2,1)S(1)}, bf16[4,3,128,128]{3,2,1,0:T(8,128)(2,1)S(1)}, b...) custom-call(s32[6,12]{1,0:T(8,128)S(1)} %add_select_fusion.places, ...), custom_call_target="tpu_custom_call", output_to_operand_aliasing={{0}: (5, {})} | custom-call | flops 1 | bytes 1 | tf_op jit(solution)/shard_map/choose_blocks/pallas_call | solution.py:117
  41.4 0.2 collective-permute-start.12
  41.6 0.4 collective-permute-start.7
  42.0 1.6 %collective-permute-start.9 = (bf16[2,3,128,128]{3,2,1,0:T(8,128)(2,1)S(1)}, bf16[2,3,128,128]{3,2,1,0:T(8,128)(2,1)S(1)}, u32[]{:S(2)}, u32[]{:S(2)}) collective-permute-start(bf16[2,3,128,128]{3,2,1,0:T(8,128)(2,1)S(1)} %add.11), channel_id=1, source_target_pairs={{0,2},{1,3},{2,0},{3,1},{4,6},{5,7},{6,4},{7,5},{8,10},{9,11},{10,... | collective-permute-start | bytes 589832 | tf_op jit(solution)/shard_map/ppermute | solution.py:24
  43.6 0.0 collective-permute-start.11
  43.6 0.0 collective-permute-done.12.y
  43.6 0.1 add.12
  43.7 1.2 %collective-permute-start.13 = (bf16[4,3,128,128]{3,2,1,0:T(8,128)(2,1)S(1)}, bf16[4,3,128,128]{3,2,1,0:T(8,128)(2,1)S(1)}, u32[]{:S(2)}, u32[]{:S(2)}) collective-permute-start(bf16[4,3,128,128]{3,2,1,0:T(8,128)(2,1)S(1)} %add.12), channel_id=1, source_target_pairs={{0,2},{1,3},{2,0},{3,1},{4,6},{5,7},{6,4},{7,5},{8,10},{9,11},{10,... | collective-permute-start | bytes 1179656 | tf_op jit(solution)/shard_map/ppermute | solution.py:24
  44.8 0.0 collective-permute-done.7.got_near
  44.8 5.0 %collective-permute-done.9.got = bf16[2,3,128,128]{3,2,1,0:T(8,128)(2,1)S(1)} collective-permute-done((bf16[2,3,128,128]{3,2,1,0:T(8,128)(2,1)S(1)}, bf16[2,3,128,128]{3,2,1,0:T(8,128)(2,1)S(1)}, u32[]{:S(2)}, u32[]{:S(2)}) %collective-permute-start.9) | collective-permute-done | bytes 196640 | tf_op jit(solution)/shard_map/ppermute | solution.py:24
  49.8 0.1 total.1.early
  49.9 0.0 collective-permute-done.11.got_near
  49.9 7.5 %collective-permute-done.13.got = bf16[4,3,128,128]{3,2,1,0:T(8,128)(2,1)S(1)} collective-permute-done((bf16[4,3,128,128]{3,2,1,0:T(8,128)(2,1)S(1)}, bf16[4,3,128,128]{3,2,1,0:T(8,128)(2,1)S(1)}, u32[]{:S(2)}, u32[]{:S(2)}) %collective-permute-start.13) | collective-permute-done | bytes 393248 | tf_op jit(solution)/shard_map/ppermute | solution.py:24
  57.5 0.9 %finish.1 = bf16[6,3,128,128]{3,2,1,0:T(8,128)(2,1)} custom-call(bf16[2,3,128,128]{3,2,1,0:T(8,128)(2,1)S(1)} %total.1.early, bf16[4,3,128,128]{3,2,1,0:T(8,128)(2,1)S(1)} %get-tuple-element.19.near, bf16[4,3,128,128]{3,2,1,0:T(8,128)(2,1)S(1)} %collective-permute-done.11.got_near, bf16[4,3,128,128]{3,2,1,0:T(8,128)(2,1)S(1)} %collective-permute-done.13.got), custom_call_target="tpu_custom_call" | custom-call | flops 1 | bytes 1 | tf_op jit(solution)/shard_map/finish/pallas_call | solution.py:178
  (6 shorter events, 0.1 us)
Async XLA Ops:
  0.0 17.7 %copy-start.4 = (s32[512]{0:T(512)S(1)}, s32[512]{0:T(512)}, u32[]{:S(2)}) copy-start(s32[512]{0:T(512)} %param.6) | copy-start | bytes 6148
  0.0 17.7 %copy-start.3 = (f32[4096]{0:T(1024)S(1)}, f32[4096]{0:T(1024)}, u32[]{:S(2)}) copy-start(f32[4096]{0:T(1024)} %param.5) | copy-start | bytes 49156
  0.0 18.9 %copy-start.2 = (s32[6,12]{1,0:T(8,128)S(1)}, s32[6,12]{1,0:T(8,128)}, u32[]{:S(2)}) copy-start(s32[6,12]{1,0:T(8,128)} %param.7) | copy-start | bytes 868
  9.1 10.4 %collective-permute-start.1 = (bf16[256,512]{1,0:T(8,128)(2,1)}, bf16[256,512]{1,0:T(8,128)(2,1)S(1)}, u32[]{:S(2)}, u32[]{:S(2)}) collective-permute-start(bf16[256,512]{1,0:T(8,128)(2,1)} %take_end.1), channel_id=1, source_target_pairs={{0,4},{4,0},{8,12},{12,8},{16,20},{20,16},{24,28},{28,24},{1,5},{5... | collective-permute-start | bytes 786440 | tf_op jit(solution)/shard_map/ppermute | solution.py:24
  12.1 1.1 %copy-start = (bf16[768,512]{1,0:T(8,128)(2,1)S(1)}, bf16[768,512]{1,0:T(8,128)(2,1)}, u32[]{:S(2)}) copy-start(bf16[768,512]{1,0:T(8,128)(2,1)} %refs_0_.1) | copy-start | bytes 2359300
  13.2 22.3 %copy-start.1 = (bf16[768,512]{1,0:T(8,128)(2,1)S(1)}, bf16[768,512]{1,0:T(8,128)(2,1)}, u32[]{:S(2)}) copy-start(bf16[768,512]{1,0:T(8,128)(2,1)} %refs_0_.1) | copy-start | bytes 2359300
  13.3 22.3 %collective-permute-start.4 = (bf16[256,512]{1,0:T(8,128)(2,1)S(1)}, bf16[256,512]{1,0:T(8,128)(2,1)S(1)}, u32[]{:S(2)}, u32[]{:S(2)}) collective-permute-start(bf16[256,512]{1,0:T(8,128)(2,1)S(1)} %take_near.2.after), channel_id=1, source_target_pairs={{0,8},{4,28},{8,16},{12,4},{16,24},{20,12},{24,0},{28,20},{1,9},{5... | collective-permute-start | bytes 786440 | tf_op jit(solution)/shard_map/ppermute | solution.py:24
  15.0 10.1 %collective-permute-start.5 = (bf16[256,512]{1,0:T(8,128)(2,1)S(1)}, bf16[256,512]{1,0:T(8,128)(2,1)S(1)}, u32[]{:S(2)}, u32[]{:S(2)}) collective-permute-start(bf16[256,512]{1,0:T(8,128)(2,1)S(1)} %take_middle.1.after), channel_id=1, source_target_pairs={{0,4},{4,0},{8,12},{12,8},{16,20},{20,16},{24,28},{28,24},{1,5},{5... | collective-permute-start | bytes 786440 | tf_op jit(solution)/shard_map/ppermute | solution.py:24
  17.6 12.3 %collective-permute-start = (bf16[256,512]{1,0:T(8,128)(2,1)S(1)}, bf16[256,512]{1,0:T(8,128)(2,1)S(1)}, u32[]{:S(2)}, u32[]{:S(2)}) collective-permute-start(bf16[256,512]{1,0:T(8,128)(2,1)S(1)} %take_near.3), channel_id=1, source_target_pairs={{0,4},{4,0},{8,12},{12,8},{16,20},{20,16},{24,28},{28,24},{1,5},{5... | collective-permute-start | bytes 786440 | tf_op jit(solution)/shard_map/ppermute | solution.py:24
  19.5 12.2 %collective-permute-start.2 = (bf16[256,512]{1,0:T(8,128)(2,1)S(1)}, bf16[256,512]{1,0:T(8,128)(2,1)S(1)}, u32[]{:S(2)}, u32[]{:S(2)}) collective-permute-start(bf16[256,512]{1,0:T(8,128)(2,1)S(1)} %collective-permute-done.1.refs_1_), channel_id=1, source_target_pairs={{0,8},{4,28},{8,16},{12,4},{16,24},{20,12},{24,0},{28,20},{1,9},{5... | collective-permute-start | bytes 786440 | tf_op jit(solution)/shard_map/ppermute | solution.py:24
  25.1 10.5 %collective-permute-start.6 = (bf16[256,512]{1,0:T(8,128)(2,1)S(1)}, bf16[256,512]{1,0:T(8,128)(2,1)S(1)}, u32[]{:S(2)}, u32[]{:S(2)}) collective-permute-start(bf16[256,512]{1,0:T(8,128)(2,1)S(1)} %collective-permute-done.5.refs_3_), channel_id=1, source_target_pairs={{0,8},{4,28},{8,16},{12,4},{16,24},{20,12},{24,0},{28,20},{1,9},{5... | collective-permute-start | bytes 786440 | tf_op jit(solution)/shard_map/ppermute | solution.py:24
  29.9 10.0 %collective-permute-start.10 = (bf16[256,512]{1,0:T(8,128)(2,1)S(1)}, bf16[256,512]{1,0:T(8,128)(2,1)S(1)}, u32[]{:S(2)}, u32[]{:S(2)}) collective-permute-start(bf16[256,512]{1,0:T(8,128)(2,1)S(1)} %collective-permute-done.near.refs_6_), channel_id=1, source_target_pairs={{0,8},{4,28},{8,16},{12,4},{16,24},{20,12},{24,0},{28,20},{1,9},{5... | collective-permute-start | bytes 786440 | tf_op jit(solution)/shard_map/ppermute | solution.py:24
  31.9 6.2 %collective-permute-start.3 = (bf16[3,128,128]{2,1,0:T(8,128)(2,1)S(1)}, bf16[3,128,128]{2,1,0:T(8,128)(2,1)S(1)}, u32[]{:S(2)}, u32[]{:S(2)}) collective-permute-start(bf16[3,128,128]{2,1,0:T(8,128)(2,1)S(1)} %end_blocks.1), channel_id=1, source_target_pairs={{0,4},{4,0},{8,12},{12,8},{16,20},{20,16},{24,28},{28,24},{1,5},{5... | collective-permute-start | bytes 294920 | tf_op jit(solution)/shard_map/ppermute | solution.py:24
  38.8 1.5 %collective-permute-start.8 = (bf16[2,3,128,128]{3,2,1,0:T(8,128)(2,1)S(1)}, bf16[2,3,128,128]{3,2,1,0:T(8,128)(2,1)S(1)}, u32[]{:S(2)}, u32[]{:S(2)}) collective-permute-start(bf16[2,3,128,128]{3,2,1,0:T(8,128)(2,1)S(1)} %get-tuple-element.17), channel_id=1, source_target_pairs={{0,1},{1,0},{2,3},{3,2},{4,5},{5,4},{6,7},{7,6},{8,9},{9,8},{10,11... | collective-permute-start | bytes 589832 | tf_op jit(solution)/shard_map/ppermute | solution.py:24
  41.4 2.2 %collective-permute-start.12 = (bf16[4,3,128,128]{3,2,1,0:T(8,128)(2,1)S(1)}, bf16[4,3,128,128]{3,2,1,0:T(8,128)(2,1)S(1)}, u32[]{:S(2)}, u32[]{:S(2)}) collective-permute-start(bf16[4,3,128,128]{3,2,1,0:T(8,128)(2,1)S(1)} %get-tuple-element.22), channel_id=1, source_target_pairs={{0,1},{1,0},{2,3},{3,2},{4,5},{5,4},{6,7},{7,6},{8,9},{9,8},{10,11... | collective-permute-start | bytes 1179656 | tf_op jit(solution)/shard_map/ppermute | solution.py:24
  41.6 3.2 %collective-permute-start.7 = (bf16[2,3,128,128]{3,2,1,0:T(8,128)(2,1)S(1)}, bf16[2,3,128,128]{3,2,1,0:T(8,128)(2,1)S(1)}, u32[]{:S(2)}, u32[]{:S(2)}) collective-permute-start(bf16[2,3,128,128]{3,2,1,0:T(8,128)(2,1)S(1)} %get-tuple-element.15), channel_id=1, source_target_pairs={{0,1},{1,0},{2,3},{3,2},{4,5},{5,4},{6,7},{7,6},{8,9},{9,8},{10,11... | collective-permute-start | bytes 589832 | tf_op jit(solution)/shard_map/ppermute | solution.py:24
  42.0 7.8 %collective-permute-start.9 = (bf16[2,3,128,128]{3,2,1,0:T(8,128)(2,1)S(1)}, bf16[2,3,128,128]{3,2,1,0:T(8,128)(2,1)S(1)}, u32[]{:S(2)}, u32[]{:S(2)}) collective-permute-start(bf16[2,3,128,128]{3,2,1,0:T(8,128)(2,1)S(1)} %add.11), channel_id=1, source_target_pairs={{0,2},{1,3},{2,0},{3,1},{4,6},{5,7},{6,4},{7,5},{8,10},{9,11},{10,... | collective-permute-start | bytes 589832 | tf_op jit(solution)/shard_map/ppermute | solution.py:24
  43.6 6.3 %collective-permute-start.11 = (bf16[4,3,128,128]{3,2,1,0:T(8,128)(2,1)S(1)}, bf16[4,3,128,128]{3,2,1,0:T(8,128)(2,1)S(1)}, u32[]{:S(2)}, u32[]{:S(2)}) collective-permute-start(bf16[4,3,128,128]{3,2,1,0:T(8,128)(2,1)S(1)} %get-tuple-element.20), channel_id=1, source_target_pairs={{0,1},{1,0},{2,3},{3,2},{4,5},{5,4},{6,7},{7,6},{8,9},{9,8},{10,11... | collective-permute-start | bytes 1179656 | tf_op jit(solution)/shard_map/ppermute | solution.py:24
  43.7 13.8 %collective-permute-start.13 = (bf16[4,3,128,128]{3,2,1,0:T(8,128)(2,1)S(1)}, bf16[4,3,128,128]{3,2,1,0:T(8,128)(2,1)S(1)}, u32[]{:S(2)}, u32[]{:S(2)}) collective-permute-start(bf16[4,3,128,128]{3,2,1,0:T(8,128)(2,1)S(1)} %add.12), channel_id=1, source_target_pairs={{0,2},{1,3},{2,0},{3,1},{4,6},{5,7},{6,4},{7,5},{8,10},{9,11},{10,... | collective-permute-start | bytes 1179656 | tf_op jit(solution)/shard_map/ppermute | solution.py:24

commit v7 on v4

--- a/solution.py
+++ b/solution.py
@@ -125,20 +125,20 @@
     )(places, left, from_partner, after, *pieces.values(), dense)
 
 
-def add_kernel(x, y, out):
+def add_kernel(x, y, after, out):
     out[...] = (x[...].astype(jnp.float32) + y[...].astype(jnp.float32)).astype(jnp.bfloat16)
 
 
-def add(x, y):
+def add(x, y, after):
     return pl.pallas_call(
         add_kernel,
         out_shape=jax.ShapeDtypeStruct(x.shape, x.dtype),
-        in_specs=[VMEM] * 2,
+        in_specs=[VMEM] * 3,
         out_specs=VMEM,
         compiler_params=pltpu.CompilerParams(vmem_limit_bytes=LIMIT),
         cost_estimate=SHORT,
         name="add",
-    )(x, y)
+    )(x, y, after)
 
 
 def total_kernel(near, got_near, got, out):
@@ -158,13 +158,19 @@
     )(near, got_near, got)
 
 
-def finish_kernel(chunks, early, near, got_near, got, out):
+def finish_kernel(chunks, early, near, got_near, got, out, rows, done):
     start, later = [natural(first, last) for first, last in chunks]
+    copies = []
     for r in range(early.shape[0]):
-        out[start + r] = early[r]
+        copies.append(pltpu.make_async_copy(early.at[r], out.at[start + r], done.at[r]))
+        copies[-1].start()
     for r in range(near.shape[0]):
         total = near[r].astype(jnp.float32) + got_near[r].astype(jnp.float32) + got[r].astype(jnp.float32)
-        out[later + r] = total.astype(jnp.bfloat16)
+        rows[r] = total.astype(jnp.bfloat16)
+        copies.append(pltpu.make_async_copy(rows.at[r], out.at[later + r], done.at[early.shape[0] + r]))
+        copies[-1].start()
+    for copy in copies:
+        copy.wait()
 
 
 def finish(chunks, early, near, got_near, got):
@@ -172,11 +178,28 @@
         functools.partial(finish_kernel, chunks),
         out_shape=jax.ShapeDtypeStruct((CL,) + near.shape[1:], near.dtype),
         in_specs=[VMEM] * 4,
-        out_specs=VMEM,
+        out_specs=pl.BlockSpec(memory_space=pl.ANY),
+        scratch_shapes=[pltpu.VMEM(near.shape, near.dtype), pltpu.SemaphoreType.DMA((CL,))],
         compiler_params=pltpu.CompilerParams(vmem_limit_bytes=LIMIT),
         cost_estimate=SHORT,
         name="finish",
     )(early, near, got_near, got)
+
+
+def hold_kernel(rows, out):
+    out[...] = rows[...]
+
+
+def hold(rows):
+    return pl.pallas_call(
+        hold_kernel,
+        out_shape=jax.ShapeDtypeStruct(rows.shape, rows.dtype),
+        in_specs=[VMEM],
+        out_specs=VMEM,
+        compiler_params=pltpu.CompilerParams(vmem_limit_bytes=LIMIT),
+        cost_estimate=LONG,
+        name="hold",
+    )(rows)
 
 
 def take_kernel(which, slab, after, out, done):
@@ -213,16 +236,16 @@
     scaled = (slab.astype(jnp.float32) * weight[None, :]).astype(jnp.bfloat16)
 
     early = {0: slab}
-    middle_rows = take(slab, "middle", jnp.zeros((8, 128), jnp.float32))
     end_rows = take(slab, "end", jnp.zeros((8, 128), jnp.float32))
     later_rows = take(slab, "near", jnp.zeros((8, 128), jnp.float32))
+    middle_rows = take(slab, "middle", jnp.zeros((8, 128), jnp.float32))
     near_rows = take(slab, "near", later_rows)
-    early[-4] = move(middle_rows, "wide", partner)
     early[-6] = move(end_rows, "wide", partner)
     early[12] = move(later_rows, "wide", outward)
+    early[-4] = move(middle_rows, "wide", partner)
     near = move(near_rows, "wide", partner)
+    early[6] = move(early[-6], "wide", outward)
     early[8] = move(early[-4], "wide", outward)
-    early[6] = move(early[-6], "wide", outward)
     early[-2] = near
     late = {10: move(near, "wide", outward)}
     from_partner = move(end_blocks(weight, near, early[6]), "wide", partner)
@@ -238,9 +261,9 @@
         )
         got_far = move(send_far, "narrow", lambda n: n ^ 1)
         got_near = move(send_near, "narrow", lambda n: n ^ 1)
-        parts.append((keep_near, got_near, move(add(keep_far, got_far), "narrow", lambda n: n ^ 2)))
+        parts.append((keep_near, got_near, move(add(keep_far, got_far, late[10]), "narrow", lambda n: n ^ 2)))
         after = got_far
-    return finish(chunks, total(*parts[0]), *parts[1])
+    return finish(chunks, hold(total(*parts[0])), *parts[1])
 
 
 def solution(mesh):

time: 50.5 us -> 50.9 us (level)
  starting transfers between devices: 21.8 us -> 22.7 us
    ppermute x14, starting transfers between devices: 21.8 us -> 22.7 us  [move(): lax.ppermute(value, axis, [(s, target(s) % count) for s in range(count)])]
  transfers between devices with their start and end apart: 14 -> 14, of which waited for: 7 -> 7; matrix products, arithmetic and copies ran while one was open for 3% -> 3% of each run, Pallas kernels for 6% -> 8%
where the time goes in v7:
time: 50.9 us; the launch traced here: 50.8 us
  starting transfers between devices  22.7 us (45%)
  waiting for transfers between devices  20.4 us (40%)
  Pallas kernels  5.07 us (10%)
  other arithmetic  1.37 us (3%)
  local copies, waits for them, and re-layouts  1.16 us (2%)
    ppermute x14, starting transfers between devices, move(): lax.ppermute(value, axis, [(s, target(s) % count) for s in range(count)])  22.7 us
    ppermute x14, waiting for transfers between devices, move(): lax.ppermute(value, axis, [(s, target(s) % count) for s in range(count)])  20.4 us
    pallas_call x1, Pallas kernels, pieces_blocks(): pl.pallas_call(functools.partial(pieces_kernel, list(pieces)), out_shape=...  1.85 us
    pallas_call x2, Pallas kernels, choose_blocks(): pl.pallas_call(functools.partial(choose_kernel, share, list(pieces), chun...  1.73 us
    reduce_sum x1, other arithmetic, per_device(): jnp.sum(jnp.where(picks, occupation[None, :], jnp.float32(0.0)), axis=1)  1.22 us
    unnamed x10, local copies, waits for them, and re-layouts  1.16 us
  transfers between devices with their start and end apart: 14, of which 7 were waited for; matrix products, arithmetic and copies ran while one was open for 3% of the time, Pallas kernels for 8%

profile of v7, /device:TPU:0, one launch (start us, length us, event | category | flops | bytes accessed | tf_op | source)
XLA Modules:
  0.0 50.8 jit_solution(2241306311345530770)
XLA Ops:
  0.0 0.0 copy-start.2
  0.0 0.0 copy-start
  0.0 1.1 %copy-done = bf16[768,512]{1,0:T(8,128)(2,1)S(1)} copy-done((bf16[768,512]{1,0:T(8,128)(2,1)S(1)}, bf16[768,512]{1,0:T(8,128)(2,1)}, u32[]{:S(2)}) %copy-start) | copy-done | bytes 786456
  1.1 0.0 copy-start.3
  1.2 0.0 copy-start.4
  1.2 0.0 copy-start.1
  1.2 3.0 %collective-permute-start.1 = (bf16[256,512]{1,0:T(8,128)(2,1)S(1)}, bf16[256,512]{1,0:T(8,128)(2,1)S(1)}, u32[]{:S(2)}, u32[]{:S(2)}) collective-permute-start(bf16[256,512]{1,0:T(8,128)(2,1)S(1)} %take_end.1), channel_id=1, source_target_pairs={{0,4},{4,0},{8,12},{12,8},{16,20},{20,16},{24,28},{28,24},{1,5},{5... | collective-permute-start | bytes 786440 | tf_op jit(solution)/shard_map/ppermute | solution.py:23
  4.3 0.1 collective-permute-start.5
  4.4 2.1 %collective-permute-start.4 = (bf16[256,512]{1,0:T(8,128)(2,1)S(1)}, bf16[256,512]{1,0:T(8,128)(2,1)S(1)}, u32[]{:S(2)}, u32[]{:S(2)}) collective-permute-start(bf16[256,512]{1,0:T(8,128)(2,1)S(1)} %take_near.2.after), channel_id=1, source_target_pairs={{0,8},{4,28},{8,16},{12,4},{16,24},{20,12},{24,0},{28,20},{1,9},{5... | collective-permute-start | bytes 786440 | tf_op jit(solution)/shard_map/ppermute | solution.py:23
  6.5 3.6 %collective-permute-start = (bf16[256,512]{1,0:T(8,128)(2,1)S(1)}, bf16[256,512]{1,0:T(8,128)(2,1)S(1)}, u32[]{:S(2)}, u32[]{:S(2)}) collective-permute-start(bf16[256,512]{1,0:T(8,128)(2,1)S(1)} %take_near.3), channel_id=1, source_target_pairs={{0,4},{4,0},{8,12},{12,8},{16,20},{20,16},{24,28},{28,24},{1,5},{5... | collective-permute-start | bytes 786440 | tf_op jit(solution)/shard_map/ppermute | solution.py:23
  10.1 0.0 copy-done.3
  10.1 0.0 copy-done.4
  10.2 1.2 %select_reduce_fusion = f32[512]{0:T(512)S(1)} fusion(f32[4096]{0:T(1024)S(1)} %copy-done.3, s32[512]{0:T(512)S(1)} %copy-done.4), kind=kLoop, calls=%fused_computation | loop fusion | flops 6290944 | bytes 20480 | tf_op jit(solution)/shard_map/reduce_sum | solution.py:235
  11.4 0.0 copy-done.2
  11.4 0.0 collective-permute-done.1.refs_1_
  11.4 2.1 %collective-permute-start.2 = (bf16[256,512]{1,0:T(8,128)(2,1)S(1)}, bf16[256,512]{1,0:T(8,128)(2,1)S(1)}, u32[]{:S(2)}, u32[]{:S(2)}) collective-permute-start(bf16[256,512]{1,0:T(8,128)(2,1)S(1)} %collective-permute-done.1.refs_1_), channel_id=1, source_target_pairs={{0,8},{4,28},{8,16},{12,4},{16,24},{20,12},{24,0},{28,20},{1,9},{5... | collective-permute-start | bytes 786440 | tf_op jit(solution)/shard_map/ppermute | solution.py:23
  13.5 3.5 %collective-permute-done.5.refs_3_ = bf16[256,512]{1,0:T(8,128)(2,1)S(1)} collective-permute-done((bf16[256,512]{1,0:T(8,128)(2,1)S(1)}, bf16[256,512]{1,0:T(8,128)(2,1)S(1)}, u32[]{:S(2)}, u32[]{:S(2)}) %collective-permute-start.5) | collective-permute-done | bytes 262176 | tf_op jit(solution)/shard_map/ppermute | solution.py:23
  17.0 2.1 %collective-permute-start.6 = (bf16[256,512]{1,0:T(8,128)(2,1)S(1)}, bf16[256,512]{1,0:T(8,128)(2,1)S(1)}, u32[]{:S(2)}, u32[]{:S(2)}) collective-permute-start(bf16[256,512]{1,0:T(8,128)(2,1)S(1)} %collective-permute-done.5.refs_3_), channel_id=1, source_target_pairs={{0,8},{4,28},{8,16},{12,4},{16,24},{20,12},{24,0},{28,20},{1,9},{5... | collective-permute-start | bytes 786440 | tf_op jit(solution)/shard_map/ppermute | solution.py:23
  19.1 0.0 copy-done.1
  19.1 0.1 multiply_convert_fusion.left.after
  19.2 2.5 %collective-permute-done.near.refs_6_ = bf16[256,512]{1,0:T(8,128)(2,1)S(1)} collective-permute-done((bf16[256,512]{1,0:T(8,128)(2,1)S(1)}, bf16[256,512]{1,0:T(8,128)(2,1)S(1)}, u32[]{:S(2)}, u32[]{:S(2)}) %collective-permute-start) | collective-permute-done | bytes 262176 | tf_op jit(solution)/shard_map/ppermute | solution.py:23
  21.8 1.8 %collective-permute-start.9 = (bf16[256,512]{1,0:T(8,128)(2,1)S(1)}, bf16[256,512]{1,0:T(8,128)(2,1)S(1)}, u32[]{:S(2)}, u32[]{:S(2)}) collective-permute-start(bf16[256,512]{1,0:T(8,128)(2,1)S(1)} %collective-permute-done.near.refs_6_), channel_id=1, source_target_pairs={{0,8},{4,28},{8,16},{12,4},{16,24},{20,12},{24,0},{28,20},{1,9},{5... | collective-permute-start | bytes 786440 | tf_op jit(solution)/shard_map/ppermute | solution.py:23
  23.6 0.0 collective-permute-done.2.far.refs_4_
  23.6 0.3 end_blocks.1
  23.9 3.6 %collective-permute-start.3 = (bf16[3,128,128]{2,1,0:T(8,128)(2,1)S(1)}, bf16[3,128,128]{2,1,0:T(8,128)(2,1)S(1)}, u32[]{:S(2)}, u32[]{:S(2)}) collective-permute-start(bf16[3,128,128]{2,1,0:T(8,128)(2,1)S(1)} %end_blocks.1), channel_id=1, source_target_pairs={{0,4},{4,0},{8,12},{12,8},{16,20},{20,16},{24,28},{28,24},{1,5},{5... | collective-permute-start | bytes 294920 | tf_op jit(solution)/shard_map/ppermute | solution.py:23
  27.5 0.0 collective-permute-done.4.refs_2_
  27.5 0.0 collective-permute-done.6.refs_5_
  27.5 1.8 %pieces_blocks.1.refs_0_ = bf16[6,22,128,128]{3,2,1,0:T(8,128)(2,1)S(1)} custom-call(bf16[768,512]{1,0:T(8,128)(2,1)S(1)} %multiply_convert_fusion.left.after, bf16[768,512]{1,0:T(8,128)(2,1)S(1)} %copy-done.1, bf16[256,512]{1,0:T(8,128)(2,1)S(1)} %collective-permute-done.1.refs_1_, bf16[256,512]{1,0:T(8,128)(2,1)S(1)} %collective-permute-done.4.refs_2_, ...), custom_call_target="tpu_custom_call" | custom-call | flops 20000000000 | bytes 1 | tf_op jit(solution)/shard_map/pieces_blocks/pallas_call | solution.py:62
  29.3 0.7 %collective-permute-done.3.from_partner = bf16[3,128,128]{2,1,0:T(8,128)(2,1)S(1)} collective-permute-done((bf16[3,128,128]{2,1,0:T(8,128)(2,1)S(1)}, bf16[3,128,128]{2,1,0:T(8,128)(2,1)S(1)}, u32[]{:S(2)}, u32[]{:S(2)}) %collective-permute-start.3) | collective-permute-done | bytes 98336 | tf_op jit(solution)/shard_map/ppermute | solution.py:23
  30.1 0.7 %choose_blocks.2 = (bf16[6,22,128,128]{3,2,1,0:T(8,128)(2,1)S(1)}, bf16[2,3,128,128]{3,2,1,0:T(8,128)(2,1)S(1)}, bf16[2,3,128,128]{3,2,1,0:T(8,128)(2,1)S(1)}, b...) custom-call(s32[6,12]{1,0:T(8,128)S(1)} %add_select_fusion.places, ...), custom_call_target="tpu_custom_call", output_to_operand_aliasing={{0}: (4, {})} | custom-call | flops 1 | bytes 1 | tf_op jit(solution)/shard_map/choose_blocks/pallas_call | solution.py:116
  30.7 0.1 collective-permute-start.8
  30.8 0.5 collective-permute-start.7
  31.3 0.1 collective-permute-done.9.after.refs_0_
  31.4 0.8 %collective-permute-done.8.y.after = bf16[2,3,128,128]{3,2,1,0:T(8,128)(2,1)S(1)} collective-permute-done((bf16[2,3,128,128]{3,2,1,0:T(8,128)(2,1)S(1)}, bf16[2,3,128,128]{3,2,1,0:T(8,128)(2,1)S(1)}, u32[]{:S(2)}, u32[]{:S(2)}) %collective-permute-start.8) | collective-permute-done | bytes 196640 | tf_op jit(solution)/shard_map/ppermute | solution.py:23
  32.3 1.6 %collective-permute-start.10 = (bf16[2,3,128,128]{3,2,1,0:T(8,128)(2,1)S(1)}, bf16[2,3,128,128]{3,2,1,0:T(8,128)(2,1)S(1)}, u32[]{:S(2)}, u32[]{:S(2)}) collective-permute-start(bf16[2,3,128,128]{3,2,1,0:T(8,128)(2,1)S(1)} %add.11), channel_id=1, source_target_pairs={{0,2},{1,3},{2,0},{3,1},{4,6},{5,7},{6,4},{7,5},{8,10},{9,11},{10,... | collective-permute-start | bytes 589832 | tf_op jit(solution)/shard_map/ppermute | solution.py:23
  33.9 1.0 %choose_blocks.3 = (bf16[6,22,128,128]{3,2,1,0:T(8,128)(2,1)S(1)}, bf16[4,3,128,128]{3,2,1,0:T(8,128)(2,1)S(1)}, bf16[4,3,128,128]{3,2,1,0:T(8,128)(2,1)S(1)}, b...) custom-call(s32[6,12]{1,0:T(8,128)S(1)} %add_select_fusion.places, ...), custom_call_target="tpu_custom_call", output_to_operand_aliasing={{0}: (5, {})} | custom-call | flops 1 | bytes 1 | tf_op jit(solution)/shard_map/choose_blocks/pallas_call | solution.py:116
  34.9 0.1 collective-permute-start.11
  35.0 0.5 collective-permute-start.12
  35.5 0.0 collective-permute-done.7.got_near
  35.5 3.8 %collective-permute-done.10.got = bf16[2,3,128,128]{3,2,1,0:T(8,128)(2,1)S(1)} collective-permute-done((bf16[2,3,128,128]{3,2,1,0:T(8,128)(2,1)S(1)}, bf16[2,3,128,128]{3,2,1,0:T(8,128)(2,1)S(1)}, u32[]{:S(2)}, u32[]{:S(2)}) %collective-permute-start.10) | collective-permute-done | bytes 196640 | tf_op jit(solution)/shard_map/ppermute | solution.py:23
  39.3 0.1 total.1.rows
  39.4 0.0 collective-permute-done.12.y
  39.4 0.1 add.12
  39.5 1.6 %collective-permute-start.13 = (bf16[4,3,128,128]{3,2,1,0:T(8,128)(2,1)S(1)}, bf16[4,3,128,128]{3,2,1,0:T(8,128)(2,1)S(1)}, u32[]{:S(2)}, u32[]{:S(2)}) collective-permute-start(bf16[4,3,128,128]{3,2,1,0:T(8,128)(2,1)S(1)} %add.12), channel_id=1, source_target_pairs={{0,2},{1,3},{2,0},{3,1},{4,6},{5,7},{6,4},{7,5},{8,10},{9,11},{10,... | collective-permute-start | bytes 1179656 | tf_op jit(solution)/shard_map/ppermute | solution.py:23
  41.1 0.0 collective-permute-done.11.got_near
  41.1 8.8 %collective-permute-done.13.got = bf16[4,3,128,128]{3,2,1,0:T(8,128)(2,1)S(1)} collective-permute-done((bf16[4,3,128,128]{3,2,1,0:T(8,128)(2,1)S(1)}, bf16[4,3,128,128]{3,2,1,0:T(8,128)(2,1)S(1)}, u32[]{:S(2)}, u32[]{:S(2)}) %collective-permute-start.13) | collective-permute-done | bytes 393248 | tf_op jit(solution)/shard_map/ppermute | solution.py:23
  49.9 0.9 %finish.1 = bf16[6,3,128,128]{3,2,1,0:T(8,128)(2,1)} custom-call(bf16[2,3,128,128]{3,2,1,0:T(8,128)(2,1)S(1)} %hold.1.early, bf16[4,3,128,128]{3,2,1,0:T(8,128)(2,1)S(1)} %get-tuple-element.19.near, bf16[4,3,128,128]{3,2,1,0:T(8,128)(2,1)S(1)} %collective-permute-done.11.got_near, bf16[4,3,128,128]{3,2,1,0:T(8,128)(2,1)S(1)} %collective-permute-done.13.got), custom_call_target="tpu_custom_call" | custom-call | flops 1 | bytes 1 | tf_op jit(solution)/shard_map/finish/pallas_call | solution.py:177
  (8 shorter events, 0.2 us)
Async XLA Ops:
  0.0 11.4 %copy-start.2 = (s32[6,12]{1,0:T(8,128)S(1)}, s32[6,12]{1,0:T(8,128)}, u32[]{:S(2)}) copy-start(s32[6,12]{1,0:T(8,128)} %param.7) | copy-start | bytes 868
  0.0 1.1 %copy-start = (bf16[768,512]{1,0:T(8,128)(2,1)S(1)}, bf16[768,512]{1,0:T(8,128)(2,1)}, u32[]{:S(2)}) copy-start(bf16[768,512]{1,0:T(8,128)(2,1)} %refs_0_.1) | copy-start | bytes 2359300
  1.1 9.0 %copy-start.3 = (f32[4096]{0:T(1024)S(1)}, f32[4096]{0:T(1024)}, u32[]{:S(2)}) copy-start(f32[4096]{0:T(1024)} %param.5) | copy-start | bytes 49156
  1.2 9.0 %copy-start.4 = (s32[512]{0:T(512)S(1)}, s32[512]{0:T(512)}, u32[]{:S(2)}) copy-start(s32[512]{0:T(512)} %param.6) | copy-start | bytes 6148
  1.2 17.9 %copy-start.1 = (bf16[768,512]{1,0:T(8,128)(2,1)S(1)}, bf16[768,512]{1,0:T(8,128)(2,1)}, u32[]{:S(2)}) copy-start(bf16[768,512]{1,0:T(8,128)(2,1)} %refs_0_.1) | copy-start | bytes 2359300
  1.2 10.2 %collective-permute-start.1 = (bf16[256,512]{1,0:T(8,128)(2,1)S(1)}, bf16[256,512]{1,0:T(8,128)(2,1)S(1)}, u32[]{:S(2)}, u32[]{:S(2)}) collective-permute-start(bf16[256,512]{1,0:T(8,128)(2,1)S(1)} %take_end.1), channel_id=1, source_target_pairs={{0,4},{4,0},{8,12},{12,8},{16,20},{20,16},{24,28},{28,24},{1,5},{5... | collective-permute-start | bytes 786440 | tf_op jit(solution)/shard_map/ppermute | solution.py:23
  4.3 12.7 %collective-permute-start.5 = (bf16[256,512]{1,0:T(8,128)(2,1)S(1)}, bf16[256,512]{1,0:T(8,128)(2,1)S(1)}, u32[]{:S(2)}, u32[]{:S(2)}) collective-permute-start(bf16[256,512]{1,0:T(8,128)(2,1)S(1)} %take_middle.1), channel_id=1, source_target_pairs={{0,4},{4,0},{8,12},{12,8},{16,20},{20,16},{24,28},{28,24},{1,5},{5... | collective-permute-start | bytes 786440 | tf_op jit(solution)/shard_map/ppermute | solution.py:23
  4.4 23.1 %collective-permute-start.4 = (bf16[256,512]{1,0:T(8,128)(2,1)S(1)}, bf16[256,512]{1,0:T(8,128)(2,1)S(1)}, u32[]{:S(2)}, u32[]{:S(2)}) collective-permute-start(bf16[256,512]{1,0:T(8,128)(2,1)S(1)} %take_near.2.after), channel_id=1, source_target_pairs={{0,8},{4,28},{8,16},{12,4},{16,24},{20,12},{24,0},{28,20},{1,9},{5... | collective-permute-start | bytes 786440 | tf_op jit(solution)/shard_map/ppermute | solution.py:23
  6.5 15.2 %collective-permute-start = (bf16[256,512]{1,0:T(8,128)(2,1)S(1)}, bf16[256,512]{1,0:T(8,128)(2,1)S(1)}, u32[]{:S(2)}, u32[]{:S(2)}) collective-permute-start(bf16[256,512]{1,0:T(8,128)(2,1)S(1)} %take_near.3), channel_id=1, source_target_pairs={{0,4},{4,0},{8,12},{12,8},{16,20},{20,16},{24,28},{28,24},{1,5},{5... | collective-permute-start | bytes 786440 | tf_op jit(solution)/shard_map/ppermute | solution.py:23
  11.4 12.2 %collective-permute-start.2 = (bf16[256,512]{1,0:T(8,128)(2,1)S(1)}, bf16[256,512]{1,0:T(8,128)(2,1)S(1)}, u32[]{:S(2)}, u32[]{:S(2)}) collective-permute-start(bf16[256,512]{1,0:T(8,128)(2,1)S(1)} %collective-permute-done.1.refs_1_), channel_id=1, source_target_pairs={{0,8},{4,28},{8,16},{12,4},{16,24},{20,12},{24,0},{28,20},{1,9},{5... | collective-permute-start | bytes 786440 | tf_op jit(solution)/shard_map/ppermute | solution.py:23
  17.0 10.5 %collective-permute-start.6 = (bf16[256,512]{1,0:T(8,128)(2,1)S(1)}, bf16[256,512]{1,0:T(8,128)(2,1)S(1)}, u32[]{:S(2)}, u32[]{:S(2)}) collective-permute-start(bf16[256,512]{1,0:T(8,128)(2,1)S(1)} %collective-permute-done.5.refs_3_), channel_id=1, source_target_pairs={{0,8},{4,28},{8,16},{12,4},{16,24},{20,12},{24,0},{28,20},{1,9},{5... | collective-permute-start | bytes 786440 | tf_op jit(solution)/shard_map/ppermute | solution.py:23
  21.8 9.7 %collective-permute-start.9 = (bf16[256,512]{1,0:T(8,128)(2,1)S(1)}, bf16[256,512]{1,0:T(8,128)(2,1)S(1)}, u32[]{:S(2)}, u32[]{:S(2)}) collective-permute-start(bf16[256,512]{1,0:T(8,128)(2,1)S(1)} %collective-permute-done.near.refs_6_), channel_id=1, source_target_pairs={{0,8},{4,28},{8,16},{12,4},{16,24},{20,12},{24,0},{28,20},{1,9},{5... | collective-permute-start | bytes 786440 | tf_op jit(solution)/shard_map/ppermute | solution.py:23
  23.9 6.2 %collective-permute-start.3 = (bf16[3,128,128]{2,1,0:T(8,128)(2,1)S(1)}, bf16[3,128,128]{2,1,0:T(8,128)(2,1)S(1)}, u32[]{:S(2)}, u32[]{:S(2)}) collective-permute-start(bf16[3,128,128]{2,1,0:T(8,128)(2,1)S(1)} %end_blocks.1), channel_id=1, source_target_pairs={{0,4},{4,0},{8,12},{12,8},{16,20},{20,16},{24,28},{28,24},{1,5},{5... | collective-permute-start | bytes 294920 | tf_op jit(solution)/shard_map/ppermute | solution.py:23
  30.7 1.5 %collective-permute-start.8 = (bf16[2,3,128,128]{3,2,1,0:T(8,128)(2,1)S(1)}, bf16[2,3,128,128]{3,2,1,0:T(8,128)(2,1)S(1)}, u32[]{:S(2)}, u32[]{:S(2)}) collective-permute-start(bf16[2,3,128,128]{3,2,1,0:T(8,128)(2,1)S(1)} %get-tuple-element.17), channel_id=1, source_target_pairs={{0,1},{1,0},{2,3},{3,2},{4,5},{5,4},{6,7},{7,6},{8,9},{9,8},{10,11... | collective-permute-start | bytes 589832 | tf_op jit(solution)/shard_map/ppermute | solution.py:23
  30.8 4.7 %collective-permute-start.7 = (bf16[2,3,128,128]{3,2,1,0:T(8,128)(2,1)S(1)}, bf16[2,3,128,128]{3,2,1,0:T(8,128)(2,1)S(1)}, u32[]{:S(2)}, u32[]{:S(2)}) collective-permute-start(bf16[2,3,128,128]{3,2,1,0:T(8,128)(2,1)S(1)} %get-tuple-element.15), channel_id=1, source_target_pairs={{0,1},{1,0},{2,3},{3,2},{4,5},{5,4},{6,7},{7,6},{8,9},{9,8},{10,11... | collective-permute-start | bytes 589832 | tf_op jit(solution)/shard_map/ppermute | solution.py:23
  32.3 7.0 %collective-permute-start.10 = (bf16[2,3,128,128]{3,2,1,0:T(8,128)(2,1)S(1)}, bf16[2,3,128,128]{3,2,1,0:T(8,128)(2,1)S(1)}, u32[]{:S(2)}, u32[]{:S(2)}) collective-permute-start(bf16[2,3,128,128]{3,2,1,0:T(8,128)(2,1)S(1)} %add.11), channel_id=1, source_target_pairs={{0,2},{1,3},{2,0},{3,1},{4,6},{5,7},{6,4},{7,5},{8,10},{9,11},{10,... | collective-permute-start | bytes 589832 | tf_op jit(solution)/shard_map/ppermute | solution.py:23
  34.9 6.2 %collective-permute-start.11 = (bf16[4,3,128,128]{3,2,1,0:T(8,128)(2,1)S(1)}, bf16[4,3,128,128]{3,2,1,0:T(8,128)(2,1)S(1)}, u32[]{:S(2)}, u32[]{:S(2)}) collective-permute-start(bf16[4,3,128,128]{3,2,1,0:T(8,128)(2,1)S(1)} %get-tuple-element.20), channel_id=1, source_target_pairs={{0,1},{1,0},{2,3},{3,2},{4,5},{5,4},{6,7},{7,6},{8,9},{9,8},{10,11... | collective-permute-start | bytes 1179656 | tf_op jit(solution)/shard_map/ppermute | solution.py:23
  35.0 4.4 %collective-permute-start.12 = (bf16[4,3,128,128]{3,2,1,0:T(8,128)(2,1)S(1)}, bf16[4,3,128,128]{3,2,1,0:T(8,128)(2,1)S(1)}, u32[]{:S(2)}, u32[]{:S(2)}) collective-permute-start(bf16[4,3,128,128]{3,2,1,0:T(8,128)(2,1)S(1)} %get-tuple-element.22), channel_id=1, source_target_pairs={{0,1},{1,0},{2,3},{3,2},{4,5},{5,4},{6,7},{7,6},{8,9},{9,8},{10,11... | collective-permute-start | bytes 1179656 | tf_op jit(solution)/shard_map/ppermute | solution.py:23
  39.5 10.4 %collective-permute-start.13 = (bf16[4,3,128,128]{3,2,1,0:T(8,128)(2,1)S(1)}, bf16[4,3,128,128]{3,2,1,0:T(8,128)(2,1)S(1)}, u32[]{:S(2)}, u32[]{:S(2)}) collective-permute-start(bf16[4,3,128,128]{3,2,1,0:T(8,128)(2,1)S(1)} %add.12), channel_id=1, source_target_pairs={{0,2},{1,3},{2,0},{3,1},{4,6},{5,7},{6,4},{7,5},{8,10},{9,11},{10,... | collective-permute-start | bytes 1179656 | tf_op jit(solution)/shard_map/ppermute | solution.py:23

commit v8 on v6

--- a/solution.py
+++ b/solution.py
@@ -14,7 +14,6 @@
 VMEM = pl.BlockSpec(memory_space=pltpu.VMEM)
 SMEM = pl.BlockSpec(memory_space=pltpu.SMEM)
 LIMIT = 40 * 1024 * 1024
-WHOLE = 65280 * 1024
 LONG = pl.CostEstimate(flops=20 * 10**9, bytes_accessed=1, transcendentals=0)
 SHORT = pl.CostEstimate(flops=1, bytes_accessed=1, transcendentals=0)
 
@@ -94,13 +93,17 @@
     )(weight[None, :], near, far)
 
 
-def choose_kernel(share, marks, chunk, ends, places, left, from_partner, after, *refs):
+def choose_kernel(share, marks, chunk, ends, all_places, left, from_partner, after, *refs):
     dense = refs[len(marks) + 1]
-    outs = refs[len(marks) + 2 :]
+    outs = refs[len(marks) + 2 : -2]
+    places, done = refs[-2:]
+    fetch = pltpu.make_async_copy(all_places, places, done)
+    fetch.start()
     add_pieces(marks, refs[: len(marks)], left, dense)
     if ends:
         for at, (c, m) in enumerate(((0, -7), (0, -8), (1, -7))):
             dense[natural(c, c), natural(m, m) + REACH] = from_partner[at]
+    fetch.wait()
     first, last = chunk
     start = natural(first, last)
     me = lax.axis_index("narrow")
@@ -117,8 +120,9 @@
     return pl.pallas_call(
         functools.partial(choose_kernel, share, list(pieces), chunk, ends),
         out_shape=shapes,
-        in_specs=[SMEM] + [VMEM] * (4 + len(pieces)),
+        in_specs=[VMEM] * (5 + len(pieces)),
         out_specs=[VMEM] * len(shapes),
+        scratch_shapes=[pltpu.SMEM(places.shape, places.dtype), pltpu.SemaphoreType.DMA],
         input_output_aliases={4 + len(pieces): 0},
         compiler_params=pltpu.CompilerParams(vmem_limit_bytes=LIMIT),
         cost_estimate=SHORT,
@@ -195,27 +199,6 @@
     copy.wait()
 
 
-def first_take_kernel(slab, out, done):
-    odd = lax.rem(lax.axis_index("wide"), 2)
-    copy = pltpu.make_async_copy(slab.at[pl.ds(pl.multiple_of(odd * 2 * PAIR * B, PAIR * B), PAIR * B), :], out, done)
-    copy.start()
-    copy.wait()
-
-
-def first_take(slab):
-    hbm = pl.BlockSpec(memory_space=pl.ANY)
-    return pl.pallas_call(
-        first_take_kernel,
-        out_shape=jax.ShapeDtypeStruct((PAIR * B, slab.shape[1]), slab.dtype),
-        in_specs=[hbm],
-        out_specs=hbm,
-        scratch_shapes=[pltpu.SemaphoreType.DMA],
-        compiler_params=pltpu.CompilerParams(vmem_limit_bytes=WHOLE),
-        cost_estimate=SHORT,
-        name="take_end",
-    )(slab)
-
-
 def take(slab, which, after):
     return pl.pallas_call(
         functools.partial(take_kernel, which),
@@ -242,10 +225,10 @@
     scaled = (slab.astype(jnp.float32) * weight[None, :]).astype(jnp.bfloat16)
 
     early = {0: slab}
-    end_rows = first_take(slab)
+    end_rows = take(slab, "end", jnp.zeros((8, 128), jnp.float32))
     later_rows = take(slab, "near", jnp.zeros((8, 128), jnp.float32))
-    middle_rows = take(slab, "middle", later_rows)
-    near_rows = take(slab, "near", middle_rows)
+    middle_rows = take(slab, "middle", jnp.zeros((8, 128), jnp.float32))
+    near_rows = take(slab, "near", later_rows)
     early[-6] = move(end_rows, "wide", partner)
     early[12] = move(later_rows, "wide", outward)
     early[-4] = move(middle_rows, "wide", partner)

time: 58.5 us -> 50 us (0.85)
  Pallas kernels: 14.1 us -> 4.74 us
  starting transfers between devices: 20.4 us -> 21.8 us
  other arithmetic: 2.51 us -> 1.37 us
  waiting for transfers between devices: 20.1 us -> 20.7 us
    pallas_call x1 -> x0, Pallas kernels: 9.05 us -> none  [first_take(): pl.pallas_call(first_take_kernel, out_shape=jax.ShapeDtypeStruct((PAIR *...]
    ppermute x14, starting transfers between devices: 20.4 us -> 21.8 us  [move(): lax.ppermute(value, axis, [(s, target(s) % count) for s in range(count)])]
    convert_element_type x1, other arithmetic: 1.27 us -> 0.14 us  [per_device(): scaled = (slab.astype(jnp.float32) * weight[None, :]).astype(jnp.bfloat16)]
    ppermute x14, waiting for transfers between devices: 20.1 us -> 20.7 us  [move(): lax.ppermute(value, axis, [(s, target(s) % count) for s in range(count)])]
  transfers between devices with their start and end apart: 14 -> 14, of which waited for: 8 -> 7; matrix products, arithmetic and copies ran while one was open for 4% -> 3% of each run, Pallas kernels for 5% -> 6%
where the time goes in v8:
time: 50 us; the launch traced here: 49.9 us
  starting transfers between devices  21.8 us (44%)
  waiting for transfers between devices  20.7 us (41%)
  Pallas kernels  4.74 us (9%)
  other arithmetic  1.37 us (3%)
  local copies, waits for them, and re-layouts  1.16 us (2%)
    ppermute x14, starting transfers between devices, move(): lax.ppermute(value, axis, [(s, target(s) % count) for s in range(count)])  21.8 us
    ppermute x14, waiting for transfers between devices, move(): lax.ppermute(value, axis, [(s, target(s) % count) for s in range(count)])  20.7 us
    pallas_call x1, Pallas kernels, pieces_blocks(): pl.pallas_call(functools.partial(pieces_kernel, list(pieces)), out_shape=...  1.85 us
    pallas_call x2, Pallas kernels, choose_blocks(): pl.pallas_call(functools.partial(choose_kernel, share, list(pieces), chun...  1.4 us
    reduce_sum x1, other arithmetic, per_device(): jnp.sum(jnp.where(picks, occupation[None, :], jnp.float32(0.0)), axis=1)  1.22 us
    unnamed x10, local copies, waits for them, and re-layouts  1.16 us
  transfers between devices with their start and end apart: 14, of which 7 were waited for; matrix products, arithmetic and copies ran while one was open for 3% of the time, Pallas kernels for 6%

profile of v8, /device:TPU:0, one launch (start us, length us, event | category | flops | bytes accessed | tf_op | source)
XLA Modules:
  0.0 49.9 jit_solution(8743956505292520585)
XLA Ops:
  0.0 0.0 copy-start.2
  0.0 0.0 copy-start
  0.0 1.1 %copy-done = bf16[768,512]{1,0:T(8,128)(2,1)S(1)} copy-done((bf16[768,512]{1,0:T(8,128)(2,1)S(1)}, bf16[768,512]{1,0:T(8,128)(2,1)}, u32[]{:S(2)}) %copy-start) | copy-done | bytes 786456
  1.1 0.0 copy-start.3
  1.2 0.0 copy-start.4
  1.2 0.0 copy-start.1
  1.2 3.0 %collective-permute-start.1 = (bf16[256,512]{1,0:T(8,128)(2,1)S(1)}, bf16[256,512]{1,0:T(8,128)(2,1)S(1)}, u32[]{:S(2)}, u32[]{:S(2)}) collective-permute-start(bf16[256,512]{1,0:T(8,128)(2,1)S(1)} %take_end.1), channel_id=1, source_target_pairs={{0,4},{4,0},{8,12},{12,8},{16,20},{20,16},{24,28},{28,24},{1,5},{5... | collective-permute-start | bytes 786440 | tf_op jit(solution)/shard_map/ppermute | solution.py:23
  4.3 0.1 collective-permute-start.5
  4.4 2.1 %collective-permute-start.4 = (bf16[256,512]{1,0:T(8,128)(2,1)S(1)}, bf16[256,512]{1,0:T(8,128)(2,1)S(1)}, u32[]{:S(2)}, u32[]{:S(2)}) collective-permute-start(bf16[256,512]{1,0:T(8,128)(2,1)S(1)} %take_near.2.after), channel_id=1, source_target_pairs={{0,8},{4,28},{8,16},{12,4},{16,24},{20,12},{24,0},{28,20},{1,9},{5... | collective-permute-start | bytes 786440 | tf_op jit(solution)/shard_map/ppermute | solution.py:23
  6.5 3.6 %collective-permute-start = (bf16[256,512]{1,0:T(8,128)(2,1)S(1)}, bf16[256,512]{1,0:T(8,128)(2,1)S(1)}, u32[]{:S(2)}, u32[]{:S(2)}) collective-permute-start(bf16[256,512]{1,0:T(8,128)(2,1)S(1)} %take_near.3), channel_id=1, source_target_pairs={{0,4},{4,0},{8,12},{12,8},{16,20},{20,16},{24,28},{28,24},{1,5},{5... | collective-permute-start | bytes 786440 | tf_op jit(solution)/shard_map/ppermute | solution.py:23
  10.1 0.0 copy-done.3
  10.1 0.0 copy-done.4
  10.2 1.2 %select_reduce_fusion = f32[512]{0:T(512)S(1)} fusion(f32[4096]{0:T(1024)S(1)} %copy-done.3, s32[512]{0:T(512)S(1)} %copy-done.4), kind=kLoop, calls=%fused_computation | loop fusion | flops 6290944 | bytes 20480 | tf_op jit(solution)/shard_map/reduce_sum | solution.py:224
  11.4 0.0 copy-done.2
  11.4 0.0 collective-permute-done.1.refs_1_
  11.4 2.1 %collective-permute-start.2 = (bf16[256,512]{1,0:T(8,128)(2,1)S(1)}, bf16[256,512]{1,0:T(8,128)(2,1)S(1)}, u32[]{:S(2)}, u32[]{:S(2)}) collective-permute-start(bf16[256,512]{1,0:T(8,128)(2,1)S(1)} %collective-permute-done.1.refs_1_), channel_id=1, source_target_pairs={{0,8},{4,28},{8,16},{12,4},{16,24},{20,12},{24,0},{28,20},{1,9},{5... | collective-permute-start | bytes 786440 | tf_op jit(solution)/shard_map/ppermute | solution.py:23
  13.5 3.5 %collective-permute-done.5.refs_3_ = bf16[256,512]{1,0:T(8,128)(2,1)S(1)} collective-permute-done((bf16[256,512]{1,0:T(8,128)(2,1)S(1)}, bf16[256,512]{1,0:T(8,128)(2,1)S(1)}, u32[]{:S(2)}, u32[]{:S(2)}) %collective-permute-start.5) | collective-permute-done | bytes 262176 | tf_op jit(solution)/shard_map/ppermute | solution.py:23
  17.0 2.1 %collective-permute-start.6 = (bf16[256,512]{1,0:T(8,128)(2,1)S(1)}, bf16[256,512]{1,0:T(8,128)(2,1)S(1)}, u32[]{:S(2)}, u32[]{:S(2)}) collective-permute-start(bf16[256,512]{1,0:T(8,128)(2,1)S(1)} %collective-permute-done.5.refs_3_), channel_id=1, source_target_pairs={{0,8},{4,28},{8,16},{12,4},{16,24},{20,12},{24,0},{28,20},{1,9},{5... | collective-permute-start | bytes 786440 | tf_op jit(solution)/shard_map/ppermute | solution.py:23
  19.1 0.0 copy-done.1
  19.1 0.1 multiply_convert_fusion.left.after
  19.2 2.5 %collective-permute-done.near.refs_6_ = bf16[256,512]{1,0:T(8,128)(2,1)S(1)} collective-permute-done((bf16[256,512]{1,0:T(8,128)(2,1)S(1)}, bf16[256,512]{1,0:T(8,128)(2,1)S(1)}, u32[]{:S(2)}, u32[]{:S(2)}) %collective-permute-start) | collective-permute-done | bytes 262176 | tf_op jit(solution)/shard_map/ppermute | solution.py:23
  21.8 1.8 %collective-permute-start.10 = (bf16[256,512]{1,0:T(8,128)(2,1)S(1)}, bf16[256,512]{1,0:T(8,128)(2,1)S(1)}, u32[]{:S(2)}, u32[]{:S(2)}) collective-permute-start(bf16[256,512]{1,0:T(8,128)(2,1)S(1)} %collective-permute-done.near.refs_6_), channel_id=1, source_target_pairs={{0,8},{4,28},{8,16},{12,4},{16,24},{20,12},{24,0},{28,20},{1,9},{5... | collective-permute-start | bytes 786440 | tf_op jit(solution)/shard_map/ppermute | solution.py:23
  23.6 0.0 collective-permute-done.2.far.refs_4_
  23.6 0.3 end_blocks.1
  23.9 3.6 %collective-permute-start.3 = (bf16[3,128,128]{2,1,0:T(8,128)(2,1)S(1)}, bf16[3,128,128]{2,1,0:T(8,128)(2,1)S(1)}, u32[]{:S(2)}, u32[]{:S(2)}) collective-permute-start(bf16[3,128,128]{2,1,0:T(8,128)(2,1)S(1)} %end_blocks.1), channel_id=1, source_target_pairs={{0,4},{4,0},{8,12},{12,8},{16,20},{20,16},{24,28},{28,24},{1,5},{5... | collective-permute-start | bytes 294920 | tf_op jit(solution)/shard_map/ppermute | solution.py:23
  27.5 0.0 collective-permute-done.4.refs_2_
  27.5 0.0 collective-permute-done.6.refs_5_
  27.5 1.9 %pieces_blocks.1.refs_0_ = bf16[6,22,128,128]{3,2,1,0:T(8,128)(2,1)S(1)} custom-call(bf16[768,512]{1,0:T(8,128)(2,1)S(1)} %multiply_convert_fusion.left.after, bf16[768,512]{1,0:T(8,128)(2,1)S(1)} %copy-done.1, bf16[256,512]{1,0:T(8,128)(2,1)S(1)} %collective-permute-done.1.refs_1_, bf16[256,512]{1,0:T(8,128)(2,1)S(1)} %collective-permute-done.4.refs_2_, ...), custom_call_target="tpu_custom_call" | custom-call | flops 20000000000 | bytes 1 | tf_op jit(solution)/shard_map/pieces_blocks/pallas_call | solution.py:62
  29.3 0.7 %collective-permute-done.3.from_partner = bf16[3,128,128]{2,1,0:T(8,128)(2,1)S(1)} collective-permute-done((bf16[3,128,128]{2,1,0:T(8,128)(2,1)S(1)}, bf16[3,128,128]{2,1,0:T(8,128)(2,1)S(1)}, u32[]{:S(2)}, u32[]{:S(2)}) %collective-permute-start.3) | collective-permute-done | bytes 98336 | tf_op jit(solution)/shard_map/ppermute | solution.py:23
  30.1 0.7 %choose_blocks.2 = (bf16[6,22,128,128]{3,2,1,0:T(8,128)(2,1)S(1)}, bf16[2,3,128,128]{3,2,1,0:T(8,128)(2,1)S(1)}, bf16[2,3,128,128]{3,2,1,0:T(8,128)(2,1)S(1)}, b...) custom-call(s32[6,12]{1,0:T(8,128)S(1)} %add_select_fusion.all_places, ...), custom_call_target="tpu_custom_call", output_to_operand_aliasing={{0}: (4, {})} | custom-call | flops 1 | bytes 1 | tf_op jit(solution)/shard_map/choose_blocks/pallas_call | solution.py:120
  30.7 0.1 collective-permute-start.8
  30.8 0.6 %collective-permute-done.10.refs_0_ = bf16[256,512]{1,0:T(8,128)(2,1)S(1)} collective-permute-done((bf16[256,512]{1,0:T(8,128)(2,1)S(1)}, bf16[256,512]{1,0:T(8,128)(2,1)S(1)}, u32[]{:S(2)}, u32[]{:S(2)}) %collective-permute-start.10) | collective-permute-done | bytes 262176 | tf_op jit(solution)/shard_map/ppermute | solution.py:23
  31.4 0.8 %collective-permute-done.8.y.after = bf16[2,3,128,128]{3,2,1,0:T(8,128)(2,1)S(1)} collective-permute-done((bf16[2,3,128,128]{3,2,1,0:T(8,128)(2,1)S(1)}, bf16[2,3,128,128]{3,2,1,0:T(8,128)(2,1)S(1)}, u32[]{:S(2)}, u32[]{:S(2)}) %collective-permute-start.8) | collective-permute-done | bytes 196640 | tf_op jit(solution)/shard_map/ppermute | solution.py:23
  32.2 0.7 %choose_blocks.3 = (bf16[6,22,128,128]{3,2,1,0:T(8,128)(2,1)S(1)}, bf16[4,3,128,128]{3,2,1,0:T(8,128)(2,1)S(1)}, bf16[4,3,128,128]{3,2,1,0:T(8,128)(2,1)S(1)}, b...) custom-call(s32[6,12]{1,0:T(8,128)S(1)} %add_select_fusion.all_places, ...), custom_call_target="tpu_custom_call", output_to_operand_aliasing={{0}: (5, {})} | custom-call | flops 1 | bytes 1 | tf_op jit(solution)/shard_map/choose_blocks/pallas_call | solution.py:120
  33.0 0.2 collective-permute-start.12
  33.2 0.4 collective-permute-start.7
  33.6 1.6 %collective-permute-start.9 = (bf16[2,3,128,128]{3,2,1,0:T(8,128)(2,1)S(1)}, bf16[2,3,128,128]{3,2,1,0:T(8,128)(2,1)S(1)}, u32[]{:S(2)}, u32[]{:S(2)}) collective-permute-start(bf16[2,3,128,128]{3,2,1,0:T(8,128)(2,1)S(1)} %add.11), channel_id=1, source_target_pairs={{0,2},{1,3},{2,0},{3,1},{4,6},{5,7},{6,4},{7,5},{8,10},{9,11},{10,... | collective-permute-start | bytes 589832 | tf_op jit(solution)/shard_map/ppermute | solution.py:23
  35.2 0.0 collective-permute-start.11
  35.2 0.0 collective-permute-done.12.y
  35.2 0.1 add.12
  35.3 1.2 %collective-permute-start.13 = (bf16[4,3,128,128]{3,2,1,0:T(8,128)(2,1)S(1)}, bf16[4,3,128,128]{3,2,1,0:T(8,128)(2,1)S(1)}, u32[]{:S(2)}, u32[]{:S(2)}) collective-permute-start(bf16[4,3,128,128]{3,2,1,0:T(8,128)(2,1)S(1)} %add.12), channel_id=1, source_target_pairs={{0,2},{1,3},{2,0},{3,1},{4,6},{5,7},{6,4},{7,5},{8,10},{9,11},{10,... | collective-permute-start | bytes 1179656 | tf_op jit(solution)/shard_map/ppermute | solution.py:23
  36.4 0.0 collective-permute-done.7.got_near
  36.4 5.0 %collective-permute-done.9.got = bf16[2,3,128,128]{3,2,1,0:T(8,128)(2,1)S(1)} collective-permute-done((bf16[2,3,128,128]{3,2,1,0:T(8,128)(2,1)S(1)}, bf16[2,3,128,128]{3,2,1,0:T(8,128)(2,1)S(1)}, u32[]{:S(2)}, u32[]{:S(2)}) %collective-permute-start.9) | collective-permute-done | bytes 196640 | tf_op jit(solution)/shard_map/ppermute | solution.py:23
  41.4 0.1 total.1.early
  41.5 0.0 collective-permute-done.11.got_near
  41.5 7.5 %collective-permute-done.13.got = bf16[4,3,128,128]{3,2,1,0:T(8,128)(2,1)S(1)} collective-permute-done((bf16[4,3,128,128]{3,2,1,0:T(8,128)(2,1)S(1)}, bf16[4,3,128,128]{3,2,1,0:T(8,128)(2,1)S(1)}, u32[]{:S(2)}, u32[]{:S(2)}) %collective-permute-start.13) | collective-permute-done | bytes 393248 | tf_op jit(solution)/shard_map/ppermute | solution.py:23
  49.0 0.9 %finish.1 = bf16[6,3,128,128]{3,2,1,0:T(8,128)(2,1)} custom-call(bf16[2,3,128,128]{3,2,1,0:T(8,128)(2,1)S(1)} %total.1.early, bf16[4,3,128,128]{3,2,1,0:T(8,128)(2,1)S(1)} %get-tuple-element.19.near, bf16[4,3,128,128]{3,2,1,0:T(8,128)(2,1)S(1)} %collective-permute-done.11.got_near, bf16[4,3,128,128]{3,2,1,0:T(8,128)(2,1)S(1)} %collective-permute-done.13.got), custom_call_target="tpu_custom_call" | custom-call | flops 1 | bytes 1 | tf_op jit(solution)/shard_map/finish/pallas_call | solution.py:182
  (7 shorter events, 0.2 us)
Async XLA Ops:
  0.0 11.4 %copy-start.2 = (s32[6,12]{1,0:T(8,128)S(1)}, s32[6,12]{1,0:T(8,128)}, u32[]{:S(2)}) copy-start(s32[6,12]{1,0:T(8,128)} %param.7) | copy-start | bytes 868
  0.0 1.1 %copy-start = (bf16[768,512]{1,0:T(8,128)(2,1)S(1)}, bf16[768,512]{1,0:T(8,128)(2,1)}, u32[]{:S(2)}) copy-start(bf16[768,512]{1,0:T(8,128)(2,1)} %refs_0_.1) | copy-start | bytes 2359300
  1.1 9.0 %copy-start.3 = (f32[4096]{0:T(1024)S(1)}, f32[4096]{0:T(1024)}, u32[]{:S(2)}) copy-start(f32[4096]{0:T(1024)} %param.5) | copy-start | bytes 49156
  1.2 9.0 %copy-start.4 = (s32[512]{0:T(512)S(1)}, s32[512]{0:T(512)}, u32[]{:S(2)}) copy-start(s32[512]{0:T(512)} %param.6) | copy-start | bytes 6148
  1.2 17.9 %copy-start.1 = (bf16[768,512]{1,0:T(8,128)(2,1)S(1)}, bf16[768,512]{1,0:T(8,128)(2,1)}, u32[]{:S(2)}) copy-start(bf16[768,512]{1,0:T(8,128)(2,1)} %refs_0_.1) | copy-start | bytes 2359300
  1.2 10.2 %collective-permute-start.1 = (bf16[256,512]{1,0:T(8,128)(2,1)S(1)}, bf16[256,512]{1,0:T(8,128)(2,1)S(1)}, u32[]{:S(2)}, u32[]{:S(2)}) collective-permute-start(bf16[256,512]{1,0:T(8,128)(2,1)S(1)} %take_end.1), channel_id=1, source_target_pairs={{0,4},{4,0},{8,12},{12,8},{16,20},{20,16},{24,28},{28,24},{1,5},{5... | collective-permute-start | bytes 786440 | tf_op jit(solution)/shard_map/ppermute | solution.py:23
  4.3 12.7 %collective-permute-start.5 = (bf16[256,512]{1,0:T(8,128)(2,1)S(1)}, bf16[256,512]{1,0:T(8,128)(2,1)S(1)}, u32[]{:S(2)}, u32[]{:S(2)}) collective-permute-start(bf16[256,512]{1,0:T(8,128)(2,1)S(1)} %take_middle.1), channel_id=1, source_target_pairs={{0,4},{4,0},{8,12},{12,8},{16,20},{20,16},{24,28},{28,24},{1,5},{5... | collective-permute-start | bytes 786440 | tf_op jit(solution)/shard_map/ppermute | solution.py:23
  4.4 23.1 %collective-permute-start.4 = (bf16[256,512]{1,0:T(8,128)(2,1)S(1)}, bf16[256,512]{1,0:T(8,128)(2,1)S(1)}, u32[]{:S(2)}, u32[]{:S(2)}) collective-permute-start(bf16[256,512]{1,0:T(8,128)(2,1)S(1)} %take_near.2.after), channel_id=1, source_target_pairs={{0,8},{4,28},{8,16},{12,4},{16,24},{20,12},{24,0},{28,20},{1,9},{5... | collective-permute-start | bytes 786440 | tf_op jit(solution)/shard_map/ppermute | solution.py:23
  6.5 15.2 %collective-permute-start = (bf16[256,512]{1,0:T(8,128)(2,1)S(1)}, bf16[256,512]{1,0:T(8,128)(2,1)S(1)}, u32[]{:S(2)}, u32[]{:S(2)}) collective-permute-start(bf16[256,512]{1,0:T(8,128)(2,1)S(1)} %take_near.3), channel_id=1, source_target_pairs={{0,4},{4,0},{8,12},{12,8},{16,20},{20,16},{24,28},{28,24},{1,5},{5... | collective-permute-start | bytes 786440 | tf_op jit(solution)/shard_map/ppermute | solution.py:23
  11.4 12.2 %collective-permute-start.2 = (bf16[256,512]{1,0:T(8,128)(2,1)S(1)}, bf16[256,512]{1,0:T(8,128)(2,1)S(1)}, u32[]{:S(2)}, u32[]{:S(2)}) collective-permute-start(bf16[256,512]{1,0:T(8,128)(2,1)S(1)} %collective-permute-done.1.refs_1_), channel_id=1, source_target_pairs={{0,8},{4,28},{8,16},{12,4},{16,24},{20,12},{24,0},{28,20},{1,9},{5... | collective-permute-start | bytes 786440 | tf_op jit(solution)/shard_map/ppermute | solution.py:23
  17.0 10.5 %collective-permute-start.6 = (bf16[256,512]{1,0:T(8,128)(2,1)S(1)}, bf16[256,512]{1,0:T(8,128)(2,1)S(1)}, u32[]{:S(2)}, u32[]{:S(2)}) collective-permute-start(bf16[256,512]{1,0:T(8,128)(2,1)S(1)} %collective-permute-done.5.refs_3_), channel_id=1, source_target_pairs={{0,8},{4,28},{8,16},{12,4},{16,24},{20,12},{24,0},{28,20},{1,9},{5... | collective-permute-start | bytes 786440 | tf_op jit(solution)/shard_map/ppermute | solution.py:23
  21.8 9.7 %collective-permute-start.10 = (bf16[256,512]{1,0:T(8,128)(2,1)S(1)}, bf16[256,512]{1,0:T(8,128)(2,1)S(1)}, u32[]{:S(2)}, u32[]{:S(2)}) collective-permute-start(bf16[256,512]{1,0:T(8,128)(2,1)S(1)} %collective-permute-done.near.refs_6_), channel_id=1, source_target_pairs={{0,8},{4,28},{8,16},{12,4},{16,24},{20,12},{24,0},{28,20},{1,9},{5... | collective-permute-start | bytes 786440 | tf_op jit(solution)/shard_map/ppermute | solution.py:23
  23.9 6.2 %collective-permute-start.3 = (bf16[3,128,128]{2,1,0:T(8,128)(2,1)S(1)}, bf16[3,128,128]{2,1,0:T(8,128)(2,1)S(1)}, u32[]{:S(2)}, u32[]{:S(2)}) collective-permute-start(bf16[3,128,128]{2,1,0:T(8,128)(2,1)S(1)} %end_blocks.1), channel_id=1, source_target_pairs={{0,4},{4,0},{8,12},{12,8},{16,20},{20,16},{24,28},{28,24},{1,5},{5... | collective-permute-start | bytes 294920 | tf_op jit(solution)/shard_map/ppermute | solution.py:23
  30.7 1.5 %collective-permute-start.8 = (bf16[2,3,128,128]{3,2,1,0:T(8,128)(2,1)S(1)}, bf16[2,3,128,128]{3,2,1,0:T(8,128)(2,1)S(1)}, u32[]{:S(2)}, u32[]{:S(2)}) collective-permute-start(bf16[2,3,128,128]{3,2,1,0:T(8,128)(2,1)S(1)} %get-tuple-element.17), channel_id=1, source_target_pairs={{0,1},{1,0},{2,3},{3,2},{4,5},{5,4},{6,7},{7,6},{8,9},{9,8},{10,11... | collective-permute-start | bytes 589832 | tf_op jit(solution)/shard_map/ppermute | solution.py:23
  33.0 2.2 %collective-permute-start.12 = (bf16[4,3,128,128]{3,2,1,0:T(8,128)(2,1)S(1)}, bf16[4,3,128,128]{3,2,1,0:T(8,128)(2,1)S(1)}, u32[]{:S(2)}, u32[]{:S(2)}) collective-permute-start(bf16[4,3,128,128]{3,2,1,0:T(8,128)(2,1)S(1)} %get-tuple-element.22), channel_id=1, source_target_pairs={{0,1},{1,0},{2,3},{3,2},{4,5},{5,4},{6,7},{7,6},{8,9},{9,8},{10,11... | collective-permute-start | bytes 1179656 | tf_op jit(solution)/shard_map/ppermute | solution.py:23
  33.2 3.2 %collective-permute-start.7 = (bf16[2,3,128,128]{3,2,1,0:T(8,128)(2,1)S(1)}, bf16[2,3,128,128]{3,2,1,0:T(8,128)(2,1)S(1)}, u32[]{:S(2)}, u32[]{:S(2)}) collective-permute-start(bf16[2,3,128,128]{3,2,1,0:T(8,128)(2,1)S(1)} %get-tuple-element.15), channel_id=1, source_target_pairs={{0,1},{1,0},{2,3},{3,2},{4,5},{5,4},{6,7},{7,6},{8,9},{9,8},{10,11... | collective-permute-start | bytes 589832 | tf_op jit(solution)/shard_map/ppermute | solution.py:23
  33.6 7.8 %collective-permute-start.9 = (bf16[2,3,128,128]{3,2,1,0:T(8,128)(2,1)S(1)}, bf16[2,3,128,128]{3,2,1,0:T(8,128)(2,1)S(1)}, u32[]{:S(2)}, u32[]{:S(2)}) collective-permute-start(bf16[2,3,128,128]{3,2,1,0:T(8,128)(2,1)S(1)} %add.11), channel_id=1, source_target_pairs={{0,2},{1,3},{2,0},{3,1},{4,6},{5,7},{6,4},{7,5},{8,10},{9,11},{10,... | collective-permute-start | bytes 589832 | tf_op jit(solution)/shard_map/ppermute | solution.py:23
  35.2 6.3 %collective-permute-start.11 = (bf16[4,3,128,128]{3,2,1,0:T(8,128)(2,1)S(1)}, bf16[4,3,128,128]{3,2,1,0:T(8,128)(2,1)S(1)}, u32[]{:S(2)}, u32[]{:S(2)}) collective-permute-start(bf16[4,3,128,128]{3,2,1,0:T(8,128)(2,1)S(1)} %get-tuple-element.20), channel_id=1, source_target_pairs={{0,1},{1,0},{2,3},{3,2},{4,5},{5,4},{6,7},{7,6},{8,9},{9,8},{10,11... | collective-permute-start | bytes 1179656 | tf_op jit(solution)/shard_map/ppermute | solution.py:23
  35.3 13.8 %collective-permute-start.13 = (bf16[4,3,128,128]{3,2,1,0:T(8,128)(2,1)S(1)}, bf16[4,3,128,128]{3,2,1,0:T(8,128)(2,1)S(1)}, u32[]{:S(2)}, u32[]{:S(2)}) collective-permute-start(bf16[4,3,128,128]{3,2,1,0:T(8,128)(2,1)S(1)} %add.12), channel_id=1, source_target_pairs={{0,2},{1,3},{2,0},{3,1},{4,6},{5,7},{6,4},{7,5},{8,10},{9,11},{10,... | collective-permute-start | bytes 1179656 | tf_op jit(solution)/shard_map/ppermute | solution.py:23

commit v9 on v8

--- a/solution.py
+++ b/solution.py
@@ -146,49 +146,52 @@
     )(x, y)
 
 
-def total_kernel(near, got_near, got, out):
-    total = near[...].astype(jnp.float32) + got_near[...].astype(jnp.float32) + got[...].astype(jnp.float32)
-    out[...] = total.astype(jnp.bfloat16)
-
-
-def total(near, got_near, got):
+def total_kernel(near, got, out):
+    out[...] = near[...].astype(jnp.float32) + got[...].astype(jnp.float32)
+
+
+def total(near, got):
     return pl.pallas_call(
         total_kernel,
-        out_shape=jax.ShapeDtypeStruct(near.shape, near.dtype),
-        in_specs=[VMEM] * 3,
+        out_shape=jax.ShapeDtypeStruct(near.shape, jnp.float32),
+        in_specs=[VMEM] * 2,
         out_specs=VMEM,
         compiler_params=pltpu.CompilerParams(vmem_limit_bytes=LIMIT),
         cost_estimate=LONG,
         name="total",
-    )(near, got_near, got)
-
-
-def finish_kernel(chunks, early, near, got_near, got, out, rows, done):
-    start, later = [natural(first, last) for first, last in chunks]
+    )(near, got)
+
+
+def finish_kernel(chunks, early, got_early, near, got_near, got, out, rows, done):
     copies = []
+
+    def write(chunk, r, total):
+        at = len(copies)
+        rows[at] = total.astype(jnp.bfloat16)
+        copies.append(pltpu.make_async_copy(rows.at[at], out.at[natural(*chunk) + r], done.at[at]))
+        copies[-1].start()
+
     for r in range(early.shape[0]):
-        copies.append(pltpu.make_async_copy(early.at[r], out.at[start + r], done.at[r]))
-        copies[-1].start()
+        write(chunks[0], r, early[r] + got_early[r].astype(jnp.float32))
     for r in range(near.shape[0]):
         total = near[r].astype(jnp.float32) + got_near[r].astype(jnp.float32) + got[r].astype(jnp.float32)
-        rows[r] = total.astype(jnp.bfloat16)
-        copies.append(pltpu.make_async_copy(rows.at[r], out.at[later + r], done.at[early.shape[0] + r]))
-        copies[-1].start()
+        write(chunks[1], r, total)
     for copy in copies:
         copy.wait()
 
 
-def finish(chunks, early, near, got_near, got):
+def finish(chunks, early, got_early, near, got_near, got):
+    shape = (CL,) + near.shape[1:]
     return pl.pallas_call(
         functools.partial(finish_kernel, chunks),
-        out_shape=jax.ShapeDtypeStruct((CL,) + near.shape[1:], near.dtype),
-        in_specs=[VMEM] * 4,
+        out_shape=jax.ShapeDtypeStruct(shape, near.dtype),
+        in_specs=[VMEM] * 5,
         out_specs=pl.BlockSpec(memory_space=pl.ANY),
-        scratch_shapes=[pltpu.VMEM(near.shape, near.dtype), pltpu.SemaphoreType.DMA((CL,))],
+        scratch_shapes=[pltpu.VMEM(shape, near.dtype), pltpu.SemaphoreType.DMA((CL,))],
         compiler_params=pltpu.CompilerParams(vmem_limit_bytes=LIMIT),
         cost_estimate=SHORT,
         name="finish",
-    )(early, near, got_near, got)
+    )(early, got_early, near, got_near, got)
 
 
 def take_kernel(which, slab, after, out, done):
@@ -253,7 +256,8 @@
         got_near = move(send_near, "narrow", lambda n: n ^ 1)
         parts.append((keep_near, got_near, got))
         after = got_far
-    return finish(chunks, total(*parts[0]), *parts[1])
+    (near, got_near, got), later = parts
+    return finish(chunks, total(near, got), got_near, *later)
 
 
 def solution(mesh):

time: 50 us -> 49.9 us (level)
  no operation moved by 1% of the time
where the time goes in v9:
time: 49.9 us; the launch traced here: 49.8 us
  starting transfers between devices  21.8 us (44%)
  waiting for transfers between devices  20.6 us (41%)
  Pallas kernels  4.71 us (9%)
  other arithmetic  1.37 us (3%)
  local copies, waits for them, and re-layouts  1.16 us (2%)
    ppermute x14, starting transfers between devices, move(): lax.ppermute(value, axis, [(s, target(s) % count) for s in range(count)])  21.8 us
    ppermute x14, waiting for transfers between devices, move(): lax.ppermute(value, axis, [(s, target(s) % count) for s in range(count)])  20.6 us
    pallas_call x1, Pallas kernels, pieces_blocks(): pl.pallas_call(functools.partial(pieces_kernel, list(pieces)), out_shape=...  1.85 us
    pallas_call x2, Pallas kernels, choose_blocks(): pl.pallas_call(functools.partial(choose_kernel, share, list(pieces), chun...  1.4 us
    reduce_sum x1, other arithmetic, per_device(): jnp.sum(jnp.where(picks, occupation[None, :], jnp.float32(0.0)), axis=1)  1.22 us
    unnamed x10, local copies, waits for them, and re-layouts  1.16 us
  transfers between devices with their start and end apart: 14, of which 7 were waited for; matrix products, arithmetic and copies ran while one was open for 3% of the time, Pallas kernels for 6%

profile of v9, /device:TPU:0, one launch (start us, length us, event | category | flops | bytes accessed | tf_op | source)
XLA Modules:
  0.0 49.8 jit_solution(1522380128400938729)
XLA Ops:
  0.0 0.0 copy-start.2
  0.0 0.0 copy-start
  0.0 1.1 %copy-done = bf16[768,512]{1,0:T(8,128)(2,1)S(1)} copy-done((bf16[768,512]{1,0:T(8,128)(2,1)S(1)}, bf16[768,512]{1,0:T(8,128)(2,1)}, u32[]{:S(2)}) %copy-start) | copy-done | bytes 786456
  1.1 0.0 copy-start.3
  1.2 0.0 copy-start.4
  1.2 0.0 copy-start.1
  1.2 3.0 %collective-permute-start.1 = (bf16[256,512]{1,0:T(8,128)(2,1)S(1)}, bf16[256,512]{1,0:T(8,128)(2,1)S(1)}, u32[]{:S(2)}, u32[]{:S(2)}) collective-permute-start(bf16[256,512]{1,0:T(8,128)(2,1)S(1)} %take_end.1), channel_id=1, source_target_pairs={{0,4},{4,0},{8,12},{12,8},{16,20},{20,16},{24,28},{28,24},{1,5},{5... | collective-permute-start | bytes 786440 | tf_op jit(solution)/shard_map/ppermute | solution.py:23
  4.3 0.1 collective-permute-start.5
  4.4 2.1 %collective-permute-start.4 = (bf16[256,512]{1,0:T(8,128)(2,1)S(1)}, bf16[256,512]{1,0:T(8,128)(2,1)S(1)}, u32[]{:S(2)}, u32[]{:S(2)}) collective-permute-start(bf16[256,512]{1,0:T(8,128)(2,1)S(1)} %take_near.2.after), channel_id=1, source_target_pairs={{0,8},{4,28},{8,16},{12,4},{16,24},{20,12},{24,0},{28,20},{1,9},{5... | collective-permute-start | bytes 786440 | tf_op jit(solution)/shard_map/ppermute | solution.py:23
  6.5 3.6 %collective-permute-start = (bf16[256,512]{1,0:T(8,128)(2,1)S(1)}, bf16[256,512]{1,0:T(8,128)(2,1)S(1)}, u32[]{:S(2)}, u32[]{:S(2)}) collective-permute-start(bf16[256,512]{1,0:T(8,128)(2,1)S(1)} %take_near.3), channel_id=1, source_target_pairs={{0,4},{4,0},{8,12},{12,8},{16,20},{20,16},{24,28},{28,24},{1,5},{5... | collective-permute-start | bytes 786440 | tf_op jit(solution)/shard_map/ppermute | solution.py:23
  10.1 0.0 copy-done.3
  10.1 0.0 copy-done.4
  10.2 1.2 %select_reduce_fusion = f32[512]{0:T(512)S(1)} fusion(f32[4096]{0:T(1024)S(1)} %copy-done.3, s32[512]{0:T(512)S(1)} %copy-done.4), kind=kLoop, calls=%fused_computation | loop fusion | flops 6290944 | bytes 20480 | tf_op jit(solution)/shard_map/reduce_sum | solution.py:227
  11.4 0.0 copy-done.2
  11.4 0.0 collective-permute-done.1.refs_1_
  11.4 2.1 %collective-permute-start.2 = (bf16[256,512]{1,0:T(8,128)(2,1)S(1)}, bf16[256,512]{1,0:T(8,128)(2,1)S(1)}, u32[]{:S(2)}, u32[]{:S(2)}) collective-permute-start(bf16[256,512]{1,0:T(8,128)(2,1)S(1)} %collective-permute-done.1.refs_1_), channel_id=1, source_target_pairs={{0,8},{4,28},{8,16},{12,4},{16,24},{20,12},{24,0},{28,20},{1,9},{5... | collective-permute-start | bytes 786440 | tf_op jit(solution)/shard_map/ppermute | solution.py:23
  13.5 3.5 %collective-permute-done.5.refs_3_ = bf16[256,512]{1,0:T(8,128)(2,1)S(1)} collective-permute-done((bf16[256,512]{1,0:T(8,128)(2,1)S(1)}, bf16[256,512]{1,0:T(8,128)(2,1)S(1)}, u32[]{:S(2)}, u32[]{:S(2)}) %collective-permute-start.5) | collective-permute-done | bytes 262176 | tf_op jit(solution)/shard_map/ppermute | solution.py:23
  17.0 2.1 %collective-permute-start.6 = (bf16[256,512]{1,0:T(8,128)(2,1)S(1)}, bf16[256,512]{1,0:T(8,128)(2,1)S(1)}, u32[]{:S(2)}, u32[]{:S(2)}) collective-permute-start(bf16[256,512]{1,0:T(8,128)(2,1)S(1)} %collective-permute-done.5.refs_3_), channel_id=1, source_target_pairs={{0,8},{4,28},{8,16},{12,4},{16,24},{20,12},{24,0},{28,20},{1,9},{5... | collective-permute-start | bytes 786440 | tf_op jit(solution)/shard_map/ppermute | solution.py:23
  19.1 0.0 copy-done.1
  19.1 0.1 multiply_convert_fusion.left.after
  19.2 2.5 %collective-permute-done.near.refs_6_ = bf16[256,512]{1,0:T(8,128)(2,1)S(1)} collective-permute-done((bf16[256,512]{1,0:T(8,128)(2,1)S(1)}, bf16[256,512]{1,0:T(8,128)(2,1)S(1)}, u32[]{:S(2)}, u32[]{:S(2)}) %collective-permute-start) | collective-permute-done | bytes 262176 | tf_op jit(solution)/shard_map/ppermute | solution.py:23
  21.8 1.8 %collective-permute-start.10 = (bf16[256,512]{1,0:T(8,128)(2,1)S(1)}, bf16[256,512]{1,0:T(8,128)(2,1)S(1)}, u32[]{:S(2)}, u32[]{:S(2)}) collective-permute-start(bf16[256,512]{1,0:T(8,128)(2,1)S(1)} %collective-permute-done.near.refs_6_), channel_id=1, source_target_pairs={{0,8},{4,28},{8,16},{12,4},{16,24},{20,12},{24,0},{28,20},{1,9},{5... | collective-permute-start | bytes 786440 | tf_op jit(solution)/shard_map/ppermute | solution.py:23
  23.6 0.0 collective-permute-done.2.far.refs_4_
  23.6 0.3 end_blocks.1
  23.9 3.6 %collective-permute-start.3 = (bf16[3,128,128]{2,1,0:T(8,128)(2,1)S(1)}, bf16[3,128,128]{2,1,0:T(8,128)(2,1)S(1)}, u32[]{:S(2)}, u32[]{:S(2)}) collective-permute-start(bf16[3,128,128]{2,1,0:T(8,128)(2,1)S(1)} %end_blocks.1), channel_id=1, source_target_pairs={{0,4},{4,0},{8,12},{12,8},{16,20},{20,16},{24,28},{28,24},{1,5},{5... | collective-permute-start | bytes 294920 | tf_op jit(solution)/shard_map/ppermute | solution.py:23
  27.5 0.0 collective-permute-done.4.refs_2_
  27.5 0.0 collective-permute-done.6.refs_5_
  27.5 1.9 %pieces_blocks.1.refs_0_ = bf16[6,22,128,128]{3,2,1,0:T(8,128)(2,1)S(1)} custom-call(bf16[768,512]{1,0:T(8,128)(2,1)S(1)} %multiply_convert_fusion.left.after, bf16[768,512]{1,0:T(8,128)(2,1)S(1)} %copy-done.1, bf16[256,512]{1,0:T(8,128)(2,1)S(1)} %collective-permute-done.1.refs_1_, bf16[256,512]{1,0:T(8,128)(2,1)S(1)} %collective-permute-done.4.refs_2_, ...), custom_call_target="tpu_custom_call" | custom-call | flops 20000000000 | bytes 1 | tf_op jit(solution)/shard_map/pieces_blocks/pallas_call | solution.py:62
  29.3 0.7 %collective-permute-done.3.from_partner = bf16[3,128,128]{2,1,0:T(8,128)(2,1)S(1)} collective-permute-done((bf16[3,128,128]{2,1,0:T(8,128)(2,1)S(1)}, bf16[3,128,128]{2,1,0:T(8,128)(2,1)S(1)}, u32[]{:S(2)}, u32[]{:S(2)}) %collective-permute-start.3) | collective-permute-done | bytes 98336 | tf_op jit(solution)/shard_map/ppermute | solution.py:23
  30.1 0.7 %choose_blocks.2 = (bf16[6,22,128,128]{3,2,1,0:T(8,128)(2,1)S(1)}, bf16[2,3,128,128]{3,2,1,0:T(8,128)(2,1)S(1)}, bf16[2,3,128,128]{3,2,1,0:T(8,128)(2,1)S(1)}, b...) custom-call(s32[6,12]{1,0:T(8,128)S(1)} %add_select_fusion.all_places, ...), custom_call_target="tpu_custom_call", output_to_operand_aliasing={{0}: (4, {})} | custom-call | flops 1 | bytes 1 | tf_op jit(solution)/shard_map/choose_blocks/pallas_call | solution.py:120
  30.7 0.1 collective-permute-start.7
  30.8 0.6 %collective-permute-done.10.refs_0_ = bf16[256,512]{1,0:T(8,128)(2,1)S(1)} collective-permute-done((bf16[256,512]{1,0:T(8,128)(2,1)S(1)}, bf16[256,512]{1,0:T(8,128)(2,1)S(1)}, u32[]{:S(2)}, u32[]{:S(2)}) %collective-permute-start.10) | collective-permute-done | bytes 262176 | tf_op jit(solution)/shard_map/ppermute | solution.py:23
  31.4 0.8 %collective-permute-done.7.y.after = bf16[2,3,128,128]{3,2,1,0:T(8,128)(2,1)S(1)} collective-permute-done((bf16[2,3,128,128]{3,2,1,0:T(8,128)(2,1)S(1)}, bf16[2,3,128,128]{3,2,1,0:T(8,128)(2,1)S(1)}, u32[]{:S(2)}, u32[]{:S(2)}) %collective-permute-start.7) | collective-permute-done | bytes 196640 | tf_op jit(solution)/shard_map/ppermute | solution.py:23
  32.2 0.7 %choose_blocks.3 = (bf16[6,22,128,128]{3,2,1,0:T(8,128)(2,1)S(1)}, bf16[4,3,128,128]{3,2,1,0:T(8,128)(2,1)S(1)}, bf16[4,3,128,128]{3,2,1,0:T(8,128)(2,1)S(1)}, b...) custom-call(s32[6,12]{1,0:T(8,128)S(1)} %add_select_fusion.all_places, ...), custom_call_target="tpu_custom_call", output_to_operand_aliasing={{0}: (5, {})} | custom-call | flops 1 | bytes 1 | tf_op jit(solution)/shard_map/choose_blocks/pallas_call | solution.py:120
  33.0 0.2 collective-permute-start.12
  33.2 1.6 %collective-permute-start.8 = (bf16[2,3,128,128]{3,2,1,0:T(8,128)(2,1)S(1)}, bf16[2,3,128,128]{3,2,1,0:T(8,128)(2,1)S(1)}, u32[]{:S(2)}, u32[]{:S(2)}) collective-permute-start(bf16[2,3,128,128]{3,2,1,0:T(8,128)(2,1)S(1)} %add.11), channel_id=1, source_target_pairs={{0,2},{1,3},{2,0},{3,1},{4,6},{5,7},{6,4},{7,5},{8,10},{9,11},{10,... | collective-permute-start | bytes 589832 | tf_op jit(solution)/shard_map/ppermute | solution.py:23
  34.8 0.1 collective-permute-start.9
  34.9 0.4 collective-permute-start.11
  35.3 0.0 collective-permute-done.12.y
  35.3 0.1 add.12
  35.4 1.0 %collective-permute-start.13 = (bf16[4,3,128,128]{3,2,1,0:T(8,128)(2,1)S(1)}, bf16[4,3,128,128]{3,2,1,0:T(8,128)(2,1)S(1)}, u32[]{:S(2)}, u32[]{:S(2)}) collective-permute-start(bf16[4,3,128,128]{3,2,1,0:T(8,128)(2,1)S(1)} %add.12), channel_id=1, source_target_pairs={{0,2},{1,3},{2,0},{3,1},{4,6},{5,7},{6,4},{7,5},{8,10},{9,11},{10,... | collective-permute-start | bytes 1179656 | tf_op jit(solution)/shard_map/ppermute | solution.py:23
  36.4 4.6 %collective-permute-done.8.got = bf16[2,3,128,128]{3,2,1,0:T(8,128)(2,1)S(1)} collective-permute-done((bf16[2,3,128,128]{3,2,1,0:T(8,128)(2,1)S(1)}, bf16[2,3,128,128]{3,2,1,0:T(8,128)(2,1)S(1)}, u32[]{:S(2)}, u32[]{:S(2)}) %collective-permute-start.8) | collective-permute-done | bytes 196640 | tf_op jit(solution)/shard_map/ppermute | solution.py:23
  41.1 0.0 collective-permute-done.9.got_early
  41.1 0.0 collective-permute-done.11.got_near
  41.1 7.8 %collective-permute-done.13.got = bf16[4,3,128,128]{3,2,1,0:T(8,128)(2,1)S(1)} collective-permute-done((bf16[4,3,128,128]{3,2,1,0:T(8,128)(2,1)S(1)}, bf16[4,3,128,128]{3,2,1,0:T(8,128)(2,1)S(1)}, u32[]{:S(2)}, u32[]{:S(2)}) %collective-permute-start.13) | collective-permute-done | bytes 393248 | tf_op jit(solution)/shard_map/ppermute | solution.py:23
  48.9 0.9 %finish.1 = bf16[6,3,128,128]{3,2,1,0:T(8,128)(2,1)} custom-call(f32[2,3,128,128]{3,2,1,0:T(8,128)S(1)} %total.1.early, bf16[2,3,128,128]{3,2,1,0:T(8,128)(2,1)S(1)} %collective-permute-done.9.got_early, bf16[4,3,128,128]{3,2,1,0:T(8,128)(2,1)S(1)} %get-tuple-element.19.near, bf16[4,3,128,128]{3,2,1,0:T(8,128)(2,1)S(1)} %collective-permute-done.11.got_near, ...), custom_call_target="tpu_custom_call" | custom-call | flops 1 | bytes 1 | tf_op jit(solution)/shard_map/finish/pallas_call | solution.py:185
  (8 shorter events, 0.2 us)
Async XLA Ops:
  0.0 11.4 %copy-start.2 = (s32[6,12]{1,0:T(8,128)S(1)}, s32[6,12]{1,0:T(8,128)}, u32[]{:S(2)}) copy-start(s32[6,12]{1,0:T(8,128)} %param.7) | copy-start | bytes 868
  0.0 1.1 %copy-start = (bf16[768,512]{1,0:T(8,128)(2,1)S(1)}, bf16[768,512]{1,0:T(8,128)(2,1)}, u32[]{:S(2)}) copy-start(bf16[768,512]{1,0:T(8,128)(2,1)} %refs_0_.1) | copy-start | bytes 2359300
  1.1 9.0 %copy-start.3 = (f32[4096]{0:T(1024)S(1)}, f32[4096]{0:T(1024)}, u32[]{:S(2)}) copy-start(f32[4096]{0:T(1024)} %param.5) | copy-start | bytes 49156
  1.2 9.0 %copy-start.4 = (s32[512]{0:T(512)S(1)}, s32[512]{0:T(512)}, u32[]{:S(2)}) copy-start(s32[512]{0:T(512)} %param.6) | copy-start | bytes 6148
  1.2 17.9 %copy-start.1 = (bf16[768,512]{1,0:T(8,128)(2,1)S(1)}, bf16[768,512]{1,0:T(8,128)(2,1)}, u32[]{:S(2)}) copy-start(bf16[768,512]{1,0:T(8,128)(2,1)} %refs_0_.1) | copy-start | bytes 2359300
  1.2 10.2 %collective-permute-start.1 = (bf16[256,512]{1,0:T(8,128)(2,1)S(1)}, bf16[256,512]{1,0:T(8,128)(2,1)S(1)}, u32[]{:S(2)}, u32[]{:S(2)}) collective-permute-start(bf16[256,512]{1,0:T(8,128)(2,1)S(1)} %take_end.1), channel_id=1, source_target_pairs={{0,4},{4,0},{8,12},{12,8},{16,20},{20,16},{24,28},{28,24},{1,5},{5... | collective-permute-start | bytes 786440 | tf_op jit(solution)/shard_map/ppermute | solution.py:23
  4.3 12.7 %collective-permute-start.5 = (bf16[256,512]{1,0:T(8,128)(2,1)S(1)}, bf16[256,512]{1,0:T(8,128)(2,1)S(1)}, u32[]{:S(2)}, u32[]{:S(2)}) collective-permute-start(bf16[256,512]{1,0:T(8,128)(2,1)S(1)} %take_middle.1), channel_id=1, source_target_pairs={{0,4},{4,0},{8,12},{12,8},{16,20},{20,16},{24,28},{28,24},{1,5},{5... | collective-permute-start | bytes 786440 | tf_op jit(solution)/shard_map/ppermute | solution.py:23
  4.4 23.1 %collective-permute-start.4 = (bf16[256,512]{1,0:T(8,128)(2,1)S(1)}, bf16[256,512]{1,0:T(8,128)(2,1)S(1)}, u32[]{:S(2)}, u32[]{:S(2)}) collective-permute-start(bf16[256,512]{1,0:T(8,128)(2,1)S(1)} %take_near.2.after), channel_id=1, source_target_pairs={{0,8},{4,28},{8,16},{12,4},{16,24},{20,12},{24,0},{28,20},{1,9},{5... | collective-permute-start | bytes 786440 | tf_op jit(solution)/shard_map/ppermute | solution.py:23
  6.5 15.2 %collective-permute-start = (bf16[256,512]{1,0:T(8,128)(2,1)S(1)}, bf16[256,512]{1,0:T(8,128)(2,1)S(1)}, u32[]{:S(2)}, u32[]{:S(2)}) collective-permute-start(bf16[256,512]{1,0:T(8,128)(2,1)S(1)} %take_near.3), channel_id=1, source_target_pairs={{0,4},{4,0},{8,12},{12,8},{16,20},{20,16},{24,28},{28,24},{1,5},{5... | collective-permute-start | bytes 786440 | tf_op jit(solution)/shard_map/ppermute | solution.py:23
  11.4 12.2 %collective-permute-start.2 = (bf16[256,512]{1,0:T(8,128)(2,1)S(1)}, bf16[256,512]{1,0:T(8,128)(2,1)S(1)}, u32[]{:S(2)}, u32[]{:S(2)}) collective-permute-start(bf16[256,512]{1,0:T(8,128)(2,1)S(1)} %collective-permute-done.1.refs_1_), channel_id=1, source_target_pairs={{0,8},{4,28},{8,16},{12,4},{16,24},{20,12},{24,0},{28,20},{1,9},{5... | collective-permute-start | bytes 786440 | tf_op jit(solution)/shard_map/ppermute | solution.py:23
  17.0 10.5 %collective-permute-start.6 = (bf16[256,512]{1,0:T(8,128)(2,1)S(1)}, bf16[256,512]{1,0:T(8,128)(2,1)S(1)}, u32[]{:S(2)}, u32[]{:S(2)}) collective-permute-start(bf16[256,512]{1,0:T(8,128)(2,1)S(1)} %collective-permute-done.5.refs_3_), channel_id=1, source_target_pairs={{0,8},{4,28},{8,16},{12,4},{16,24},{20,12},{24,0},{28,20},{1,9},{5... | collective-permute-start | bytes 786440 | tf_op jit(solution)/shard_map/ppermute | solution.py:23
  21.8 9.7 %collective-permute-start.10 = (bf16[256,512]{1,0:T(8,128)(2,1)S(1)}, bf16[256,512]{1,0:T(8,128)(2,1)S(1)}, u32[]{:S(2)}, u32[]{:S(2)}) collective-permute-start(bf16[256,512]{1,0:T(8,128)(2,1)S(1)} %collective-permute-done.near.refs_6_), channel_id=1, source_target_pairs={{0,8},{4,28},{8,16},{12,4},{16,24},{20,12},{24,0},{28,20},{1,9},{5... | collective-permute-start | bytes 786440 | tf_op jit(solution)/shard_map/ppermute | solution.py:23
  23.9 6.2 %collective-permute-start.3 = (bf16[3,128,128]{2,1,0:T(8,128)(2,1)S(1)}, bf16[3,128,128]{2,1,0:T(8,128)(2,1)S(1)}, u32[]{:S(2)}, u32[]{:S(2)}) collective-permute-start(bf16[3,128,128]{2,1,0:T(8,128)(2,1)S(1)} %end_blocks.1), channel_id=1, source_target_pairs={{0,4},{4,0},{8,12},{12,8},{16,20},{20,16},{24,28},{28,24},{1,5},{5... | collective-permute-start | bytes 294920 | tf_op jit(solution)/shard_map/ppermute | solution.py:23
  30.7 1.5 %collective-permute-start.7 = (bf16[2,3,128,128]{3,2,1,0:T(8,128)(2,1)S(1)}, bf16[2,3,128,128]{3,2,1,0:T(8,128)(2,1)S(1)}, u32[]{:S(2)}, u32[]{:S(2)}) collective-permute-start(bf16[2,3,128,128]{3,2,1,0:T(8,128)(2,1)S(1)} %get-tuple-element.16), channel_id=1, source_target_pairs={{0,1},{1,0},{2,3},{3,2},{4,5},{5,4},{6,7},{7,6},{8,9},{9,8},{10,11... | collective-permute-start | bytes 589832 | tf_op jit(solution)/shard_map/ppermute | solution.py:23
  33.0 2.3 %collective-permute-start.12 = (bf16[4,3,128,128]{3,2,1,0:T(8,128)(2,1)S(1)}, bf16[4,3,128,128]{3,2,1,0:T(8,128)(2,1)S(1)}, u32[]{:S(2)}, u32[]{:S(2)}) collective-permute-start(bf16[4,3,128,128]{3,2,1,0:T(8,128)(2,1)S(1)} %get-tuple-element.22), channel_id=1, source_target_pairs={{0,1},{1,0},{2,3},{3,2},{4,5},{5,4},{6,7},{7,6},{8,9},{9,8},{10,11... | collective-permute-start | bytes 1179656 | tf_op jit(solution)/shard_map/ppermute | solution.py:23
  33.2 7.8 %collective-permute-start.8 = (bf16[2,3,128,128]{3,2,1,0:T(8,128)(2,1)S(1)}, bf16[2,3,128,128]{3,2,1,0:T(8,128)(2,1)S(1)}, u32[]{:S(2)}, u32[]{:S(2)}) collective-permute-start(bf16[2,3,128,128]{3,2,1,0:T(8,128)(2,1)S(1)} %add.11), channel_id=1, source_target_pairs={{0,2},{1,3},{2,0},{3,1},{4,6},{5,7},{6,4},{7,5},{8,10},{9,11},{10,... | collective-permute-start | bytes 589832 | tf_op jit(solution)/shard_map/ppermute | solution.py:23
  34.8 6.3 %collective-permute-start.9 = (bf16[2,3,128,128]{3,2,1,0:T(8,128)(2,1)S(1)}, bf16[2,3,128,128]{3,2,1,0:T(8,128)(2,1)S(1)}, u32[]{:S(2)}, u32[]{:S(2)}) collective-permute-start(bf16[2,3,128,128]{3,2,1,0:T(8,128)(2,1)S(1)} %get-tuple-element.17), channel_id=1, source_target_pairs={{0,1},{1,0},{2,3},{3,2},{4,5},{5,4},{6,7},{7,6},{8,9},{9,8},{10,11... | collective-permute-start | bytes 589832 | tf_op jit(solution)/shard_map/ppermute | solution.py:23
  34.9 6.2 %collective-permute-start.11 = (bf16[4,3,128,128]{3,2,1,0:T(8,128)(2,1)S(1)}, bf16[4,3,128,128]{3,2,1,0:T(8,128)(2,1)S(1)}, u32[]{:S(2)}, u32[]{:S(2)}) collective-permute-start(bf16[4,3,128,128]{3,2,1,0:T(8,128)(2,1)S(1)} %get-tuple-element.20), channel_id=1, source_target_pairs={{0,1},{1,0},{2,3},{3,2},{4,5},{5,4},{6,7},{7,6},{8,9},{9,8},{10,11... | collective-permute-start | bytes 1179656 | tf_op jit(solution)/shard_map/ppermute | solution.py:23
  35.4 13.5 %collective-permute-start.13 = (bf16[4,3,128,128]{3,2,1,0:T(8,128)(2,1)S(1)}, bf16[4,3,128,128]{3,2,1,0:T(8,128)(2,1)S(1)}, u32[]{:S(2)}, u32[]{:S(2)}) collective-permute-start(bf16[4,3,128,128]{3,2,1,0:T(8,128)(2,1)S(1)} %add.12), channel_id=1, source_target_pairs={{0,2},{1,3},{2,0},{3,1},{4,6},{5,7},{6,4},{7,5},{8,10},{9,11},{10,... | collective-permute-start | bytes 1179656 | tf_op jit(solution)/shard_map/ppermute | solution.py:23
